TPU v7x, 128 devices: a whole 4x4x4 slice. The times are simulated.
128 devices in a mesh: tm: 16 (over y, z), rows: 8 (over x, core).
Axes of the slice: x: 4, y: 4, z: 4, core: 2. Of those that a mesh axis runs over, the one named last changes fastest.
Arguments:
- feat: bfloat16 [64, 128, 128, 256], P('tm', 'rows')
- gamma: float32 [256], replicated, may hold values from 0.1 to 1.9
- beta: float32 [256], replicated, may hold values from -3 to 3
- conv_weight: bfloat16 [3, 3, 768, 256], replicated, may hold values from -0.078125 to 0.078125
- conv_bias: float32 [256], replicated, may hold values from -3 to 3
- proj: bfloat16 [256, 16], replicated, may hold values from -0.375 to 0.375
- proj_bias: float32 [16], replicated, may hold values from -3 to 3
- clip_len: int32 [16], replicated, may hold values from 1 to 8, 64 in all
- owner: int32 [16], replicated, may hold values from 0 to 15, as said below
Outputs:
- block: bfloat16 [64, 128, 128, 256], P('tm', 'rows')
- latent_seq: bfloat16 [128, 128, 2048], P('tm', 'rows')
Inputs may be any that keep to these rules, and one draw needn't show every extreme that they name: `clip_len`: the lengths sum to 64; the longest clip has exactly 8 frames. `owner`: each tm index owns exactly one clip.
All inputs are finite; a program needn't handle non-finite values.
Results may differ from a plain program's by a relative error of at most 0.0052.
Values may be sent and summed in bfloat16 or wider, within the bound.
No kernel may reach another device: no remote copies, remote signals or barrier semaphores. Data moves between devices by JAX's collectives and lax.ppermute only.
A program may use at most 256 MiB of HBM per device.

v0:
```python
import jax
import jax.numpy as jnp
from jax import lax
from jax.sharding import PartitionSpec as P

GROUPS = 32
SEQ_CAP = 8


def passed_along(block, axis, distance):
    devices = range(lax.axis_size(axis))
    route = [(i - distance, i) for i in devices if i - distance in devices]
    return lax.ppermute(block, axis, route)


def with_halo(array, sides, width):
    for axis, dim in sides:
        size, length = (lax.axis_size(axis), array.shape[dim])
        up = [(i, (i + 1) % size) for i in range(size - 1)]
        down = [(j, i) for i, j in up]
        last = lax.slice_in_dim(array, length - width, length, axis=dim)
        first = lax.slice_in_dim(array, 0, width, axis=dim)
        before = lax.ppermute(last, axis, up)
        after = lax.ppermute(first, axis, down)
        array = jnp.concatenate([before, array, after], axis=dim)
    return array


def clip_layout(clip_len, frame_ids):
    ends = jnp.cumsum(clip_len)
    starts = ends - clip_len
    clip_of = jnp.sum((frame_ids[:, None] >= ends[None, :]).astype(jnp.int32), axis=1)
    member_int = (
        clip_of[None, :] == jnp.arange(clip_len.shape[0], dtype=jnp.int32)[:, None]
    ).astype(jnp.int32)
    frame_start = jnp.sum(member_int * starts[:, None], axis=0)
    return (member_int, frame_start)


def on_device(feat, gamma, beta, conv_weight, conv_bias, proj, proj_bias, clip_len, owner):
    frames, band, width, chans = feat.shape
    latent_ch = proj.shape[1]
    n_time = lax.axis_size("tm")
    n_bands = lax.axis_size("rows")
    tm_index = lax.axis_index("tm")
    local_ids = jnp.arange(frames, dtype=jnp.int32)
    frame_ids = tm_index * frames + local_ids
    member_int, frame_start = clip_layout(clip_len, frame_ids)
    member = member_int.astype(jnp.float32)
    values = feat.astype(jnp.float32)
    grouped = values.reshape(frames, band, width, GROUPS, chans // GROUPS)
    part_one = jnp.dot(member, jnp.sum(grouped, axis=(1, 2, 4)), precision=lax.Precision.HIGHEST)
    part_two = jnp.dot(
        member, jnp.sum(grouped * grouped, axis=(1, 2, 4)), precision=lax.Precision.HIGHEST
    )
    tot_one, tot_two = lax.psum((part_one, part_two), ("tm", "rows"))
    count = (clip_len.astype(jnp.float32) * float(band * n_bands * width * (chans // GROUPS)))[
        :, None
    ]
    mean = tot_one / count
    var = tot_two / count - mean * mean
    inv = lax.rsqrt(var + 1e-06)
    frame_mean = jnp.dot(member.T, mean, precision=lax.Precision.HIGHEST)
    frame_inv = jnp.dot(member.T, inv, precision=lax.Precision.HIGHEST)
    frame_mean = jnp.repeat(frame_mean, chans // GROUPS, axis=1)[:, None, None, :]
    frame_inv = jnp.repeat(frame_inv, chans // GROUPS, axis=1)[:, None, None, :]
    hidden = jax.nn.silu((values - frame_mean) * frame_inv * gamma + beta).astype(jnp.bfloat16)
    past = passed_along(hidden[frames - 2 :], "tm", 1)
    extended = jnp.concatenate([past, hidden], axis=0)
    padded = with_halo(extended, (("rows", 1),), 1)
    local_start = frame_start - tm_index * frames + 2
    picks = jnp.maximum(
        local_ids[:, None] + jnp.arange(3, dtype=jnp.int32)[None, :], local_start[:, None]
    )
    taps = jnp.take(padded, picks.reshape(-1), axis=0)
    wide = jnp.pad(taps, ((0, 0), (0, 0), (1, 1), (0, 0))).reshape(
        frames, 3, band + 2, width + 2, chans
    )
    summed = jnp.zeros((frames * band * width, chans), jnp.float32)
    for tap_time in range(3):
        for tap_row in range(3):
            columns = jnp.concatenate(
                [
                    wide[:, tap_time, tap_row : tap_row + band, tap_col : tap_col + width]
                    for tap_col in range(3)
                ],
                axis=-1,
            )
            summed = summed + jnp.dot(
                columns.reshape(-1, 3 * chans),
                conv_weight[tap_time, tap_row],
                preferred_element_type=jnp.float32,
            )
    block = (values + summed.reshape(frames, band, width, chans) + conv_bias).astype(jnp.bfloat16)
    latent = (
        jnp.dot(block.reshape(-1, chans), proj, preferred_element_type=jnp.float32) + proj_bias
    ).astype(jnp.bfloat16)
    latent = latent.reshape(frames, band * width * latent_ch)
    all_ids = jnp.arange(n_time * frames, dtype=jnp.int32)
    all_member, all_start = clip_layout(clip_len, all_ids)
    all_owner = jnp.sum(all_member * owner[:, None], axis=0)
    all_codes = all_owner * SEQ_CAP + all_ids - all_start
    every_slot = jnp.arange(n_time * SEQ_CAP, dtype=jnp.int32)
    placing = (all_codes[None, :] == every_slot[:, None]).astype(jnp.bfloat16)
    shares = lax.all_to_all(latent, "tm", split_axis=1, concat_axis=0, tiled=True)
    placed = jnp.dot(placing, shares, preferred_element_type=jnp.float32).astype(jnp.bfloat16)
    sequence = lax.all_to_all(placed, "tm", split_axis=0, concat_axis=1, tiled=True)
    latent_seq = sequence.reshape(SEQ_CAP, band, width * latent_ch)
    return (block, latent_seq)


def solution(mesh):
    in_specs = (P("tm", "rows", None, None), P(), P(), P(), P(), P(), P(), P(), P())
    out_specs = (P("tm", "rows", None, None), P("tm", "rows", None))
    return jax.shard_map(
        on_device, mesh=mesh, in_specs=in_specs, out_specs=out_specs, check_vma=False
    )
```

profile of v0, /device:TPU:0, one launch (start us, length us, event | category | flops | bytes accessed | tf_op | source)
XLA Modules:
  0.0 388.6 jit_solution(1164917693997343417)
XLA Ops:
  0.6 0.0 copy-start
  0.6 0.7 convert_multiply_fusion.1
  1.3 0.7 copy.21
  2.1 0.1 reduce.4
  2.2 3.3 convert_reduce_fusion
  5.5 0.1 reduce_sum.80
  5.6 0.1 reduce_sum.83
  5.7 0.1 reduce_sum.81
  5.8 0.1 reduce_sum.84
  5.9 0.2 convert_reduce_fusion.2
  6.1 0.3 fusion.124
  6.3 0.3 fusion.120
  6.6 68.4 %all-reduce.1 = (f32[16,32]{1,0:T(8,128)S(1)}, f32[16,32]{1,0:T(8,128)S(1)}) all-reduce(f32[16,32]{1,0:T(8,128)S(1)} %fusion.120, f32[16,32]{1,0:T(8,128)S(1)} %fusion.124), channel_id=1, replica_groups=mesh['tm'=16,'rows'=8] {'tm','rows'}, use_global_device_ids=true, to_apply=%region_8.9 | all-reduce | flops 1024 | bytes 8192 | tf_op jit(solution)/shard_map/psum | solution.py:56
  75.0 0.2 fusion.122
  75.2 0.2 fusion.111
  75.4 0.1 broadcast_in_dim.12
  75.5 0.1 sub.34
  75.6 0.1 broadcast_in_dim.13
  75.7 0.1 mul.76
  75.8 4.7 %fusion.87 = bf16[4,16,128,256]{3,2,1,0:T(8,128)(2,1)S(1)} fusion(bf16[4,16,128,256]{3,2,1,0:T(8,128)(2,1)} %param.9, f32[256]{0:T(256)} %param.11, f32[256]{0:T(256)} %param.10, f32[4,256]{1,0:T(4,128)S(1)} %mul.76, f32[4,256]{1,0:T(4,128)S(1)} %sub.34), kind=kLoop, calls=%fused_computation.78 | loop fusion | flops 20971520 | bytes 8398848 | tf_op jit(solution)/shard_map/convert_element_type | solution.py:67
  80.5 2.0 copy-done.2
  82.5 1.5 slice.158
  84.0 1.7 collective-permute-start
  85.7 0.2 select_reduce_fusion.2
  85.9 0.3 copy-done.10
  86.2 0.1 add_maximum_fusion
  86.3 0.1 max.27
  86.4 44.4 %collective-permute-done = bf16[2,16,128,256]{3,2,1,0:T(8,128)(2,1)S(1)} collective-permute-done((bf16[2,16,128,256]{3,2,1,0:T(8,128)(2,1)}, bf16[2,16,128,256]{3,2,1,0:T(8,128)(2,1)S(1)}, u32[]{:S(2)}, u32[]{:S(2)}) %collective-permute-start) | collective-permute-done | bytes 2097184 | tf_op jit(solution)/shard_map/ppermute | solution.py:13
  130.8 1.8 pad_maximum_fusion.2
  132.6 1.3 collective-permute-start.1
  133.9 1.5 collective-permute-start.2
  135.4 0.1 max.26
  135.5 0.6 convert_reduce_fusion.1
  136.1 2.5 collective-permute-done.2
  138.6 6.0 %pad_maximum_fusion = bf16[6,18,128,256]{3,2,1,0:T(8,128)(2,1)} fusion(bf16[6,1,128,256]{3,2,1,0:T(8,128)(2,1)S(1)} %collective-permute-done.2, bf16[4,16,128,256]{3,2,1,0:T(8,128)(2,1)} %copy-done.2, bf16[2,16,128,256]{3,2,1,0:T(8,128)(2,1)S(1)} %collective-permute-done, bf16[6,1,128,256]{3,2,1,0:T(8,128)(2,1)S(1)} %collective-permute-done.1), kind=kLoop, calls=%fused_computation.82 | loop fusion | flops 10616832 | bytes 14155776 | tf_op jit(solution)/shard_map/concatenate | solution.py:25
  144.6 9.5 %gather_fusion = bf16[12,18,128,256]{3,2,1,0:T(8,128)(2,1)} fusion(bf16[6,18,128,256]{3,2,1,0:T(8,128)(2,1)} %pad_maximum_fusion, s32[1024]{0:T(1024)S(1)} %pad_clamp_fusion), kind=kCustom, calls=%fused_computation | custom fusion | bytes 28311600 | tf_op jit(solution)/shard_map/jit(_take)/gather | solution.py:75
  154.1 6.9 %broadcast_select_fusion = bf16[12,18,128,256]{3,2,1,0:T(8,128)(2,1)S(1)} fusion(bf16[12,18,128,256]{3,2,1,0:T(8,128)(2,1)} %gather_fusion, pred[12]{0:T(512)(128)(4,1)S(1)} %compare_and_fusion), kind=kLoop, calls=%fused_computation.5 | loop fusion | flops 7077888 | bytes 28311564 | tf_op jit(solution)/shard_map/jit(_take)/select_n | solution.py:75
  161.0 8.7 %pad.4 = bf16[12,18,130,256]{3,2,1,0:T(8,128)(2,1)S(1)} pad(bf16[12,18,128,256]{3,2,1,0:T(8,128)(2,1)S(1)} %broadcast_select_fusion, bf16[]{:T(256)} %constant.45.clone.1), padding=0_0x0_0x1_1x0_0 | pad | bytes 28532738 | tf_op jit(solution)/shard_map/jit(_pad)/pad | solution.py:76
  169.8 5.3 %copy-done.1 = bf16[12,18,130,256]{3,2,1,0:T(8,128)(2,1)} copy-done((bf16[12,18,130,256]{3,2,1,0:T(8,128)(2,1)}, bf16[12,18,130,256]{3,2,1,0:T(8,128)(2,1)S(1)}, u32[]{:S(2)}) %copy-start.1) | copy-done | bytes 14376984
  175.1 13.2 %fusion.146 = (bf16[4,1,16,128,256]{4,3,2,1,0:T(8,128)(2,1)}, bf16[4,1,16,128,256]{4,3,2,1,0:T(8,128)(2,1)}, bf16[4,1,16,128,256]{4,3,2,1,0:T(8,128)(2,1)}, bf16...) fusion(bf16[4,3,18,130,256]{4,3,2,1,0:T(8,128)(2,1)S(1)} %bitca, ...), kind=kLoop, calls=%fused_computation.160 | loop fusion | bytes 67108864 | tf_op jit(solution)/shard_map/slice | solution.py:84
  188.3 56.5 %fusion.145 = (bf16[4,1,16,128,256]{4,3,2,1,0:T(8,128)(2,1)}, bf16[4,1,16,128,256]{4,3,2,1,0:T(8,128)(2,1)}, bf16[4,1,16,128,256]{4,3,2,1,0:T(8,128)(2,1)}, bf16...) fusion(bf16[4,3,18,130,256]{4,3,2,1,0:T(8,128)(2,1)} %bitcast.70), kind=kLoop, calls=%fused_computation.159 | loop fusion | bytes 159383552 | tf_op jit(solution)/shard_map/slice | solution.py:84
  244.8 7.9 %fusion = f32[8192,256]{1,0:T(8,128)} fusion(bf16[8192,256]{1,0:T(8,128)(2,1)S(1)} %bitcast.97, bf16[8192,256]{1,0:T(8,128)(2,1)} %bitcast.98, bf16[8192,256]{1,0:T(8,128)(2,1)} %bitcast.99, bf16[3,3,768,256]{3,2,1,0:T(8,128)(2,1)} %param.12), kind=kOutput, calls=%fused_computation.6 | convolution fusion | flops 3258974208 | bytes 21364736 | tf_op jit(solution)/shard_map/dot_general | solution.py:89
  252.7 11.6 %fusion.75 = f32[8192,256]{1,0:T(8,128)} fusion(f32[8192,256]{1,0:T(8,128)} %fusion, bf16[8192,256]{1,0:T(8,128)(2,1)} %bitcast.94, bf16[8192,256]{1,0:T(8,128)(2,1)} %bitcast.95, bf16[8192,256]{1,0:T(8,128)(2,1)} %bitcast.96, bf16[3,3,768,256]{3,2,1,0:T(8,128)(2,1)} %param.12), kind=kOutput, calls=%fused_computation.67 | convolution fusion | flops 3261071360 | bytes 29753344 | tf_op jit(solution)/shard_map/dot_general | solution.py:89
  264.3 11.8 %fusion.72 = f32[8192,256]{1,0:T(8,128)} fusion(f32[8192,256]{1,0:T(8,128)} %fusion.75, bf16[8192,256]{1,0:T(8,128)(2,1)} %bitcast.93, bf16[8192,256]{1,0:T(8,128)(2,1)} %bitcast.92, bf16[8192,256]{1,0:T(8,128)(2,1)} %bitcast.91, bf16[3,3,768,256]{3,2,1,0:T(8,128)(2,1)} %param.12), kind=kOutput, calls=%fused_computation.66 | convolution fusion | flops 3261071360 | bytes 29753344 | tf_op jit(solution)/shard_map/dot_general | solution.py:89
  276.2 11.6 %fusion.69 = f32[8192,256]{1,0:T(8,128)} fusion(f32[8192,256]{1,0:T(8,128)} %fusion.72, bf16[8192,256]{1,0:T(8,128)(2,1)} %bitcast.88, bf16[8192,256]{1,0:T(8,128)(2,1)} %bitcast.89, bf16[8192,256]{1,0:T(8,128)(2,1)} %bitcast.90, bf16[3,3,768,256]{3,2,1,0:T(8,128)(2,1)} %param.12), kind=kOutput, calls=%fused_computation.65 | convolution fusion | flops 3261071360 | bytes 29753344 | tf_op jit(solution)/shard_map/dot_general | solution.py:89
  287.8 11.6 %fusion.66 = f32[8192,256]{1,0:T(8,128)} fusion(f32[8192,256]{1,0:T(8,128)} %fusion.69, bf16[8192,256]{1,0:T(8,128)(2,1)} %bitcast.85, bf16[8192,256]{1,0:T(8,128)(2,1)} %bitcast.86, bf16[8192,256]{1,0:T(8,128)(2,1)} %bitcast.87, bf16[3,3,768,256]{3,2,1,0:T(8,128)(2,1)} %param.12), kind=kOutput, calls=%fused_computation.64 | convolution fusion | flops 3261071360 | bytes 29753344 | tf_op jit(solution)/shard_map/dot_general | solution.py:89
  299.4 11.6 %fusion.63 = f32[8192,256]{1,0:T(8,128)} fusion(f32[8192,256]{1,0:T(8,128)} %fusion.66, bf16[8192,256]{1,0:T(8,128)(2,1)} %bitcast.82, bf16[8192,256]{1,0:T(8,128)(2,1)} %bitcast.83, bf16[8192,256]{1,0:T(8,128)(2,1)} %bitcast.84, bf16[3,3,768,256]{3,2,1,0:T(8,128)(2,1)} %param.12), kind=kOutput, calls=%fused_computation.63 | convolution fusion | flops 3261071360 | bytes 29753344 | tf_op jit(solution)/shard_map/dot_general | solution.py:89
  311.0 11.6 %fusion.60 = f32[8192,256]{1,0:T(8,128)} fusion(f32[8192,256]{1,0:T(8,128)} %fusion.63, bf16[8192,256]{1,0:T(8,128)(2,1)} %bitcast.79, bf16[8192,256]{1,0:T(8,128)(2,1)} %bitcast.80, bf16[8192,256]{1,0:T(8,128)(2,1)} %bitcast.81, bf16[3,3,768,256]{3,2,1,0:T(8,128)(2,1)} %param.12), kind=kOutput, calls=%fused_computation.62 | convolution fusion | flops 3261071360 | bytes 29753344 | tf_op jit(solution)/shard_map/dot_general | solution.py:89
  322.6 9.8 %fusion.57 = f32[8192,256]{1,0:T(8,128)} fusion(f32[8192,256]{1,0:T(8,128)} %fusion.60, bf16[8192,256]{1,0:T(8,128)(2,1)} %bitcast.76, bf16[8192,256]{1,0:T(8,128)(2,1)} %bitcast.77, bf16[8192,256]{1,0:T(8,128)(2,1)S(1)} %bitcast.78, bf16[3,3,768,256]{3,2,1,0:T(8,128)(2,1)} %param.12), kind=kOutput, calls=%fused_computation.61 | convolution fusion | flops 3261071360 | bytes 29753344 | tf_op jit(solution)/shard_map/dot_general | solution.py:89
  332.4 12.0 %fusion.54 = f32[8192,256]{1,0:T(8,128)} fusion(f32[8192,256]{1,0:T(8,128)} %fusion.57, bf16[8192,256]{1,0:T(8,128)(2,1)} %bitcast.74, bf16[8192,256]{1,0:T(8,128)(2,1)} %bitcast.75, bf16[8192,256]{1,0:T(8,128)(2,1)} %bitcast.73, bf16[3,3,768,256]{3,2,1,0:T(8,128)(2,1)} %param.12), kind=kOutput, calls=%fused_computation.60 | convolution fusion | flops 3261071360 | bytes 29753344 | tf_op jit(solution)/shard_map/dot_general | solution.py:89
  344.4 0.0 copy-start.6
  344.4 4.8 %fusion.90 = bf16[4,16,128,256]{3,2,1,0:T(8,128)(2,1)S(1)} fusion(f32[4,16,128,256]{3,2,1,0:T(8,128)} %bitcast.72, bf16[4,16,128,256]{3,2,1,0:T(8,128)(2,1)S(1)} %copy-done.3, f32[256]{0:T(256)S(1)} %copy-done.7), kind=kLoop, calls=%fused_computation.81 | loop fusion | flops 8388608 | bytes 16778240 | tf_op jit(solution)/shard_map/convert_element_type | solution.py:94
  349.3 2.0 copy-done.4
  351.3 1.2 fusion.78
  352.5 1.0 copy.22
  353.5 3.6 all_to_all.26
  357.2 0.9 copy.23
  358.1 7.0 %all-to-all-start = ((bf16[4,16,2048]{2,0,1:T(4,128)(2,1)}), bf16[4,16,2048]{2,0,1:T(4,128)(2,1)S(1)}, u32[]{:S(2)}, u32[]{:S(2)}) async-start(bf16[4,16,2048]{2,0,1:T(4,128)(2,1)} %copy.23), calls=%async_computation | async-start | bytes 524288 | tf_op jit(solution)/shard_map/all_to_all | solution.py:105
  365.1 0.1 select_reduce_fusion.1
  365.2 8.3 %all-to-all-done = bf16[4,16,2048]{2,0,1:T(4,128)(2,1)S(1)} async-done(((bf16[4,16,2048]{2,0,1:T(4,128)(2,1)}), bf16[4,16,2048]{2,0,1:T(4,128)(2,1)S(1)}, u32[]{:S(2)}, u32[]{:S(2)}) %all-to-all-start) | async-done | bytes 262176 | tf_op jit(solution)/shard_map/all_to_all | solution.py:105
  373.6 0.1 all_to_all.29
  373.7 0.3 fusion.91
  373.9 13.6 %all_to_all.35 = bf16[16,8,2048]{2,1,0:T(8,128)(2,1)S(1)} all-to-all(bf16[16,8,2048]{2,1,0:T(8,128)(2,1)S(1)} %fusion.91), channel_id=1, replica_groups=mesh['tm'=16,'rows'=8] {'tm'}, dimensions={0} | all-to-all | bytes 1048576 | tf_op jit(solution)/shard_map/all_to_all | solution.py:107
  387.5 1.1 copy.24
  (29 shorter events, 0.1 us)
Async XLA Ops:
  0.6 350.7 %copy-start = (bf16[256,16]{0,1:T(8,128)(2,1)S(1)}, bf16[256,16]{0,1:T(8,128)(2,1)}, u32[]{:S(2)}) copy-start(bf16[256,16]{0,1:T(8,128)(2,1)} %param.14) | copy-start | bytes 24580
  2.2 83.5 %copy-start.8 = (s32[16]{0:T(128)S(1)}, s32[16]{0:T(128)}, u32[]{:S(2)}) copy-start(s32[16]{0:T(128)} %param.16) | copy-start | bytes 196
  80.4 2.0 copy-start.2
  84.0 46.8 %collective-permute-start = (bf16[2,16,128,256]{3,2,1,0:T(8,128)(2,1)}, bf16[2,16,128,256]{3,2,1,0:T(8,128)(2,1)S(1)}, u32[]{:S(2)}, u32[]{:S(2)}) collective-permute-start(bf16[2,16,128,256]{3,2,1,0:T(8,128)(2,1)} %slice.158), channel_id=1, source_target_pairs={{0,8},{8,16},{16,24},{24,32},{32,40},{40,48},{48,56},{56,64},{64,7... | collective-permute-start | bytes 6291464 | tf_op jit(solution)/shard_map/ppermute | solution.py:13
  85.7 0.5 copy-start.10
  132.6 3.5 collective-permute-start.1
  133.9 4.7 %collective-permute-start.2 = (bf16[6,1,128,256]{3,2,1,0:T(8,128)(2,1)S(1)}, bf16[6,1,128,256]{3,2,1,0:T(8,128)(2,1)S(1)}, u32[]{:S(2)}, u32[]{:S(2)}) collective-permute-start(bf16[6,1,128,256]{3,2,1,0:T(8,128)(2,1)S(1)} %get-tuple-element.40), channel_id=1, source_target_pairs={{1,0},{2,1},{3,2},{4,3},{5,4},{6,5},{7,6},{9,8},{10,9},{11,10},{12... | collective-permute-start | bytes 1179656 | tf_op jit(solution)/shard_map/ppermute | solution.py:24
  169.7 5.3 %copy-start.1 = (bf16[12,18,130,256]{3,2,1,0:T(8,128)(2,1)}, bf16[12,18,130,256]{3,2,1,0:T(8,128)(2,1)S(1)}, u32[]{:S(2)}) copy-start(bf16[12,18,130,256]{3,2,1,0:T(8,128)(2,1)S(1)} %pad.4) | copy-start | bytes 43130884
  188.3 56.5 %copy-start.5 = (bf16[4,1,16,128,256]{4,3,2,1,0:T(8,128)(2,1)S(1)}, bf16[4,1,16,128,256]{4,3,2,1,0:T(8,128)(2,1)}, u32[]{:S(2)}) copy-start(bf16[4,1,16,128,256]{4,3,2,1,0:T(8,128)(2,1)} %get-tuple-element.36) | copy-start | bytes 12582916
  332.4 12.0 %copy-start.3 = (bf16[4,16,128,256]{3,2,1,0:T(8,128)(2,1)S(1)}, bf16[4,16,128,256]{3,2,1,0:T(8,128)(2,1)}, u32[]{:S(2)}) copy-start(bf16[4,16,128,256]{3,2,1,0:T(8,128)(2,1)} %param.9) | copy-start | bytes 12582916
  332.4 12.0 %copy-start.7 = (f32[256]{0:T(256)S(1)}, f32[256]{0:T(256)}, u32[]{:S(2)}) copy-start(f32[256]{0:T(256)} %param.13) | copy-start | bytes 3076
  344.4 6.9 %copy-start.6 = (f32[16]{0:T(128)S(1)}, f32[16]{0:T(128)}, u32[]{:S(2)}) copy-start(f32[16]{0:T(128)} %param.15) | copy-start | bytes 196
  349.3 2.0 copy-start.4
  349.3 15.8 %copy-start.9 = (s32[16]{0:T(128)S(1)}, s32[16]{0:T(128)}, u32[]{:S(2)}) copy-start(s32[16]{0:T(128)} %param.17) | copy-start | bytes 196
  349.3 15.8 %copy-start.11 = (s32[16]{0:T(128)S(1)}, s32[16]{0:T(128)}, u32[]{:S(2)}) copy-start(s32[16]{0:T(128)} %copy-done.10) | copy-start | bytes 196
  349.3 15.8 %copy-start.12 = (s32[64]{0:T(128)S(1)}, s32[64]{0:T(128)}, u32[]{:S(2)}) copy-start(s32[64]{0:T(128)} %convert_reduce_fusion.1) | copy-start | bytes 772
  358.1 15.5 %all-to-all-start = ((bf16[4,16,2048]{2,0,1:T(4,128)(2,1)}), bf16[4,16,2048]{2,0,1:T(4,128)(2,1)S(1)}, u32[]{:S(2)}, u32[]{:S(2)}) async-start(bf16[4,16,2048]{2,0,1:T(4,128)(2,1)} %copy.23), calls=%async_computation | async-start | bytes 524288 | tf_op jit(solution)/shard_map/all_to_all | solution.py:105
where the time goes:
time: 396 us; the launch traced here: 389 us
  local copies, waits for them, and re-layouts  107 us (27%)
  matrix products  102 us (26%)
  blocking collectives  82 us (21%)
  waiting for transfers between devices  55.2 us (14%)
  other arithmetic  29.7 us (8%)
  starting transfers between devices  11.5 us (3%)
    dot_general x9, matrix products, on_device(): jnp.dot(columns.reshape(-1, 3 * chans), conv_weight[tap_time, tap_row], p...  99.6 us
    slice x2, local copies, waits for them, and re-layouts, on_device(): wide[:, tap_time, tap_row:tap_row + band, tap_col:tap_col + width]  69.7 us
    psum x1, blocking collectives, on_device(): tot_one, tot_two = lax.psum((part_one, part_two), ('tm', 'rows'))  68.4 us
    ppermute x1, waiting for transfers between devices, passed_along(): return lax.ppermute(block, axis, route)  44.4 us
    all_to_all x1, blocking collectives, on_device(): lax.all_to_all(placed, 'tm', split_axis=0, concat_axis=1, tiled=True)  13.6 us
    unnamed x27, local copies, waits for them, and re-layouts  10.8 us
    gather x1, local copies, waits for them, and re-layouts, on_device(): taps = jnp.take(padded, picks.reshape(-1), axis=0)  9.54 us
    pad x1, local copies, waits for them, and re-layouts, on_device(): jnp.pad(taps, ((0, 0), (0, 0), (1, 1), (0, 0)))  8.71 us
  transfers between devices with their start and end apart: 4, of which 3 were waited for; matrix products, arithmetic and copies ran while one was open for 0% of the time, Pallas kernels for 0%

commit v1 on v0

v1 whole, which is shorter than its diff:
```python
import jax
import jax.numpy as jnp
from jax import lax
from jax.experimental import pallas as pl
from jax.experimental.pallas import tpu as pltpu
from jax.sharding import PartitionSpec as P

GROUPS = 32
SEQ_CAP = 8
F32 = jnp.float32
BF16 = jnp.bfloat16
MIB = 2**20


def stats_kernel(x_ref, o_ref):
    f = pl.program_id(0)
    x = x_ref[0].astype(F32)
    x = x.reshape(-1, 8, x.shape[-1])
    one = jnp.sum(jnp.sum(x, axis=0), axis=0, keepdims=True)
    two = jnp.sum(jnp.sum(x * x, axis=0), axis=0, keepdims=True)
    o_ref[pl.ds(f, 1), :] = one
    o_ref[pl.ds(4 + f, 1), :] = two


def channel_stats(feat):
    frames, band, width, chans = feat.shape
    return pl.pallas_call(
        stats_kernel,
        grid=(frames,),
        in_specs=[pl.BlockSpec((1, band, width, chans), lambda f: (f, 0, 0, 0))],
        out_specs=pl.BlockSpec((2 * frames, chans), lambda f: (0, 0)),
        out_shape=jax.ShapeDtypeStruct((2 * frames, chans), F32),
        compiler_params=pltpu.CompilerParams(vmem_limit_bytes=24 * MIB),
        cost_estimate=pl.CostEstimate(
            flops=4 * feat.size, bytes_accessed=2 * feat.size, transcendentals=0
        ),
        name="channel_stats",
    )(feat)


def normed_rows(x, half_scale, half_shift):
    u = x.astype(F32) * half_scale + half_shift
    return u + u * jnp.tanh(u)


def put_rows(slab, row, h):
    width, chans = h.shape
    col = lax.broadcasted_iota(jnp.int32, h.shape, 0)
    left = jnp.where(col == 0, 0.0, pltpu.roll(h, 1, 0))
    right = jnp.where(col == width - 1, 0.0, pltpu.roll(h, width - 1, 0))
    slab[row, :, 0:chans] = left.astype(BF16)
    slab[row, :, chans : 2 * chans] = h.astype(BF16)
    slab[row, :, 2 * chans :] = right.astype(BF16)


def tap_dots(total, slab, weights, row, rows):
    for tap_row in range(3):
        lhs = slab[pl.ds(row + tap_row, rows)]
        lhs = lhs.reshape(rows * lhs.shape[1], lhs.shape[2])
        total = total + jnp.dot(lhs, weights[tap_row], preferred_element_type=F32)
    return total


def latent_frame(block, projt_ref, pbias_ref, lscr, lat_ref, f):
    rows, width, chans = block.shape
    wide = projt_ref.shape[1]
    per = wide // 16
    both = jnp.dot(
        block.reshape(rows * width, chans), projt_ref[...], preferred_element_type=F32
    ).reshape(rows, width, wide)
    col = lax.broadcasted_iota(jnp.int32, both.shape, 1)
    lane = lax.broadcasted_iota(jnp.int32, both.shape, 2)
    lscr[...] = jnp.where(col % per == lane // 16, both, 0.0)
    for j in range(width // per):
        part = jnp.sum(lscr[:, per * j : per * (j + 1), :], axis=1) + pbias_ref[...]
        lat_ref[j, f] = part.astype(BF16)


def local_kernel(
    starts, edges, feat_hbm, top_hbm, bot_hbm, w_hbm, sums_ref, mask_ref, count_ref,
    group_ref, gamma_ref, beta_ref, cbias_ref, projt_ref, pbias_ref,
    block_hbm, part_hbm, lat_ref, affine_ref,
    feat, halo, w, slab, obuf, part, lscr, sems, osems,
):
    copies = [pltpu.make_async_copy(feat_hbm.at[f], feat.at[f], sems.at[f]) for f in range(4)]
    top_copy = pltpu.make_async_copy(top_hbm, halo.at[0], sems.at[4])
    bot_copy = pltpu.make_async_copy(bot_hbm, halo.at[1], sems.at[5])
    w_copy = pltpu.make_async_copy(w_hbm, w, sems.at[6])
    top_copy.start()
    bot_copy.start()
    for c in copies:
        c.start()
    w_copy.start()

    tot = jnp.dot(
        mask_ref[...], sums_ref[...], precision=lax.Precision.HIGHEST, preferred_element_type=F32
    )
    tot = jnp.dot(
        tot, group_ref[...], precision=lax.Precision.HIGHEST, preferred_element_type=F32
    )
    mom = tot / count_ref[...]
    mean = mom[0:4]
    var = mom[4:8] - mean * mean
    scale = lax.rsqrt(var + 1e-06) * gamma_ref[...]
    affine_ref[0:4] = 0.5 * scale
    affine_ref[4:8] = 0.5 * (beta_ref[...] - mean * scale)

    top_copy.wait()
    bot_copy.wait()
    for f in range(4):
        copies[f].wait()
        hs = affine_ref[f : f + 1]
        hb = affine_ref[4 + f : 5 + f]
        page = slab.at[f]
        top_on = (edges[0] > 0).astype(F32)
        bot_on = (edges[1] > 0).astype(F32)
        put_rows(page, 0, normed_rows(halo[0, f], hs, hb) * top_on)
        put_rows(page, 17, normed_rows(halo[1, f], hs, hb) * bot_on)

        def norm_row(r, _, f=f, hs=hs, hb=hb, page=page):
            put_rows(page, r + 1, normed_rows(feat[f, r], hs, hb))
            return 0

        lax.fori_loop(0, 16, norm_row, 0, unroll=2)
    w_copy.wait()

    rows = 8
    zero = jnp.zeros((rows * 128, 256), F32)
    outs = []
    for f in (3, 2):
        src = [jnp.maximum(f - 2 + a, starts[f]) for a in range(3)]

        def chunk(m, _, f=f, src=src):
            total = zero
            for a in range(3):
                total = tap_dots(total, slab.at[src[a]], w.at[a], m * rows, rows)
            total = total.reshape(rows, 128, 256)
            r = pl.ds(m * rows, rows)
            obuf[f - 2, r] = (total + feat[f, r].astype(F32) + cbias_ref[...]).astype(BF16)
            return 0

        lax.fori_loop(0, 2, chunk, 0)
        c = pltpu.make_async_copy(obuf.at[f - 2], block_hbm.at[f], osems.at[f - 2])
        c.start()
        outs.append(c)
        latent_frame(obuf[f - 2], projt_ref, pbias_ref, lscr, lat_ref, f - 2)

    src1 = jnp.maximum(0, starts[1])

    def chunk1(m, _):
        total = tap_dots(zero, slab.at[1], w.at[2], m * rows, rows)
        total = tap_dots(total, slab.at[src1], w.at[1], m * rows, rows)
        part[1, pl.ds(m * rows, rows)] = total.reshape(rows, 128, 256)
        return 0

    lax.fori_loop(0, 2, chunk1, 0)

    def chunk0(m, _):
        total = tap_dots(zero, slab.at[0], w.at[2], m * rows, rows)
        part[0, pl.ds(m * rows, rows)] = total.reshape(rows, 128, 256)
        return 0

    lax.fori_loop(0, 2, chunk0, 0)

    @pl.when(starts[1] >= 0)
    def _():
        def more(m, _):
            r = pl.ds(m * rows, rows)
            total = part[1, r].reshape(rows * 128, 256)
            total = tap_dots(total, slab.at[src1], w.at[0], m * rows, rows)
            part[1, r] = total.reshape(rows, 128, 256)
            return 0

        lax.fori_loop(0, 2, more, 0)

    @pl.when(starts[0] >= 0)
    def _():
        def more(m, _):
            r = pl.ds(m * rows, rows)
            total = part[0, r].reshape(rows * 128, 256)
            total = tap_dots(total, slab.at[0], w.at[0], m * rows, rows)
            total = tap_dots(total, slab.at[0], w.at[1], m * rows, rows)
            part[0, r] = total.reshape(rows, 128, 256)
            return 0

        lax.fori_loop(0, 2, more, 0)

    for f in range(2):
        c = pltpu.make_async_copy(part.at[f], part_hbm.at[f], osems.at[2 + f])
        c.start()
        outs.append(c)
    for c in outs:
        c.wait()


ANY = pl.BlockSpec(memory_space=pl.ANY)
VM = pl.BlockSpec(memory_space=pltpu.VMEM)
SM = pl.BlockSpec(memory_space=pltpu.SMEM)


def local_part(starts, edges, feat, top, bot, weight, sums, mask, count, group, gamma, beta,
               cbias, projt, pbias):
    shape = feat.shape
    return pl.pallas_call(
        local_kernel,
        in_specs=[SM, SM, ANY, ANY, ANY, ANY] + [VM] * 9,
        out_specs=[ANY, ANY, VM, VM],
        out_shape=[
            jax.ShapeDtypeStruct(shape, BF16),
            jax.ShapeDtypeStruct((2,) + shape[1:], F32),
            jax.ShapeDtypeStruct((16, 2, 16, 128), BF16),
            jax.ShapeDtypeStruct((8, 256), F32),
        ],
        scratch_shapes=[
            pltpu.VMEM(shape, BF16),
            pltpu.VMEM((2, 4, 128, 256), BF16),
            pltpu.VMEM(weight.shape, BF16),
            pltpu.VMEM((4, 18, 128, 768), BF16),
            pltpu.VMEM((2, 16, 128, 256), BF16),
            pltpu.VMEM((2, 16, 128, 256), F32),
            pltpu.VMEM((16, 128, 128), F32),
            pltpu.SemaphoreType.DMA((7,)),
            pltpu.SemaphoreType.DMA((4,)),
        ],
        compiler_params=pltpu.CompilerParams(vmem_limit_bytes=56 * MIB),
        cost_estimate=pl.CostEstimate(
            flops=2 * 9 * 2048 * 2304 * 256, bytes_accessed=16 * MIB, transcendentals=feat.size
        ),
        name="local_conv",
    )(starts, edges, feat, top, bot, weight, sums, mask, count, group, gamma, beta, cbias, projt,
      pbias)


def past_kernel(
    starts, edges, one_ref, two_ref, border_ref, top_ref, bot_ref, feat_hbm, w_hbm, part_hbm,
    affine_ref, cbias_ref, projt_ref, pbias_ref, early_ref, block_in,
    block_hbm, lat_ref,
    feat, w, slab, obuf, part, lscr, sems, osems,
):
    del block_in
    copies = [
        pltpu.make_async_copy(w_hbm.at[pl.ds(0, 2)], w, sems.at[0]),
        pltpu.make_async_copy(part_hbm, part, sems.at[1]),
        pltpu.make_async_copy(feat_hbm.at[pl.ds(0, 2)], feat, sems.at[2]),
    ]
    for c in copies:
        c.start()
    hs = affine_ref[0:1]
    hb = affine_ref[4:5]
    top_on = (edges[0] > 0).astype(F32)
    bot_on = (edges[1] > 0).astype(F32)
    mains = (two_ref, one_ref)
    for p in range(2):
        @pl.when(starts[0] < p - 1)
        def _(p=p):
            page = slab.at[p]
            put_rows(page, 0, normed_rows(top_ref[p], hs, hb) * top_on)
            put_rows(page, 1, normed_rows(border_ref[p, 0], hs, hb))
            put_rows(page, 16, normed_rows(border_ref[p, 1], hs, hb))
            put_rows(page, 17, normed_rows(bot_ref[p], hs, hb) * bot_on)

            def norm_row(r, _):
                put_rows(page, r + 2, normed_rows(mains[p][r], hs, hb))
                return 0

            lax.fori_loop(0, 14, norm_row, 0, unroll=2)
    for c in copies:
        c.wait()
    rows = 8

    @pl.when(starts[1] < 0)
    def _():
        def more(m, _):
            r = pl.ds(m * rows, rows)
            total = part[1, r].reshape(rows * 128, 256)
            total = tap_dots(total, slab.at[1], w.at[0], m * rows, rows)
            part[1, r] = total.reshape(rows, 128, 256)
            return 0

        lax.fori_loop(0, 2, more, 0)

    src0 = jnp.clip(starts[0] + 2, 0, 1)

    @pl.when(starts[0] < 0)
    def _():
        def more(m, _):
            r = pl.ds(m * rows, rows)
            total = part[0, r].reshape(rows * 128, 256)
            total = tap_dots(total, slab.at[1], w.at[1], m * rows, rows)
            total = tap_dots(total, slab.at[src0], w.at[0], m * rows, rows)
            part[0, r] = total.reshape(rows, 128, 256)
            return 0

        lax.fori_loop(0, 2, more, 0)

    outs = []
    for f in (1, 0):
        def finish(r, _, f=f):
            rr = pl.ds(r * 2, 2)
            obuf[f, rr] = (part[f, rr] + feat[f, rr].astype(F32) + cbias_ref[...]).astype(BF16)
            return 0

        lax.fori_loop(0, 8, finish, 0)
        c = pltpu.make_async_copy(obuf.at[f], block_hbm.at[f], osems.at[f])
        c.start()
        outs.append(c)
        latent_frame(obuf[f], projt_ref, pbias_ref, lscr, lat_ref, f)
    lat_ref[:, 2:4] = early_ref[...]
    for c in outs:
        c.wait()


def past_part(starts, edges, one, two, border, top, bot, feat, weight, part, affine, cbias, projt,
              pbias, early, block):
    shape = feat.shape
    return pl.pallas_call(
        past_kernel,
        in_specs=[SM, SM] + [VM] * 5 + [ANY] * 3 + [VM] * 5 + [ANY],
        out_specs=[ANY, VM],
        out_shape=[
            jax.ShapeDtypeStruct(shape, BF16),
            jax.ShapeDtypeStruct((16, 4, 16, 128), BF16),
        ],
        input_output_aliases={15: 0},
        scratch_shapes=[
            pltpu.VMEM((2,) + shape[1:], BF16),
            pltpu.VMEM((2,) + weight.shape[1:], BF16),
            pltpu.VMEM((2, 18, 128, 768), BF16),
            pltpu.VMEM((2, 16, 128, 256), BF16),
            pltpu.VMEM((2, 16, 128, 256), F32),
            pltpu.VMEM((16, 128, 128), F32),
            pltpu.SemaphoreType.DMA((3,)),
            pltpu.SemaphoreType.DMA((2,)),
        ],
        compiler_params=pltpu.CompilerParams(vmem_limit_bytes=56 * MIB),
        cost_estimate=pl.CostEstimate(
            flops=2 * 3 * 2048 * 2304 * 256, bytes_accessed=12 * MIB, transcendentals=feat.size // 2
        ),
        name="past_conv",
    )(starts, edges, one, two, border, top, bot, feat, weight, part, affine, cbias, projt, pbias,
      early, block)


def place_kernel(codes, x_ref, o_ref):
    o_ref[...] = jnp.zeros_like(o_ref)

    def put(t, _):
        o_ref[codes[t]] = x_ref[t]
        return 0

    lax.fori_loop(0, x_ref.shape[0], put, 0, unroll=8)


def place(codes, shares):
    return pl.pallas_call(
        place_kernel,
        in_specs=[SM, VM],
        out_specs=VM,
        out_shape=jax.ShapeDtypeStruct((128, 16, 128), BF16),
        name="place_frames",
    )(codes, shares)


def merge_kernel(x_ref, o_ref):
    for j in range(x_ref.shape[0]):
        o_ref[:, :, 128 * j : 128 * (j + 1)] = x_ref[j]


def merge(seq):
    return pl.pallas_call(
        merge_kernel,
        in_specs=[VM],
        out_specs=VM,
        out_shape=jax.ShapeDtypeStruct((8, 16, 2048), BF16),
        name="merge_columns",
    )(seq)


def clip_tables(clip_len, frame_ids):
    ends = jnp.cumsum(clip_len)
    starts = ends - clip_len
    clip_of = jnp.sum((frame_ids[:, None] >= ends[None, :]).astype(jnp.int32), axis=1)
    member = (clip_of[:, None] == jnp.arange(clip_len.shape[0], dtype=jnp.int32)[None, :]).astype(
        jnp.int32
    )
    return clip_of, member, jnp.sum(member * starts[None, :], axis=1)


def swap(x, axis, bit):
    n = lax.axis_size(axis)
    return lax.ppermute(x, axis, [(i, i ^ bit) for i in range(n)])


def shift(x, axis, by):
    n = lax.axis_size(axis)
    return lax.ppermute(x, axis, [(i, i + by) for i in range(n) if 0 <= i + by < n])


def on_device(feat, gamma, beta, conv_weight, conv_bias, proj, proj_bias, clip_len, owner):
    frames, band, width, chans = feat.shape
    latent_ch = proj.shape[1]
    n_time = lax.axis_size("tm")
    n_bands = lax.axis_size("rows")
    tm = lax.axis_index("tm")
    row = lax.axis_index("rows")

    border = shift(jnp.stack([feat[2:, 0], feat[2:, band - 1]], axis=1), "tm", 1)
    past_one = shift(feat[3, 1 : band - 1], "tm", 1)
    past_two = shift(feat[2, 1 : band - 1], "tm", 1)
    top = shift(feat[:, band - 1], "rows", 1)
    bot = shift(feat[:, 0], "rows", -1)
    past_top = shift(border[:, 1], "rows", 1)
    past_bot = shift(border[:, 0], "rows", -1)

    ids = tm * frames + jnp.arange(frames, dtype=jnp.int32)
    clip_of, member, start = clip_tables(clip_len, ids)
    local_start = (start - tm * frames).astype(jnp.int32)
    edges = jnp.stack([row, n_bands - 1 - row]).astype(jnp.int32)
    window = jnp.stack([tm, tm ^ 1, tm - 2, (tm - 2) ^ 1, tm + 2, (tm + 2) ^ 1])
    window_ids = (window[:, None] * frames + jnp.arange(frames)[None, :]).reshape(-1)
    window_clip, _, _ = clip_tables(clip_len, window_ids.astype(jnp.int32))
    same = (clip_of[:, None] == window_clip[None, :]).astype(F32).reshape(frames, 6, frames)
    none = jnp.zeros_like(same)
    mask = jnp.concatenate(
        [jnp.stack([same, none], axis=2), jnp.stack([none, same], axis=2)], axis=0
    ).reshape(2 * frames, 12 * frames)
    length = jnp.sum(member * clip_len[None, :], axis=1)
    count = length.astype(F32) * float(band * n_bands * width * (chans // GROUPS))
    count = jnp.concatenate([count, count])[:, None]
    group = jnp.arange(chans) // (chans // GROUPS)
    group = (group[:, None] == group[None, :]).astype(F32)
    all_ids = jnp.arange(n_time * frames, dtype=jnp.int32)
    _, all_member, all_start = clip_tables(clip_len, all_ids)
    codes = jnp.sum(all_member * owner[None, :], axis=1) * SEQ_CAP + all_ids - all_start
    codes = codes.astype(jnp.int32)

    sums = channel_stats(feat)
    for bit in (1, 2, 4):
        sums = sums + swap(sums, "rows", bit)
    pair = jnp.concatenate([sums, swap(sums, "tm", 1)], axis=0)
    sums = jnp.concatenate([pair, shift(pair, "tm", 2), shift(pair, "tm", -2)], axis=0)

    cbias = conv_bias[None, :]
    projt = jnp.tile(proj, (1, 128 // latent_ch))
    pbias = jnp.tile(proj_bias, 128 // latent_ch)[None, :]
    block, part, early, affine = local_part(
        local_start, edges, feat, top, bot, conv_weight, sums, mask, count, group,
        gamma[None, :], beta[None, :], cbias, projt, pbias,
    )
    block, lat = past_part(
        local_start, edges, past_one, past_two, border, past_top, past_bot, feat, conv_weight,
        part, affine, cbias, projt, pbias, early, block,
    )
    shares = lax.all_to_all(lat, "tm", split_axis=0, concat_axis=0, tiled=True)
    placed = place(codes, shares.reshape(n_time * frames, band, 128))
    seq = lax.all_to_all(
        placed.reshape(n_time, SEQ_CAP, band, 128), "tm", split_axis=0, concat_axis=0, tiled=True
    )
    return block, merge(seq)


def solution(mesh):
    in_specs = (P("tm", "rows", None, None), P(), P(), P(), P(), P(), P(), P(), P())
    out_specs = (P("tm", "rows", None, None), P("tm", "rows", None))
    return jax.shard_map(
        on_device, mesh=mesh, in_specs=in_specs, out_specs=out_specs, check_vma=False
    )
```

time: 396 us -> 140 us (0.35); the launches traced: 389 us -> 139 us
  matrix products: 102 us -> 0 us
  local copies, waits for them, and re-layouts: 107 us -> 8.83 us
  blocking collectives: 82 us -> 15.6 us
  Pallas kernels: 0 us -> 54.2 us
  waiting for transfers between devices: 55.2 us -> 15 us
  starting transfers between devices: 11.5 us -> 40.2 us
  other arithmetic: 29.7 us -> 4.3 us
    dot_general x15 -> x0, matrix products: 102 us -> none  [the longest x9 99.6 us: on_device(): jnp.dot(columns.reshape(-1, 3 * chans), conv_weight[tap_time, tap_row], p...]
    slice x3 -> x0, local copies, waits for them, and re-layouts: 71.2 us -> none  [the longest x2 69.7 us: on_device(): wide[:, tap_time, tap_row:tap_row + band, tap_col:tap_col + width]]
    psum x1 -> x0, blocking collectives: 68.4 us -> none  [on_device(): tot_one, tot_two = lax.psum((part_one, part_two), ('tm', 'rows'))]
    pallas_call x0 -> x5, Pallas kernels: none -> 54.2 us  [the longest x1 41 us: local_part(): pl.pallas_call(local_kernel, in_specs=[SM, SM, ANY, ANY, ANY, ANY] + [VM]...]
    ppermute x3 -> x13, waiting for transfers between devices: 46.9 us -> 5.84 us  [the longest x4 5.82 us: swap(): return lax.ppermute(x, axis, [(i, i ^ bit) for i in range(n)])]
    ppermute x3 -> x13, starting transfers between devices: 4.49 us -> 34.8 us  [the longest x9 28.2 us: shift(): lax.ppermute(x, axis, [(i, i + by) for i in range(n) if 0 <= i + by < n])]
    gather x1 -> x0, local copies, waits for them, and re-layouts: 9.54 us -> none  [on_device(): taps = jnp.take(padded, picks.reshape(-1), axis=0)]
    pad x1 -> x0, local copies, waits for them, and re-layouts: 8.71 us -> none  [on_device(): jnp.pad(taps, ((0, 0), (0, 0), (1, 1), (0, 0)))]
  transfers between devices with their start and end apart: 4 -> 14, of which waited for: 3 -> 4; matrix products, arithmetic and copies ran while one was open for 0% -> 6% of each run, Pallas kernels for 0% -> 30%
where the time goes in v1:
time: 140 us; the launch traced here: 139 us
  Pallas kernels  54.2 us (39%)
  starting transfers between devices  40.2 us (29%)
  blocking collectives  15.6 us (11%)
  waiting for transfers between devices  15 us (11%)
  local copies, waits for them, and re-layouts  8.83 us (6%)
  other arithmetic  4.3 us (3%)
    pallas_call x1, Pallas kernels, local_part(): pl.pallas_call(local_kernel, in_specs=[SM, SM, ANY, ANY, ANY, ANY] + [VM]...  41 us
    ppermute x9, starting transfers between devices, shift(): lax.ppermute(x, axis, [(i, i + by) for i in range(n) if 0 <= i + by < n])  28.2 us
    all_to_all x1, blocking collectives, on_device(): lax.all_to_all(placed.reshape(n_time, SEQ_CAP, band, 128), 'tm', split_ax...  15.6 us
    all_to_all x1, waiting for transfers between devices, on_device(): shares = lax.all_to_all(lat, 'tm', split_axis=0, concat_axis=0, tiled=True)  9.2 us
    pallas_call x1, Pallas kernels, past_part(): pl.pallas_call(past_kernel, in_specs=[SM, SM] + [VM] * 5 + [ANY] * 3 + [V...  8.13 us
    ppermute x4, starting transfers between devices, swap(): return lax.ppermute(x, axis, [(i, i ^ bit) for i in range(n)])  6.56 us
    ppermute x4, waiting for transfers between devices, swap(): return lax.ppermute(x, axis, [(i, i ^ bit) for i in range(n)])  5.82 us
    all_to_all x1, starting transfers between devices, on_device(): shares = lax.all_to_all(lat, 'tm', split_axis=0, concat_axis=0, tiled=True)  5.41 us
  transfers between devices with their start and end apart: 14, of which 4 were waited for; matrix products, arithmetic and copies ran while one was open for 6% of the time, Pallas kernels for 30%

profile of v1, /device:TPU:0, one launch (start us, length us, event | category | flops | bytes accessed | tf_op | source)
XLA Modules:
  0.0 139.1 jit_solution(462546376051199570)
XLA Ops:
  0.6 0.0 copy-start
  0.6 2.2 %copy-done = bf16[4,16,128,256]{3,2,1,0:T(8,128)(2,1)S(1)} copy-done((bf16[4,16,128,256]{3,2,1,0:T(8,128)(2,1)S(1)}, bf16[4,16,128,256]{3,2,1,0:T(8,128)(2,1)}, u32[]{:S(2)}) %copy-start) | copy-done | bytes 4194328
  2.8 1.2 channel_stats.1
  4.0 0.0 copy-start.4
  4.0 0.0 copy-start.2
  4.0 0.1 collective-permute-start.7
  4.2 3.9 %collective-permute-start.2 = (bf16[2,2,128,256]{3,2,0,1:T(8,128)(2,1)S(1)}, bf16[2,2,128,256]{3,2,0,1:T(8,128)(2,1)S(1)}, u32[]{:S(2)}, u32[]{:S(2)}) collective-permute-start(bf16[2,2,128,256]{3,2,0,1:T(8,128)(2,1)S(1)} %pad_maximum_fusion), channel_id=1, source_target_pairs={{0,8},{8,16},{16,24},{24,32},{32,40},{40,48},{48,56},{56,64},{64,7... | collective-permute-start | bytes 786440 | tf_op jit(solution)/shard_map/ppermute | solution.py:396
  8.1 1.3 collective-permute-start.6
  9.4 3.0 %collective-permute-start.5 = (bf16[4,128,256]{2,1,0:T(8,128)(2,1)S(1)}, bf16[4,128,256]{2,1,0:T(8,128)(2,1)S(1)}, u32[]{:S(2)}, u32[]{:S(2)}) collective-permute-start(bf16[4,128,256]{2,1,0:T(8,128)(2,1)S(1)} %get-tuple-element.19), channel_id=1, source_target_pairs={{0,1},{1,2},{2,3},{3,4},{4,5},{5,6},{6,7},{8,9},{9,10},{10,11},{11... | collective-permute-start | bytes 786440 | tf_op jit(solution)/shard_map/ppermute | solution.py:396
  12.5 0.2 slice_bitcast_fusion
  12.7 0.1 stack.49
  12.8 0.1 iota_add_fusion
  12.9 0.1 add.69
  13.0 0.1 copy.30
  13.1 0.1 reduce
  13.2 0.2 convert_reduce_fusion.2
  13.4 0.1 convert_reduce_fusion.1
  13.5 0.2 select_reduce_fusion.2
  13.7 0.6 broadcast_subtract_fusion.starts
  14.3 0.1 eq.65
  14.3 0.1 compare_convert_fusion.1
  14.4 0.8 compare_convert_fusion.group_ref
  15.2 1.6 %collective-permute-start.8 = (f32[8,256]{1,0:T(8,128)S(1)}, f32[8,256]{1,0:T(8,128)S(1)}, u32[]{:S(2)}, u32[]{:S(2)}) collective-permute-start(f32[8,256]{1,0:T(8,128)S(1)} %add.62), channel_id=1, source_target_pairs={{0,2},{1,3},{2,0},{3,1},{4,6},{5,7},{6,4},{7,5},{8,10},{9,11},{10,... | collective-permute-start | bytes 24584 | tf_op jit(solution)/shard_map/ppermute | solution.py:391
  16.8 0.1 convert_reduce_fusion
  16.9 2.1 %collective-permute-done.8 = f32[8,256]{1,0:T(8,128)S(1)} collective-permute-done((f32[8,256]{1,0:T(8,128)S(1)}, f32[8,256]{1,0:T(8,128)S(1)}, u32[]{:S(2)}, u32[]{:S(2)}) %collective-permute-start.8) | collective-permute-done | bytes 8224 | tf_op jit(solution)/shard_map/ppermute | solution.py:391
  19.0 3.0 %collective-permute-start.9 = (f32[8,256]{1,0:T(8,128)S(1)}, f32[8,256]{1,0:T(8,128)S(1)}, u32[]{:S(2)}, u32[]{:S(2)}) collective-permute-start(f32[8,256]{1,0:T(8,128)S(1)} %add.63), channel_id=1, source_target_pairs={{0,4},{1,5},{2,6},{3,7},{4,0},{5,1},{6,2},{7,3},{8,12},{9,13},{10,... | collective-permute-start | bytes 24584 | tf_op jit(solution)/shard_map/ppermute | solution.py:391
  22.0 0.1 select_maximum_fusion
  22.1 2.1 %collective-permute-done.9 = f32[8,256]{1,0:T(8,128)S(1)} collective-permute-done((f32[8,256]{1,0:T(8,128)S(1)}, f32[8,256]{1,0:T(8,128)S(1)}, u32[]{:S(2)}, u32[]{:S(2)}) %collective-permute-start.9) | collective-permute-done | bytes 8224 | tf_op jit(solution)/shard_map/ppermute | solution.py:391
  24.1 1.9 %collective-permute-start.10 = (f32[8,256]{1,0:T(8,128)S(1)}, f32[8,256]{1,0:T(8,128)S(1)}, u32[]{:S(2)}, u32[]{:S(2)}) collective-permute-start(f32[8,256]{1,0:T(8,128)S(1)} %add.64), channel_id=1, source_target_pairs={{0,8},{8,0},{16,24},{24,16},{32,40},{40,32},{48,56},{56,48},{64,72... | collective-permute-start | bytes 24584 | tf_op jit(solution)/shard_map/ppermute | solution.py:391
  26.0 0.1 maximum_bitcast_fusion
  26.1 1.7 %collective-permute-done.10 = f32[8,256]{1,0:T(8,128)S(1)} collective-permute-done((f32[8,256]{1,0:T(8,128)S(1)}, f32[8,256]{1,0:T(8,128)S(1)}, u32[]{:S(2)}, u32[]{:S(2)}) %collective-permute-start.10) | collective-permute-done | bytes 8224 | tf_op jit(solution)/shard_map/ppermute | solution.py:391
  27.8 1.3 collective-permute-start.12
  29.1 6.1 %collective-permute-start.11 = (f32[16,256]{1,0:T(8,128)S(1)}, f32[16,256]{1,0:T(8,128)S(1)}, u32[]{:S(2)}, u32[]{:S(2)}) collective-permute-start(f32[16,256]{1,0:T(8,128)S(1)} %pad_maximum_fusion.2), channel_id=1, source_target_pairs={{0,16},{8,24},{16,32},{24,40},{32,48},{40,56},{48,64},{56,72},{64,... | collective-permute-start | bytes 49160 | tf_op jit(solution)/shard_map/ppermute | solution.py:396
  35.2 0.6 pad_add_fusion.edges
  35.8 0.6 broadcast_in_dim_tile.3.pbias_ref
  36.4 0.7 copy.36.count_ref
  37.1 0.7 copy.35.mask_ref
  37.7 0.7 copy.37.projt_ref
  38.5 3.8 %collective-permute-start.1 = (bf16[14,128,256]{2,1,0:T(8,128)(2,1)S(1)}, bf16[14,128,256]{2,1,0:T(8,128)(2,1)S(1)}, u32[]{:S(2)}, u32[]{:S(2)}) collective-permute-start(bf16[14,128,256]{2,1,0:T(8,128)(2,1)S(1)} %get-tuple-element.22), channel_id=1, source_target_pairs={{0,8},{8,16},{16,24},{24,32},{32,40},{40,48},{48,56},{56,64},{64,7... | collective-permute-start | bytes 2752520 | tf_op jit(solution)/shard_map/ppermute | solution.py:396
  42.3 0.0 collective-permute-done.11
  42.3 4.4 %collective-permute-start = (bf16[14,128,256]{2,1,0:T(8,128)(2,1)S(1)}, bf16[14,128,256]{2,1,0:T(8,128)(2,1)S(1)}, u32[]{:S(2)}, u32[]{:S(2)}) collective-permute-start(bf16[14,128,256]{2,1,0:T(8,128)(2,1)S(1)} %get-tuple-element.23), channel_id=1, source_target_pairs={{0,8},{8,16},{16,24},{24,32},{32,40},{40,48},{48,56},{56,64},{64,7... | collective-permute-start | bytes 2752520 | tf_op jit(solution)/shard_map/ppermute | solution.py:396
  46.7 0.6 pad_maximum_fusion.1.sums_ref
  47.4 0.0 collective-permute-done.2
  47.4 1.3 collective-permute-start.4
  48.7 3.0 %collective-permute-start.3 = (bf16[2,128,256]{2,1,0:T(8,128)(2,1)S(1)}, bf16[2,128,256]{2,1,0:T(8,128)(2,1)S(1)}, u32[]{:S(2)}, u32[]{:S(2)}) collective-permute-start(bf16[2,128,256]{2,1,0:T(8,128)(2,1)S(1)} %get-tuple-element.25), channel_id=1, source_target_pairs={{0,1},{1,2},{2,3},{3,4},{4,5},{5,6},{6,7},{8,9},{9,10},{10,11},{11... | collective-permute-start | bytes 393224 | tf_op jit(solution)/shard_map/ppermute | solution.py:396
  51.8 0.0 collective-permute-done.5.top_hbm
  51.8 0.0 copy-start.9
  51.8 0.7 copy-done.9
  52.5 41.0 %local_conv.1 = (bf16[4,16,128,256]{3,2,1,0:T(8,128)(2,1)}, f32[2,16,128,256]{3,2,1,0:T(8,128)}, bf16[16,2,16,128]{3,2,1,0:T(8,128)(2,1)}, f32[8,256]{1,0:T(8,128)}) custom-call(s32[4]{0:T(128)} %broadcast_subtract_fusion.starts, s32[2]{0:T(128)} %pad_add_fusion.edges, bf16[4,16,128,256]{3,2,1,0:T(8,128)(2,1)} %feat_hbm.3, bf16[4,128,256]{2,1,0:T(8,128)(2,1)} %copy-done.9, ...), custom_call_target="tpu_custom_call" | custom-call | flops 21743271936 | bytes 16777216 | tf_op jit(solution)/shard_map/local_conv/pallas_call | solution.py:204
  93.5 0.7 copy.38.border_ref
  94.2 0.0 collective-permute-done.4.bot_ref
  94.3 0.6 copy-done.10
  94.9 0.0 copy-done.11
  94.9 0.3 copy-done.6
  95.3 0.3 copy-done.7
  95.6 8.1 %past_conv.1 = (bf16[4,16,128,256]{3,2,1,0:T(8,128)(2,1)}, bf16[16,4,16,128]{3,2,1,0:T(8,128)(2,1)}) custom-call(s32[4]{0:T(128)} %broadcast_subtract_fusion.starts, s32[2]{0:T(128)} %pad_add_fusion.edges, bf16[14,128,256]{2,1,0:T(8,128)(2,1)} %copy-done.7, bf16[14,128,256]{2,1,0:T(8,128)(2,1)} %copy-done.6, ...), custom_call_target="tpu_custom_call", output_to_operand_aliasing={{0}: (15, {})} | custom-call | flops 7247757312 | bytes 12582912 | tf_op jit(solution)/shard_map/past_conv/pallas_call | solution.py:316
  103.7 5.4 %all-to-all-start = ((bf16[16,4,16,128]{3,2,1,0:T(8,128)(2,1)}), bf16[16,4,16,128]{3,2,1,0:T(8,128)(2,1)S(1)}, u32[]{:S(2)}, u32[]{:S(2)}) async-start(bf16[16,4,16,128]{3,2,1,0:T(8,128)(2,1)} %get-tuple-element.13), calls=%async_computation | async-start | bytes 524288 | tf_op jit(solution)/shard_map/all_to_all | solution.py:454
  109.1 0.1 select_reduce_fusion.1
  109.2 0.5 add_subtract_fusion.codes
  109.8 9.2 %all-to-all-done = bf16[16,4,16,128]{3,2,1,0:T(8,128)(2,1)S(1)} async-done(((bf16[16,4,16,128]{3,2,1,0:T(8,128)(2,1)}), bf16[16,4,16,128]{3,2,1,0:T(8,128)(2,1)S(1)}, u32[]{:S(2)}, u32[]{:S(2)}) %all-to-all-start) | async-done | bytes 262176 | tf_op jit(solution)/shard_map/all_to_all | solution.py:454
  119.0 0.7 copy-done.1
  119.7 1.9 %place_frames.1 = bf16[128,16,128]{2,1,0:T(8,128)(2,1)} custom-call(s32[64]{0:T(128)} %add_subtract_fusion.codes, bf16[64,16,128]{2,1,0:T(8,128)(2,1)} %bitcast.39), custom_call_target="tpu_custom_call" | custom-call | tf_op jit(solution)/shard_map/place_frames/pallas_call | solution.py:355
  121.6 15.6 %all_to_all.10.x_ref = bf16[16,8,16,128]{3,2,1,0:T(8,128)(2,1)} all-to-all(bf16[16,8,16,128]{3,2,1,0:T(8,128)(2,1)} %bitcast.38), channel_id=1, replica_groups=mesh['tm'=16,'rows'=8] {'tm'}, dimensions={0} | all-to-all | bytes 1048576 | tf_op jit(solution)/shard_map/all_to_all | solution.py:456
  137.2 2.0 %merge_columns.1 = bf16[8,16,2048]{2,1,0:T(8,128)(2,1)} custom-call(bf16[16,8,16,128]{3,2,1,0:T(8,128)(2,1)} %all_to_all.10.x_ref), custom_call_target="tpu_custom_call" | custom-call | tf_op jit(solution)/shard_map/merge_columns/pallas_call | solution.py:370
  (35 shorter events, 0.2 us)
Async XLA Ops:
  0.6 2.2 %copy-start = (bf16[4,16,128,256]{3,2,1,0:T(8,128)(2,1)S(1)}, bf16[4,16,128,256]{3,2,1,0:T(8,128)(2,1)}, u32[]{:S(2)}) copy-start(bf16[4,16,128,256]{3,2,1,0:T(8,128)(2,1)} %feat_hbm.3) | copy-start | bytes 12582916
  2.8 10.1 %copy-start.3 = (s32[16]{0:T(128)S(1)}, s32[16]{0:T(128)}, u32[]{:S(2)}) copy-start(s32[16]{0:T(128)} %param.16) | copy-start | bytes 196
  4.0 31.8 %copy-start.4 = (f32[16]{0:T(128)S(1)}, f32[16]{0:T(128)}, u32[]{:S(2)}) copy-start(f32[16]{0:T(128)} %param.15) | copy-start | bytes 196
  4.0 33.7 %copy-start.2 = (bf16[256,16]{0,1:T(8,128)(2,1)S(1)}, bf16[256,16]{0,1:T(8,128)(2,1)}, u32[]{:S(2)}) copy-start(bf16[256,16]{0,1:T(8,128)(2,1)} %param.14) | copy-start | bytes 24580
  4.0 11.2 %collective-permute-start.7 = (f32[8,256]{1,0:T(8,128)S(1)}, f32[8,256]{1,0:T(8,128)S(1)}, u32[]{:S(2)}, u32[]{:S(2)}) collective-permute-start(f32[8,256]{1,0:T(8,128)S(1)} %channel_stats.1), channel_id=1, source_target_pairs={{0,1},{1,0},{2,3},{3,2},{4,5},{5,4},{6,7},{7,6},{8,9},{9,8},{10,11... | collective-permute-start | bytes 24584 | tf_op jit(solution)/shard_map/ppermute | solution.py:391
  4.2 43.2 %collective-permute-start.2 = (bf16[2,2,128,256]{3,2,0,1:T(8,128)(2,1)S(1)}, bf16[2,2,128,256]{3,2,0,1:T(8,128)(2,1)S(1)}, u32[]{:S(2)}, u32[]{:S(2)}) collective-permute-start(bf16[2,2,128,256]{3,2,0,1:T(8,128)(2,1)S(1)} %pad_maximum_fusion), channel_id=1, source_target_pairs={{0,8},{8,16},{16,24},{24,32},{32,40},{40,48},{48,56},{56,64},{64,7... | collective-permute-start | bytes 786440 | tf_op jit(solution)/shard_map/ppermute | solution.py:396
  8.1 40.5 %collective-permute-start.6 = (bf16[4,128,256]{2,1,0:T(8,128)(2,1)S(1)}, bf16[4,128,256]{2,1,0:T(8,128)(2,1)S(1)}, u32[]{:S(2)}, u32[]{:S(2)}) collective-permute-start(bf16[4,128,256]{2,1,0:T(8,128)(2,1)S(1)} %get-tuple-element.18), channel_id=1, source_target_pairs={{1,0},{2,1},{3,2},{4,3},{5,4},{6,5},{7,6},{9,8},{10,9},{11,10},{12... | collective-permute-start | bytes 786440 | tf_op jit(solution)/shard_map/ppermute | solution.py:396
  9.4 42.3 %collective-permute-start.5 = (bf16[4,128,256]{2,1,0:T(8,128)(2,1)S(1)}, bf16[4,128,256]{2,1,0:T(8,128)(2,1)S(1)}, u32[]{:S(2)}, u32[]{:S(2)}) collective-permute-start(bf16[4,128,256]{2,1,0:T(8,128)(2,1)S(1)} %get-tuple-element.19), channel_id=1, source_target_pairs={{0,1},{1,2},{2,3},{3,4},{4,5},{5,6},{6,7},{8,9},{9,10},{10,11},{11... | collective-permute-start | bytes 786440 | tf_op jit(solution)/shard_map/ppermute | solution.py:396
  15.2 3.7 %collective-permute-start.8 = (f32[8,256]{1,0:T(8,128)S(1)}, f32[8,256]{1,0:T(8,128)S(1)}, u32[]{:S(2)}, u32[]{:S(2)}) collective-permute-start(f32[8,256]{1,0:T(8,128)S(1)} %add.62), channel_id=1, source_target_pairs={{0,2},{1,3},{2,0},{3,1},{4,6},{5,7},{6,4},{7,5},{8,10},{9,11},{10,... | collective-permute-start | bytes 24584 | tf_op jit(solution)/shard_map/ppermute | solution.py:391
  19.0 5.2 %collective-permute-start.9 = (f32[8,256]{1,0:T(8,128)S(1)}, f32[8,256]{1,0:T(8,128)S(1)}, u32[]{:S(2)}, u32[]{:S(2)}) collective-permute-start(f32[8,256]{1,0:T(8,128)S(1)} %add.63), channel_id=1, source_target_pairs={{0,4},{1,5},{2,6},{3,7},{4,0},{5,1},{6,2},{7,3},{8,12},{9,13},{10,... | collective-permute-start | bytes 24584 | tf_op jit(solution)/shard_map/ppermute | solution.py:391
  24.1 3.7 %collective-permute-start.10 = (f32[8,256]{1,0:T(8,128)S(1)}, f32[8,256]{1,0:T(8,128)S(1)}, u32[]{:S(2)}, u32[]{:S(2)}) collective-permute-start(f32[8,256]{1,0:T(8,128)S(1)} %add.64), channel_id=1, source_target_pairs={{0,8},{8,0},{16,24},{24,16},{32,40},{40,32},{48,56},{56,48},{64,72... | collective-permute-start | bytes 24584 | tf_op jit(solution)/shard_map/ppermute | solution.py:391
  27.8 10.7 %collective-permute-start.12 = (f32[16,256]{1,0:T(8,128)S(1)}, f32[16,256]{1,0:T(8,128)S(1)}, u32[]{:S(2)}, u32[]{:S(2)}) collective-permute-start(f32[16,256]{1,0:T(8,128)S(1)} %pad_maximum_fusion.2), channel_id=1, source_target_pairs={{16,0},{24,8},{32,16},{40,24},{48,32},{56,40},{64,48},{72,56},{80,... | collective-permute-start | bytes 49160 | tf_op jit(solution)/shard_map/ppermute | solution.py:396
  29.1 13.2 %collective-permute-start.11 = (f32[16,256]{1,0:T(8,128)S(1)}, f32[16,256]{1,0:T(8,128)S(1)}, u32[]{:S(2)}, u32[]{:S(2)}) collective-permute-start(f32[16,256]{1,0:T(8,128)S(1)} %pad_maximum_fusion.2), channel_id=1, source_target_pairs={{0,16},{8,24},{16,32},{24,40},{32,48},{40,56},{48,64},{56,72},{64,... | collective-permute-start | bytes 49160 | tf_op jit(solution)/shard_map/ppermute | solution.py:396
  38.5 55.8 %collective-permute-start.1 = (bf16[14,128,256]{2,1,0:T(8,128)(2,1)S(1)}, bf16[14,128,256]{2,1,0:T(8,128)(2,1)S(1)}, u32[]{:S(2)}, u32[]{:S(2)}) collective-permute-start(bf16[14,128,256]{2,1,0:T(8,128)(2,1)S(1)} %get-tuple-element.22), channel_id=1, source_target_pairs={{0,8},{8,16},{16,24},{24,32},{32,40},{40,48},{48,56},{56,64},{64,7... | collective-permute-start | bytes 2752520 | tf_op jit(solution)/shard_map/ppermute | solution.py:396
  42.3 52.0 %collective-permute-start = (bf16[14,128,256]{2,1,0:T(8,128)(2,1)S(1)}, bf16[14,128,256]{2,1,0:T(8,128)(2,1)S(1)}, u32[]{:S(2)}, u32[]{:S(2)}) collective-permute-start(bf16[14,128,256]{2,1,0:T(8,128)(2,1)S(1)} %get-tuple-element.23), channel_id=1, source_target_pairs={{0,8},{8,16},{16,24},{24,32},{32,40},{40,48},{48,56},{56,64},{64,7... | collective-permute-start | bytes 2752520 | tf_op jit(solution)/shard_map/ppermute | solution.py:396
  47.4 46.9 %collective-permute-start.4 = (bf16[2,128,256]{2,1,0:T(8,128)(2,1)S(1)}, bf16[2,128,256]{2,1,0:T(8,128)(2,1)S(1)}, u32[]{:S(2)}, u32[]{:S(2)}) collective-permute-start(bf16[2,128,256]{2,1,0:T(8,128)(2,1)S(1)} %get-tuple-element.24), channel_id=1, source_target_pairs={{1,0},{2,1},{3,2},{4,3},{5,4},{6,5},{7,6},{9,8},{10,9},{11,10},{12... | collective-permute-start | bytes 393224 | tf_op jit(solution)/shard_map/ppermute | solution.py:396
  48.7 3.1 %copy-start.8 = (bf16[4,128,256]{2,1,0:T(8,128)(2,1)}, bf16[4,128,256]{2,1,0:T(8,128)(2,1)S(1)}, u32[]{:S(2)}) copy-start(bf16[4,128,256]{2,1,0:T(8,128)(2,1)S(1)} %collective-permute-done.6.bot_hbm) | copy-start | bytes 786436
  48.7 45.5 %collective-permute-start.3 = (bf16[2,128,256]{2,1,0:T(8,128)(2,1)S(1)}, bf16[2,128,256]{2,1,0:T(8,128)(2,1)S(1)}, u32[]{:S(2)}, u32[]{:S(2)}) collective-permute-start(bf16[2,128,256]{2,1,0:T(8,128)(2,1)S(1)} %get-tuple-element.25), channel_id=1, source_target_pairs={{0,1},{1,2},{2,3},{3,4},{4,5},{5,6},{6,7},{8,9},{9,10},{10,11},{11... | collective-permute-start | bytes 393224 | tf_op jit(solution)/shard_map/ppermute | solution.py:396
  51.8 0.7 copy-start.9
  94.2 0.7 copy-start.10
  94.2 0.7 copy-start.11
  94.3 1.0 copy-start.6
  94.3 1.3 copy-start.7
  95.6 13.6 %copy-start.5 = (s32[16]{0:T(128)S(1)}, s32[16]{0:T(128)}, u32[]{:S(2)}) copy-start(s32[16]{0:T(128)} %param.17) | copy-start | bytes 196
  103.7 15.3 %all-to-all-start = ((bf16[16,4,16,128]{3,2,1,0:T(8,128)(2,1)}), bf16[16,4,16,128]{3,2,1,0:T(8,128)(2,1)S(1)}, u32[]{:S(2)}, u32[]{:S(2)}) async-start(bf16[16,4,16,128]{3,2,1,0:T(8,128)(2,1)} %get-tuple-element.13), calls=%async_computation | async-start | bytes 524288 | tf_op jit(solution)/shard_map/all_to_all | solution.py:454
  119.0 0.7 copy-start.1

commit v2 on v1

v2 whole, which is shorter than its diff:
```python
import jax
import jax.numpy as jnp
from jax import lax
from jax.experimental import pallas as pl
from jax.experimental.pallas import tpu as pltpu
from jax.sharding import PartitionSpec as P

GROUPS = 32
SEQ_CAP = 8
CLIPS = 16
NH = 128
LOW = 1000
F32 = jnp.float32
BF16 = jnp.bfloat16
MIB = 2**20
STARTS, ENDS, EDGES, CODES = 0, 4, 8, 16
ANY = pl.BlockSpec(memory_space=pl.ANY)
VM = pl.BlockSpec(memory_space=pltpu.VMEM)
SM = pl.BlockSpec(memory_space=pltpu.SMEM)


def stats_kernel(ints, feat, o_ref, table, edge_ref, past_ref, x_ref, sums, sems, osems):
    frames, band = x_ref.shape[:2]
    quarter = band // 4
    loads = [
        pltpu.make_async_copy(
            feat.at[i // 4, pl.ds((i % 4) * quarter, quarter)],
            x_ref.at[i // 4, pl.ds((i % 4) * quarter, quarter)],
            sems.at[i],
        )
        for i in range(CLIPS)
    ]
    for c in loads:
        c.start()
    passes = [
        pltpu.make_async_copy(feat.at[f, row], edge_ref.at[side, f], osems.at[2 * f + side])
        for f in range(frames)
        for side, row in enumerate((band - 1, 0))
    ]
    passes.append(pltpu.make_async_copy(feat.at[pl.ds(2, 2)], past_ref, osems.at[2 * frames]))
    for c in passes:
        c.start()

    first = ints[0] * 4
    table[EDGES] = (ints[1] > 0).astype(jnp.int32)
    table[EDGES + 1] = (ints[1] < 7).astype(jnp.int32)
    starts = [jnp.int32(0)] * 4
    ends = [jnp.int32(0)] * 4
    start = jnp.int32(0)
    for i in range(CLIPS):
        end = start + ints[2 + i]
        base = ints[2 + CLIPS + i] * SEQ_CAP
        for own in range(4):
            inside = jnp.logical_and(first + own >= start, first + own < end)
            starts[own] = jnp.where(inside, start - first, starts[own])
            ends[own] = jnp.where(inside, end - first, ends[own])
        for k in range(SEQ_CAP):
            table[CODES + start + k] = base + k
        start = end
        loads[i].wait()
        f = i // 4
        x = x_ref[f, pl.ds((i % 4) * quarter, quarter)].astype(F32)
        x = x.reshape(-1, 8, x.shape[-1])
        one = jnp.sum(x, axis=0)
        two = jnp.sum(x * x, axis=0)
        if i % 4 == 0:
            sums[f] = one
            sums[4 + f] = two
        else:
            sums[f] += one
            sums[4 + f] += two
    for own in range(4):
        table[STARTS + own] = starts[own]
        table[ENDS + own] = ends[own]
    tot = jnp.sum(sums[...], axis=1)
    for d in range(o_ref.shape[0]):
        o_ref[d] = tot
    for c in passes:
        c.wait()


def channel_stats(ints, feat, copies):
    frames, band, width, chans = feat.shape
    return pl.pallas_call(
        stats_kernel,
        in_specs=[SM, ANY],
        out_specs=[VM, SM, ANY, ANY],
        out_shape=[
            jax.ShapeDtypeStruct((copies, 2 * frames, chans), F32),
            jax.ShapeDtypeStruct((CODES + 64 + SEQ_CAP,), jnp.int32),
            jax.ShapeDtypeStruct((2, frames, width, chans), BF16),
            jax.ShapeDtypeStruct((2, band, width, chans), BF16),
        ],
        scratch_shapes=[
            pltpu.VMEM(feat.shape, BF16),
            pltpu.VMEM((2 * frames, 8, chans), F32),
            pltpu.SemaphoreType.DMA((CLIPS,)),
            pltpu.SemaphoreType.DMA((2 * frames + 1,)),
        ],
        compiler_params=pltpu.CompilerParams(vmem_limit_bytes=16 * MIB),
        cost_estimate=pl.CostEstimate(flops=LOW, bytes_accessed=LOW, transcendentals=0),
        name="channel_stats",
    )(ints, pltpu.with_memory_space_constraint(feat, pltpu.HBM))


def clip_kernel(ints, table, sums, past_in, edge_in, o_ref, past, edge):
    del past_in, edge_in, past, edge
    shape = (8, sums.shape[0])
    row = lax.broadcasted_iota(jnp.int32, shape, 0)
    col = lax.broadcasted_iota(jnp.int32, shape, 1)
    frame = (col // 8) * 4 + col % 4 - 4 * ints[0]
    start = jnp.zeros(shape, jnp.int32)
    end = jnp.zeros(shape, jnp.int32)
    for f in range(4):
        start = jnp.where(row % 4 == f, table[STARTS + f], start)
        end = jnp.where(row % 4 == f, table[ENDS + f], end)
    inside = jnp.logical_and(frame >= start, frame < end)
    mask = jnp.where(jnp.logical_and(inside, row // 4 == (col // 4) % 2), 1.0, 0.0)
    tot = jnp.dot(mask, sums[...], precision=lax.Precision.HIGHEST, preferred_element_type=F32)
    for d in range(o_ref.shape[0]):
        o_ref[d] = tot


def clip_sums(ints, table, sums, past, edge, copies):
    return pl.pallas_call(
        clip_kernel,
        in_specs=[SM, SM, VM, ANY, ANY],
        out_specs=[VM, ANY, ANY],
        out_shape=[
            jax.ShapeDtypeStruct((copies, 8, sums.shape[1]), F32),
            jax.ShapeDtypeStruct(past.shape, BF16),
            jax.ShapeDtypeStruct(edge.shape, BF16),
        ],
        input_output_aliases={3: 1, 4: 2},
        compiler_params=pltpu.CompilerParams(vmem_limit_bytes=4 * MIB),
        cost_estimate=pl.CostEstimate(flops=LOW, bytes_accessed=LOW, transcendentals=0),
        name="clip_sums",
    )(ints, table, sums, past, edge)


def sides_kernel(near, top, bot, sides, sem):
    del near
    copies = [
        pltpu.make_async_copy(src.at[pl.ds(2, 2)], sides.at[k], sem.at[k])
        for k, src in enumerate((top, bot))
    ]
    for c in copies:
        c.start()
    for c in copies:
        c.wait()


def pack_sides(near, top, bot):
    return pl.pallas_call(
        sides_kernel,
        in_specs=[ANY] * 3,
        out_specs=ANY,
        out_shape=jax.ShapeDtypeStruct((2, 2) + top.shape[1:], BF16),
        scratch_shapes=[pltpu.SemaphoreType.DMA((2,))],
        compiler_params=pltpu.CompilerParams(vmem_limit_bytes=4 * MIB),
        cost_estimate=pl.CostEstimate(flops=LOW, bytes_accessed=LOW, transcendentals=0),
        name="pack_sides",
    )(near, top, bot)


def normed_rows(x, half_scale, half_shift):
    u = x.astype(F32) * half_scale + half_shift
    return u + u * jnp.tanh(u)


def put_rows(slab, row, h):
    width, chans = h.shape
    col = lax.broadcasted_iota(jnp.int32, h.shape, 0)
    left = jnp.where(col == 0, 0.0, pltpu.roll(h, 1, 0))
    right = jnp.where(col == width - 1, 0.0, pltpu.roll(h, width - 1, 0))
    slab[row, :, 0:chans] = left.astype(BF16)
    slab[row, :, chans : 2 * chans] = h.astype(BF16)
    slab[row, :, 2 * chans :] = right.astype(BF16)


def tap_dots(total, slab, weights, row, rows):
    for tap_row in range(3):
        lhs = slab[pl.ds(row + tap_row, rows)]
        lhs = lhs.reshape(rows * lhs.shape[1], lhs.shape[2])
        total = total + jnp.dot(lhs, weights[tap_row], preferred_element_type=F32)
    return total


def spread_latent(proj_ref, pbias_ref, projt, pbias):
    latent_ch, wide = proj_ref.shape[0], projt.shape[1]
    z = lax.broadcasted_iota(jnp.int32, (latent_ch, wide), 0)
    lane = lax.broadcasted_iota(jnp.int32, (latent_ch, wide), 1)
    spread = (lane % latent_ch == z).astype(F32)
    projt[...] = lax.dot_general(
        proj_ref[...], spread.astype(BF16), (((0,), (0,)), ((), ())), preferred_element_type=F32
    ).astype(BF16)
    pbias[...] = jnp.dot(
        pbias_ref[...], spread, precision=lax.Precision.HIGHEST, preferred_element_type=F32
    )


def latent_frame(block, projt, pbias, lscr, lat_ref, f):
    rows, width, chans = block.shape
    wide = projt.shape[1]
    per = wide // 16
    both = jnp.dot(
        block.reshape(rows * width, chans), projt[...], preferred_element_type=F32
    ).reshape(rows, width, wide)
    col = lax.broadcasted_iota(jnp.int32, both.shape, 1)
    lane = lax.broadcasted_iota(jnp.int32, both.shape, 2)
    lscr[...] = jnp.where(col % per == lane // 16, both, 0.0)
    for j in range(width // per):
        part = jnp.sum(lscr[:, per * j : per * (j + 1), :], axis=1) + pbias[...]
        lat_ref[j, f] = part.astype(BF16)


def local_kernel(
    table, feat, top, bot, w, near, gamma_ref, beta_ref, cbias_ref, proj_ref, pbias_ref,
    block_hbm, part, lat_ref, affine_ref,
    slab, obuf, lscr, projt, pbias, osems,
):
    tot = jnp.sum(near[...], axis=0)
    chans = tot.shape[1]
    per = chans // GROUPS
    group = (
        lax.broadcasted_iota(jnp.int32, (chans, chans), 0) // per
        == lax.broadcasted_iota(jnp.int32, (chans, chans), 1) // per
    ).astype(F32)
    tot = jnp.dot(tot, group, precision=lax.Precision.HIGHEST, preferred_element_type=F32)
    for f in range(4):
        count = ((table[ENDS + f] - table[STARTS + f]) * (NH * feat.shape[2] * per)).astype(F32)
        mean = tot[f : f + 1] / count
        var = tot[4 + f : 5 + f] / count - mean * mean
        scale = lax.rsqrt(var + 1e-06) * gamma_ref[...]
        affine_ref[f : f + 1] = 0.5 * scale
        affine_ref[4 + f : 5 + f] = 0.5 * (beta_ref[...] - mean * scale)
    spread_latent(proj_ref, pbias_ref, projt, pbias)

    starts = [table[STARTS + f] for f in range(4)]
    top_on = table[EDGES].astype(F32)
    bot_on = table[EDGES + 1].astype(F32)
    for f in range(4):
        hs = affine_ref[f : f + 1]
        hb = affine_ref[4 + f : 5 + f]
        page = slab.at[f]
        put_rows(page, 0, normed_rows(top[f], hs, hb) * top_on)
        put_rows(page, 17, normed_rows(bot[f], hs, hb) * bot_on)

        def norm_row(r, _, f=f, hs=hs, hb=hb, page=page):
            put_rows(page, r + 1, normed_rows(feat[f, r], hs, hb))
            return 0

        lax.fori_loop(0, 16, norm_row, 0, unroll=2)

    rows = 8
    zero = jnp.zeros((rows * 128, 256), F32)
    outs = []
    for f in (3, 2):
        src = [jnp.maximum(f - 2 + a, starts[f]) for a in range(3)]

        def chunk(m, _, f=f, src=src):
            total = zero
            for a in range(3):
                total = tap_dots(total, slab.at[src[a]], w.at[a], m * rows, rows)
            total = total.reshape(rows, 128, 256)
            r = pl.ds(m * rows, rows)
            obuf[f - 2, r] = (total + feat[f, r].astype(F32) + cbias_ref[...]).astype(BF16)
            return 0

        lax.fori_loop(0, 2, chunk, 0)
        c = pltpu.make_async_copy(obuf.at[f - 2], block_hbm.at[f], osems.at[f - 2])
        c.start()
        outs.append(c)
        latent_frame(obuf[f - 2], projt, pbias, lscr, lat_ref, f - 2)

    src1 = jnp.maximum(0, starts[1])

    def chunk1(m, _):
        total = tap_dots(zero, slab.at[1], w.at[2], m * rows, rows)
        total = tap_dots(total, slab.at[src1], w.at[1], m * rows, rows)
        part[1, pl.ds(m * rows, rows)] = total.reshape(rows, 128, 256)
        return 0

    lax.fori_loop(0, 2, chunk1, 0)

    def chunk0(m, _):
        total = tap_dots(zero, slab.at[0], w.at[2], m * rows, rows)
        part[0, pl.ds(m * rows, rows)] = total.reshape(rows, 128, 256)
        return 0

    lax.fori_loop(0, 2, chunk0, 0)

    @pl.when(starts[1] >= 0)
    def _():
        def more(m, _):
            r = pl.ds(m * rows, rows)
            total = part[1, r].reshape(rows * 128, 256)
            total = tap_dots(total, slab.at[src1], w.at[0], m * rows, rows)
            part[1, r] = total.reshape(rows, 128, 256)
            return 0

        lax.fori_loop(0, 2, more, 0)

    @pl.when(starts[0] >= 0)
    def _():
        def more(m, _):
            r = pl.ds(m * rows, rows)
            total = part[0, r].reshape(rows * 128, 256)
            total = tap_dots(total, slab.at[0], w.at[0], m * rows, rows)
            total = tap_dots(total, slab.at[0], w.at[1], m * rows, rows)
            part[0, r] = total.reshape(rows, 128, 256)
            return 0

        lax.fori_loop(0, 2, more, 0)

    for c in outs:
        c.wait()


def local_part(table, feat, top, bot, weight, near, gamma, beta, cbias, proj, pbias):
    shape = feat.shape
    return pl.pallas_call(
        local_kernel,
        in_specs=[SM] + [VM] * 10,
        out_specs=[ANY, VM, VM, VM],
        out_shape=[
            jax.ShapeDtypeStruct(shape, BF16),
            jax.ShapeDtypeStruct((2,) + shape[1:], F32),
            jax.ShapeDtypeStruct((16, 2, 16, 128), BF16),
            jax.ShapeDtypeStruct((8, 256), F32),
        ],
        scratch_shapes=[
            pltpu.VMEM((4, 18, 128, 768), BF16),
            pltpu.VMEM((2, 16, 128, 256), BF16),
            pltpu.VMEM((16, 128, 128), F32),
            pltpu.VMEM((256, 128), BF16),
            pltpu.VMEM((1, 128), F32),
            pltpu.SemaphoreType.DMA((2,)),
        ],
        compiler_params=pltpu.CompilerParams(vmem_limit_bytes=36 * MIB),
        cost_estimate=pl.CostEstimate(flops=LOW, bytes_accessed=LOW, transcendentals=0),
        name="local_conv",
    )(table, feat, top, bot, weight, near, gamma, beta, cbias, proj, pbias)


def past_kernel(
    table, past, sides, feat, w, part_in, affine_ref, cbias_ref, proj_ref, pbias_ref, early_ref,
    block_in,
    block_hbm, lat_ref,
    slab, obuf, part, lscr, projt, pbias, osems,
):
    del block_in
    spread_latent(proj_ref, pbias_ref, projt, pbias)
    starts = [table[STARTS + f] for f in range(2)]
    top_on = table[EDGES].astype(F32)
    bot_on = table[EDGES + 1].astype(F32)
    hs = affine_ref[0:1]
    hb = affine_ref[4:5]
    for p in range(2):
        @pl.when(starts[0] < p - 1)
        def _(p=p):
            page = slab.at[p]
            put_rows(page, 0, normed_rows(sides[0, p], hs, hb) * top_on)
            put_rows(page, 17, normed_rows(sides[1, p], hs, hb) * bot_on)

            def norm_row(r, _):
                put_rows(page, r + 1, normed_rows(past[p, r], hs, hb))
                return 0

            lax.fori_loop(0, 16, norm_row, 0, unroll=2)
    part[...] = part_in[...]
    rows = 8

    @pl.when(starts[1] < 0)
    def _():
        def more(m, _):
            r = pl.ds(m * rows, rows)
            total = part[1, r].reshape(rows * 128, 256)
            total = tap_dots(total, slab.at[1], w.at[0], m * rows, rows)
            part[1, r] = total.reshape(rows, 128, 256)
            return 0

        lax.fori_loop(0, 2, more, 0)

    src0 = jnp.clip(starts[0] + 2, 0, 1)

    @pl.when(starts[0] < 0)
    def _():
        def more(m, _):
            r = pl.ds(m * rows, rows)
            total = part[0, r].reshape(rows * 128, 256)
            total = tap_dots(total, slab.at[1], w.at[1], m * rows, rows)
            total = tap_dots(total, slab.at[src0], w.at[0], m * rows, rows)
            part[0, r] = total.reshape(rows, 128, 256)
            return 0

        lax.fori_loop(0, 2, more, 0)

    outs = []
    for f in (1, 0):
        def finish(r, _, f=f):
            rr = pl.ds(r * 2, 2)
            obuf[f, rr] = (part[f, rr] + feat[f, rr].astype(F32) + cbias_ref[...]).astype(BF16)
            return 0

        lax.fori_loop(0, 8, finish, 0)
        c = pltpu.make_async_copy(obuf.at[f], block_hbm.at[f], osems.at[f])
        c.start()
        outs.append(c)
        latent_frame(obuf[f], projt, pbias, lscr, lat_ref, f)
    lat_ref[:, 2:4] = early_ref[...]
    for c in outs:
        c.wait()


def past_part(table, past, sides, feat, weight, part, affine, cbias, proj, pbias, early, block):
    shape = feat.shape
    head = pl.BlockSpec((2,) + shape[1:], lambda i: (0, 0, 0, 0))
    return pl.pallas_call(
        past_kernel,
        grid=(1,),
        in_specs=[SM, VM, VM, head, pl.BlockSpec((2,) + weight.shape[1:], lambda i: (0, 0, 0, 0))]
        + [VM] * 6
        + [ANY],
        out_specs=[ANY, VM],
        out_shape=[
            jax.ShapeDtypeStruct(shape, BF16),
            jax.ShapeDtypeStruct((16, 4, 16, 128), BF16),
        ],
        input_output_aliases={11: 0},
        scratch_shapes=[
            pltpu.VMEM((2, 18, 128, 768), BF16),
            pltpu.VMEM((2, 16, 128, 256), BF16),
            pltpu.VMEM((2, 16, 128, 256), F32),
            pltpu.VMEM((16, 128, 128), F32),
            pltpu.VMEM((256, 128), BF16),
            pltpu.VMEM((1, 128), F32),
            pltpu.SemaphoreType.DMA((2,)),
        ],
        compiler_params=pltpu.CompilerParams(vmem_limit_bytes=36 * MIB),
        cost_estimate=pl.CostEstimate(flops=LOW, bytes_accessed=LOW, transcendentals=0),
        name="past_conv",
    )(table, past, sides, feat, weight, part, affine, cbias, proj, pbias, early, block)


def place_kernel(table, x_ref, o_ref):
    o_ref[...] = jnp.zeros_like(o_ref)

    def put(t, _):
        o_ref[table[CODES + t]] = x_ref[t]
        return 0

    lax.fori_loop(0, x_ref.shape[0], put, 0, unroll=8)


def place(table, shares):
    return pl.pallas_call(
        place_kernel,
        in_specs=[SM, VM],
        out_specs=VM,
        out_shape=jax.ShapeDtypeStruct((128, 16, 128), BF16),
        compiler_params=pltpu.CompilerParams(vmem_limit_bytes=4 * MIB),
        name="place_frames",
    )(table, shares)


def merge_kernel(x_ref, o_ref):
    for j in range(x_ref.shape[0]):
        o_ref[:, :, 128 * j : 128 * (j + 1)] = x_ref[j]


def merge(seq):
    return pl.pallas_call(
        merge_kernel,
        in_specs=[VM],
        out_specs=VM,
        out_shape=jax.ShapeDtypeStruct((8, 16, 2048), BF16),
        compiler_params=pltpu.CompilerParams(vmem_limit_bytes=4 * MIB),
        name="merge_columns",
    )(seq)


def shift(x, axis, by):
    n = lax.axis_size(axis)
    return lax.ppermute(x, axis, [(i, i + by) for i in range(n) if 0 <= i + by < n])


def on_device(feat, gamma, beta, conv_weight, conv_bias, proj, proj_bias, clip_len, owner):
    frames, band = feat.shape[:2]
    n_time = lax.axis_size("tm")

    place_of = jnp.stack([lax.axis_index("tm"), lax.axis_index("rows")]).astype(jnp.int32)
    ints = jnp.concatenate([place_of, clip_len, owner])
    sums, table, edge, past = channel_stats(ints, feat, n_time)
    sums = lax.all_to_all(sums, "tm", split_axis=0, concat_axis=0, tiled=True)
    sums, past, edge = clip_sums(
        ints, table, sums.reshape(-1, sums.shape[-1]), past, edge, lax.axis_size("rows")
    )
    past = shift(past, "tm", 1)
    top, bot = shift(edge[0], "rows", 1), shift(edge[1], "rows", -1)
    near = lax.all_to_all(sums, "rows", split_axis=0, concat_axis=0, tiled=True)
    sides = shift(pack_sides(near, top, bot), "tm", 1)

    cbias, pbias = conv_bias[None, :], proj_bias[None, :]
    block, part, early, affine = local_part(
        table, feat, top, bot, conv_weight, near, gamma[None, :], beta[None, :], cbias, proj.T,
        pbias,
    )
    block, lat = past_part(
        table, past, sides, feat, conv_weight, part, affine, cbias, proj.T, pbias, early, block
    )
    shares = lax.all_to_all(lat, "tm", split_axis=0, concat_axis=0, tiled=True)
    placed = place(table, shares.reshape(n_time * frames, band, 128))
    seq = lax.all_to_all(
        placed.reshape(n_time, SEQ_CAP, band, 128), "tm", split_axis=0, concat_axis=0, tiled=True
    )
    return block, merge(seq)


def solution(mesh):
    in_specs = (P("tm", "rows", None, None), P(), P(), P(), P(), P(), P(), P(), P())
    out_specs = (P("tm", "rows", None, None), P("tm", "rows", None))
    return jax.shard_map(
        on_device, mesh=mesh, in_specs=in_specs, out_specs=out_specs, check_vma=False
    )
```

time: 140 us -> 118 us (0.84)
  blocking collectives: 15.6 us -> 57.8 us
  starting transfers between devices: 40.2 us -> 9.64 us
  waiting for transfers between devices: 15 us -> 0.01 us
  local copies, waits for them, and re-layouts: 8.83 us -> 0.07 us
  Pallas kernels: 54.2 us -> 47.8 us
  other arithmetic: 4.3 us -> 0.75 us
    all_to_all x0 -> x3, blocking collectives: none -> 44.3 us  [the longest x1 18.4 us: on_device(): shares = lax.all_to_all(lat, 'tm', split_axis=0, concat_axis=0, tiled=True)]
    ppermute x9 -> x4, starting transfers between devices: 28.2 us -> 9.64 us  [shift(): lax.ppermute(x, axis, [(i, i + by) for i in range(n) if 0 <= i + by < n])]
    all_to_all x1 -> x0, waiting for transfers between devices: 9.2 us -> none  [on_device(): shares = lax.all_to_all(lat, 'tm', split_axis=0, concat_axis=0, tiled=True)]
    ppermute x4 -> x0, starting transfers between devices: 6.56 us -> none  [swap(): return lax.ppermute(x, axis, [(i, i ^ bit) for i in range(n)])]
    ppermute x4 -> x0, waiting for transfers between devices: 5.82 us -> none  [swap(): return lax.ppermute(x, axis, [(i, i ^ bit) for i in range(n)])]
    all_to_all x1 -> x0, starting transfers between devices: 5.41 us -> none  [on_device(): shares = lax.all_to_all(lat, 'tm', split_axis=0, concat_axis=0, tiled=True)]
    unnamed x25 -> x14, local copies, waits for them, and re-layouts: 4.88 us -> 0.04 us
    pallas_call x3 -> x5, Pallas kernels: 50.3 us -> 46.1 us  [the longest x1 36.9 us: local_part(): pl.pallas_call(local_kernel, in_specs=[SM] + [VM] * 10, out_specs=[ANY, V...]
  transfers between devices with their start and end apart: 14 -> 4, of which waited for: 4 -> 0; matrix products, arithmetic and copies ran while one was open for 6% -> 0% of each run, Pallas kernels for 30% -> 32%
where the time goes in v2:
time: 118 us; the launch traced here: 117 us
  blocking collectives  57.8 us (49%)
  Pallas kernels  47.8 us (41%)
  starting transfers between devices  9.64 us (8%)
    pallas_call x1, Pallas kernels, local_part(): pl.pallas_call(local_kernel, in_specs=[SM] + [VM] * 10, out_specs=[ANY, V...  36.9 us
    all_to_all x1, blocking collectives, on_device(): shares = lax.all_to_all(lat, 'tm', split_axis=0, concat_axis=0, tiled=True)  18.4 us
    all_to_all x1, blocking collectives, on_device(): sums = lax.all_to_all(sums, 'tm', split_axis=0, concat_axis=0, tiled=True)  15.8 us
    all_to_all x1, blocking collectives, on_device(): lax.all_to_all(placed.reshape(n_time, SEQ_CAP, band, 128), 'tm', split_ax...  13.6 us
    all_to_all x1, blocking collectives, on_device(): near = lax.all_to_all(sums, 'rows', split_axis=0, concat_axis=0, tiled=True)  10.1 us
    ppermute x4, starting transfers between devices, shift(): lax.ppermute(x, axis, [(i, i + by) for i in range(n) if 0 <= i + by < n])  9.64 us
    pallas_call x1, Pallas kernels, channel_stats(): pl.pallas_call(stats_kernel, in_specs=[SM, ANY], out_specs=[VM, SM, ANY,...  4.65 us
    pallas_call x1, Pallas kernels, past_part(): pl.pallas_call(past_kernel, grid=(1,), in_specs=[SM, VM, VM, head, pl.Blo...  3.47 us
  transfers between devices with their start and end apart: 4, of which 0 were waited for; matrix products, arithmetic and copies ran while one was open for 0% of the time, Pallas kernels for 32%

profile of v2, /device:TPU:0, one launch (start us, length us, event | category | flops | bytes accessed | tf_op | source)
XLA Modules:
  0.0 116.9 jit_solution(7573744074672999355)
XLA Ops:
  0.6 0.8 pad_add_fusion.ints
  1.4 0.0 copy-start
  1.4 0.0 copy-start.1
  1.4 0.0 copy-start.2
  1.4 0.0 copy-start.3
  1.4 0.0 copy-start.4
  1.4 0.0 copy-start.5
  1.4 0.0 copy-start.6
  1.4 4.7 %channel_stats.1 = (f32[16,8,256]{2,1,0:T(8,128)S(1)}, s32[88]{0:T(128)S(1)}, bf16[2,4,128,256]{3,2,1,0:T(8,128)(2,1)S(1)}, bf16[2,16,128,256]{3,2,1,0:T(8,128)(2,1)S(1)}) custom-call(s32[34]{0:T(128)S(1)} %pad_add_fusion.ints, bf16[4,16,128,256]{3,2,1,0:T(8,128)(2,1)} %feat.5), custom_call_target="tpu_custom_call" | custom-call | flops 1000 | bytes 1000 | tf_op jit(solution)/shard_map/channel_stats/pallas_call | solution.py:84
  6.1 15.8 %all_to_all.20 = f32[16,8,256]{2,1,0:T(8,128)S(1)} all-to-all(f32[16,8,256]{2,1,0:T(8,128)S(1)} %get-tuple-element.16), channel_id=1, replica_groups=mesh['tm'=16,'rows'=8] {'tm'}, dimensions={0} | all-to-all | bytes 262144 | tf_op jit(solution)/shard_map/all_to_all | solution.py:495
  21.9 0.7 clip_sums.1
  22.6 2.5 %collective-permute-start = (bf16[2,16,128,256]{3,2,1,0:T(8,128)(2,1)S(1)}, bf16[2,16,128,256]{3,2,1,0:T(8,128)(2,1)S(1)}, u32[]{:S(2)}, u32[]{:S(2)}) collective-permute-start(bf16[2,16,128,256]{3,2,1,0:T(8,128)(2,1)S(1)} %get-tuple-element.19), channel_id=1, source_target_pairs={{0,8},{8,16},{16,24},{24,32},{32,40},{40,48},{48,56},{56,64},{64,7... | collective-permute-start | bytes 6291464 | tf_op jit(solution)/shard_map/ppermute | solution.py:485
  25.2 1.3 %collective-permute-start.2 = (bf16[4,128,256]{2,1,0:T(8,128)(2,1)S(1)}, bf16[4,128,256]{2,1,0:T(8,128)(2,1)S(1)}, u32[]{:S(2)}, u32[]{:S(2)}) collective-permute-start(bf16[4,128,256]{2,1,0:T(8,128)(2,1)S(1)} %get-tuple-element.28), channel_id=1, source_target_pairs={{1,0},{2,1},{3,2},{4,3},{5,4},{6,5},{7,6},{9,8},{10,9},{11,10},{12... | collective-permute-start | bytes 786440 | tf_op jit(solution)/shard_map/ppermute | solution.py:485
  26.5 3.0 %collective-permute-start.1 = (bf16[4,128,256]{2,1,0:T(8,128)(2,1)S(1)}, bf16[4,128,256]{2,1,0:T(8,128)(2,1)S(1)}, u32[]{:S(2)}, u32[]{:S(2)}) collective-permute-start(bf16[4,128,256]{2,1,0:T(8,128)(2,1)S(1)} %get-tuple-element.29), channel_id=1, source_target_pairs={{0,1},{1,2},{2,3},{3,4},{4,5},{5,6},{6,7},{8,9},{9,10},{10,11},{11... | collective-permute-start | bytes 786440 | tf_op jit(solution)/shard_map/ppermute | solution.py:485
  29.5 10.1 %all_to_all.21.near = f32[8,8,256]{2,1,0:T(8,128)S(1)} all-to-all(f32[8,8,256]{2,1,0:T(8,128)S(1)} %get-tuple-element.20), channel_id=1, replica_groups=mesh['tm'=16,'rows'=8] {'rows'}, dimensions={0} | all-to-all | bytes 131072 | tf_op jit(solution)/shard_map/all_to_all | solution.py:501
  39.6 0.0 collective-permute-done.2.bot
  39.6 0.0 collective-permute-done.1.top
  39.6 0.4 pack_sides.1
  40.0 2.8 %collective-permute-start.3 = (bf16[2,2,128,256]{3,2,1,0:T(8,128)(2,1)S(1)}, bf16[2,2,128,256]{3,2,1,0:T(8,128)(2,1)S(1)}, u32[]{:S(2)}, u32[]{:S(2)}) collective-permute-start(bf16[2,2,128,256]{3,2,1,0:T(8,128)(2,1)S(1)} %pack_sides.1), channel_id=1, source_target_pairs={{0,8},{8,16},{16,24},{24,32},{32,40},{40,48},{48,56},{56,64},{64,7... | collective-permute-start | bytes 786440 | tf_op jit(solution)/shard_map/ppermute | solution.py:485
  42.8 0.0 copy-done
  42.8 0.0 copy-done.1
  42.8 0.0 copy-done.2
  42.8 0.0 copy-done.3
  42.8 0.0 copy-done.4
  42.9 0.0 copy-done.5
  42.9 0.0 copy-done.6
  42.9 36.9 %local_conv.1 = (bf16[4,16,128,256]{3,2,1,0:T(8,128)(2,1)}, f32[2,16,128,256]{3,2,1,0:T(8,128)S(1)}, bf16[16,2,16,128]{3,2,1,0:T(8,128)(2,1)S(1)}, f32[8,256]{1,0:T(8,128)S(1)}) custom-call(s32[88]{0:T(128)S(1)} %get-tuple-element.15.table, bf16[4,16,128,256]{3,2,1,0:T(8,128)(2,1)S(1)} %copy-done, bf16[4,128,256]{2,1,0:T(8,128)(2,1)S(1)} %collective-permute-done.1.top, ...), custom_call_target="tpu_custom_call" | custom-call | flops 1000 | bytes 1000 | tf_op jit(solution)/shard_map/local_conv/pallas_call | solution.py:322
  79.8 0.0 collective-permute-done.3.sides
  79.8 0.0 collective-permute-done.past
  79.8 3.5 %past_conv.1 = (bf16[4,16,128,256]{3,2,1,0:T(8,128)(2,1)}, bf16[16,4,16,128]{3,2,1,0:T(8,128)(2,1)S(1)}) custom-call(s32[88]{0:T(128)S(1)} %get-tuple-element.15.table, bf16[2,16,128,256]{3,2,1,0:T(8,128)(2,1)S(1)} %collective-permute-done.past, bf16[2,2,128,256]{3,2,1,0:T(8,128)(2,1)S(1)} %collective-permute-done.3.sides, ...), custom_call_target="tpu_custom_call", output_to_operand_aliasing={{0}: (11, {})} | custom-call | flops 1000 | bytes 1000 | tf_op jit(solution)/shard_map/past_conv/pallas_call | solution.py:419
  83.3 18.4 %all_to_all.22 = bf16[16,4,16,128]{3,2,1,0:T(8,128)(2,1)S(1)} all-to-all(bf16[16,4,16,128]{3,2,1,0:T(8,128)(2,1)S(1)} %get-tuple-element.27), channel_id=1, replica_groups=mesh['tm'=16,'rows'=8] {'tm'}, dimensions={0} | all-to-all | bytes 524288 | tf_op jit(solution)/shard_map/all_to_all | solution.py:512
  101.7 0.7 place_frames.1
  102.4 13.6 %all_to_all.23.x_ref = bf16[16,8,16,128]{3,2,1,0:T(8,128)(2,1)S(1)} all-to-all(bf16[16,8,16,128]{3,2,1,0:T(8,128)(2,1)S(1)} %bitcast.14), channel_id=1, replica_groups=mesh['tm'=16,'rows'=8] {'tm'}, dimensions={0} | all-to-all | bytes 1048576 | tf_op jit(solution)/shard_map/all_to_all | solution.py:514
  116.0 0.9 merge_columns.1
  (1 shorter events, 0.0 us)
Async XLA Ops:
  1.4 41.4 %copy-start = (bf16[4,16,128,256]{3,2,1,0:T(8,128)(2,1)S(1)}, bf16[4,16,128,256]{3,2,1,0:T(8,128)(2,1)}, u32[]{:S(2)}) copy-start(bf16[4,16,128,256]{3,2,1,0:T(8,128)(2,1)} %feat.5) | copy-start | bytes 12582916
  1.4 41.4 %copy-start.1 = (bf16[3,3,768,256]{3,2,1,0:T(8,128)(2,1)S(1)}, bf16[3,3,768,256]{3,2,1,0:T(8,128)(2,1)}, u32[]{:S(2)}) copy-start(bf16[3,3,768,256]{3,2,1,0:T(8,128)(2,1)} %w.3) | copy-start | bytes 10616836
  1.4 41.4 %copy-start.2 = (bf16[256,16]{0,1:T(8,128)(2,1)S(1)}, bf16[256,16]{0,1:T(8,128)(2,1)}, u32[]{:S(2)}) copy-start(bf16[256,16]{0,1:T(8,128)(2,1)} %param.14) | copy-start | bytes 24580
  1.4 41.4 %copy-start.3 = (f32[256]{0:T(256)S(1)}, f32[256]{0:T(256)}, u32[]{:S(2)}) copy-start(f32[256]{0:T(256)} %param.13) | copy-start | bytes 3076
  1.4 41.4 %copy-start.4 = (f32[16]{0:T(128)S(1)}, f32[16]{0:T(128)}, u32[]{:S(2)}) copy-start(f32[16]{0:T(128)} %param.15) | copy-start | bytes 196
  1.4 41.4 %copy-start.5 = (f32[256]{0:T(256)S(1)}, f32[256]{0:T(256)}, u32[]{:S(2)}) copy-start(f32[256]{0:T(256)} %param.10) | copy-start | bytes 3076
  1.4 41.4 %copy-start.6 = (f32[256]{0:T(256)S(1)}, f32[256]{0:T(256)}, u32[]{:S(2)}) copy-start(f32[256]{0:T(256)} %param.11) | copy-start | bytes 3076
  22.6 57.2 %collective-permute-start = (bf16[2,16,128,256]{3,2,1,0:T(8,128)(2,1)S(1)}, bf16[2,16,128,256]{3,2,1,0:T(8,128)(2,1)S(1)}, u32[]{:S(2)}, u32[]{:S(2)}) collective-permute-start(bf16[2,16,128,256]{3,2,1,0:T(8,128)(2,1)S(1)} %get-tuple-element.19), channel_id=1, source_target_pairs={{0,8},{8,16},{16,24},{24,32},{32,40},{40,48},{48,56},{56,64},{64,7... | collective-permute-start | bytes 6291464 | tf_op jit(solution)/shard_map/ppermute | solution.py:485
  25.2 14.5 %collective-permute-start.2 = (bf16[4,128,256]{2,1,0:T(8,128)(2,1)S(1)}, bf16[4,128,256]{2,1,0:T(8,128)(2,1)S(1)}, u32[]{:S(2)}, u32[]{:S(2)}) collective-permute-start(bf16[4,128,256]{2,1,0:T(8,128)(2,1)S(1)} %get-tuple-element.28), channel_id=1, source_target_pairs={{1,0},{2,1},{3,2},{4,3},{5,4},{6,5},{7,6},{9,8},{10,9},{11,10},{12... | collective-permute-start | bytes 786440 | tf_op jit(solution)/shard_map/ppermute | solution.py:485
  26.5 13.2 %collective-permute-start.1 = (bf16[4,128,256]{2,1,0:T(8,128)(2,1)S(1)}, bf16[4,128,256]{2,1,0:T(8,128)(2,1)S(1)}, u32[]{:S(2)}, u32[]{:S(2)}) collective-permute-start(bf16[4,128,256]{2,1,0:T(8,128)(2,1)S(1)} %get-tuple-element.29), channel_id=1, source_target_pairs={{0,1},{1,2},{2,3},{3,4},{4,5},{5,6},{6,7},{8,9},{9,10},{10,11},{11... | collective-permute-start | bytes 786440 | tf_op jit(solution)/shard_map/ppermute | solution.py:485
  40.0 39.8 %collective-permute-start.3 = (bf16[2,2,128,256]{3,2,1,0:T(8,128)(2,1)S(1)}, bf16[2,2,128,256]{3,2,1,0:T(8,128)(2,1)S(1)}, u32[]{:S(2)}, u32[]{:S(2)}) collective-permute-start(bf16[2,2,128,256]{3,2,1,0:T(8,128)(2,1)S(1)} %pack_sides.1), channel_id=1, source_target_pairs={{0,8},{8,16},{16,24},{24,32},{32,40},{40,48},{48,56},{56,64},{64,7... | collective-permute-start | bytes 786440 | tf_op jit(solution)/shard_map/ppermute | solution.py:485

commit v3 on v2

v3 whole, which is shorter than its diff:
```python
import functools

import jax
import jax.numpy as jnp
from jax import lax
from jax.experimental import pallas as pl
from jax.experimental.pallas import tpu as pltpu
from jax.sharding import PartitionSpec as P

GROUPS = 32
SEQ_CAP = 8
CLIPS = 16
NH = 128
LOW = 1000
LOCAL_VMEM = 35
PAST_VMEM = 26
LATE = 7
AHEAD = 3
F32 = jnp.float32
BF16 = jnp.bfloat16
MIB = 2**20
STARTS, ENDS, EDGES, CODES = 0, 4, 8, 16
ANY = pl.BlockSpec(memory_space=pl.ANY)
VM = pl.BlockSpec(memory_space=pltpu.VMEM)
SM = pl.BlockSpec(memory_space=pltpu.SMEM)
HBM = pl.BlockSpec(memory_space=pltpu.HBM)


def stats_kernel(ints, feat, o_ref, table, edge_ref, one_ref, mid_ref, two_ref, x_ref, sums, sems, osems):
    frames, band = x_ref.shape[:2]
    quarter = band // 4
    loads = [
        pltpu.make_async_copy(
            feat.at[i // 4, pl.ds((i % 4) * quarter, quarter)],
            x_ref.at[i // 4, pl.ds((i % 4) * quarter, quarter)],
            sems.at[i],
        )
        for i in range(CLIPS)
    ]
    for c in loads:
        c.start()
    passes = [
        pltpu.make_async_copy(feat.at[f, row], edge_ref.at[side, f], osems.at[2 * f + side])
        for f in range(frames)
        for side, row in enumerate((band - 1, 0))
    ]
    split = band - AHEAD
    for i, (src, dst) in enumerate((
        (feat.at[3], one_ref.at[pl.ds(AHEAD, band)]),
        (feat.at[2, pl.ds(split, AHEAD)], one_ref.at[pl.ds(0, AHEAD)]),
        (feat.at[2, pl.ds(LATE, split - LATE)], mid_ref),
        (feat.at[2, pl.ds(0, LATE)], two_ref),
    )):
        passes.append(pltpu.make_async_copy(src, dst, osems.at[2 * frames + i]))
    for c in passes:
        c.start()

    first = ints[0] * 4
    table[EDGES] = (ints[1] > 0).astype(jnp.int32)
    table[EDGES + 1] = (ints[1] < 7).astype(jnp.int32)
    starts = [jnp.int32(0)] * 4
    ends = [jnp.int32(0)] * 4
    start = jnp.int32(0)
    for i in range(CLIPS):
        end = start + ints[2 + i]
        base = ints[2 + CLIPS + i] * SEQ_CAP
        for own in range(4):
            inside = jnp.logical_and(first + own >= start, first + own < end)
            starts[own] = jnp.where(inside, start - first, starts[own])
            ends[own] = jnp.where(inside, end - first, ends[own])
        for k in range(SEQ_CAP):
            table[CODES + start + k] = base + k
        start = end
        loads[i].wait()
        f = i // 4
        x = x_ref[f, pl.ds((i % 4) * quarter, quarter)].astype(F32)
        x = x.reshape(-1, 8, x.shape[-1])
        one = jnp.sum(x, axis=0)
        two = jnp.sum(x * x, axis=0)
        if i % 4 == 0:
            sums[f] = one
            sums[4 + f] = two
        else:
            sums[f] += one
            sums[4 + f] += two
    for own in range(4):
        table[STARTS + own] = starts[own]
        table[ENDS + own] = ends[own]
    tot = jnp.sum(sums[...], axis=1)
    for d in range(o_ref.shape[0]):
        o_ref[d] = tot
    for c in passes:
        c.wait()


def channel_stats(ints, feat, copies):
    frames, band, width, chans = feat.shape
    return pl.pallas_call(
        stats_kernel,
        in_specs=[SM, ANY],
        out_specs=[VM, SM, ANY, HBM, HBM, HBM],
        out_shape=[
            jax.ShapeDtypeStruct((copies, 2 * frames, chans), F32),
            jax.ShapeDtypeStruct((CODES + 64 + SEQ_CAP,), jnp.int32),
            jax.ShapeDtypeStruct((2, frames, width, chans), BF16),
            jax.ShapeDtypeStruct((band + AHEAD, width, chans), BF16),
            jax.ShapeDtypeStruct((band - AHEAD - LATE, width, chans), BF16),
            jax.ShapeDtypeStruct((LATE, width, chans), BF16),
        ],
        scratch_shapes=[
            pltpu.VMEM(feat.shape, BF16),
            pltpu.VMEM((2 * frames, 8, chans), F32),
            pltpu.SemaphoreType.DMA((CLIPS,)),
            pltpu.SemaphoreType.DMA((2 * frames + 4,)),
        ],
        compiler_params=pltpu.CompilerParams(vmem_limit_bytes=16 * MIB),
        cost_estimate=pl.CostEstimate(flops=LOW, bytes_accessed=LOW, transcendentals=0),
        name="channel_stats",
    )(ints, pltpu.with_memory_space_constraint(feat, pltpu.HBM))


def clip_kernel(ints, table, sums, past_in, edge_in, o_ref, past, edge):
    del past_in, edge_in, past, edge
    shape = (8, sums.shape[0])
    row = lax.broadcasted_iota(jnp.int32, shape, 0)
    col = lax.broadcasted_iota(jnp.int32, shape, 1)
    frame = (col // 8) * 4 + col % 4 - 4 * ints[0]
    start = jnp.zeros(shape, jnp.int32)
    end = jnp.zeros(shape, jnp.int32)
    for f in range(4):
        start = jnp.where(row % 4 == f, table[STARTS + f], start)
        end = jnp.where(row % 4 == f, table[ENDS + f], end)
    inside = jnp.logical_and(frame >= start, frame < end)
    mask = jnp.where(jnp.logical_and(inside, row // 4 == (col // 4) % 2), 1.0, 0.0)
    tot = jnp.dot(mask, sums[...], precision=lax.Precision.HIGHEST, preferred_element_type=F32)
    for d in range(o_ref.shape[0]):
        o_ref[d] = tot


def clip_sums(ints, table, sums, past, edge, copies):
    return pl.pallas_call(
        clip_kernel,
        in_specs=[SM, SM, VM, HBM, ANY],
        out_specs=[VM, HBM, ANY],
        out_shape=[
            jax.ShapeDtypeStruct((copies, 8, sums.shape[1]), F32),
            jax.ShapeDtypeStruct(past.shape, BF16),
            jax.ShapeDtypeStruct(edge.shape, BF16),
        ],
        input_output_aliases={3: 1, 4: 2},
        compiler_params=pltpu.CompilerParams(vmem_limit_bytes=4 * MIB),
        cost_estimate=pl.CostEstimate(flops=LOW, bytes_accessed=LOW, transcendentals=0),
        name="clip_sums",
    )(ints, table, sums, past, edge)


def sides_kernel(near, top, bot, mid, sides, sem):
    del near
    copies = [
        pltpu.make_async_copy(src.at[2 + p], sides.at[2 * k + p], sem.at[2 * k + p])
        for k, src in enumerate((top, bot))
        for p in range(2)
    ]
    copies.append(pltpu.make_async_copy(mid, sides.at[pl.ds(4, mid.shape[0])], sem.at[4]))
    for c in copies:
        c.start()
    for c in copies:
        c.wait()


def pack_sides(near, top, bot, mid):
    return pl.pallas_call(
        sides_kernel,
        in_specs=[ANY] * 3 + [HBM],
        out_specs=ANY,
        out_shape=jax.ShapeDtypeStruct((4 + mid.shape[0],) + mid.shape[1:], BF16),
        scratch_shapes=[pltpu.SemaphoreType.DMA((5,))],
        compiler_params=pltpu.CompilerParams(vmem_limit_bytes=4 * MIB),
        cost_estimate=pl.CostEstimate(flops=LOW, bytes_accessed=LOW, transcendentals=0),
        name="pack_sides",
    )(near, top, bot, mid)


def normed_rows(x, half_scale, half_shift):
    u = x.astype(F32) * half_scale + half_shift
    return u + u * jnp.tanh(u)


def put_rows(slab, row, h):
    width, chans = h.shape
    col = lax.broadcasted_iota(jnp.int32, h.shape, 0)
    left = jnp.where(col == 0, 0.0, pltpu.roll(h, 1, 0))
    right = jnp.where(col == width - 1, 0.0, pltpu.roll(h, width - 1, 0))
    slab[row, :, 0:chans] = left.astype(BF16)
    slab[row, :, chans : 2 * chans] = h.astype(BF16)
    slab[row, :, 2 * chans :] = right.astype(BF16)


PAIRS = 8
UPPER, LOWER = range(0, 4), range(4, 8)
TAP0, TAP1, TAP2, TAP01, TAP012, NONE = 0, 1, 2, 3, 4, 5


def bank_kernel(w, sides, page_in, bank, page):
    del sides, page_in, page

    def step(i, _):
        r = pl.ds(pl.multiple_of(i * 16, 16), 16)
        taps = [[w[a, b, r].astype(F32) for b in range(3)] for a in range(3)]
        first = [x + y for x, y in zip(taps[0], taps[1])]
        taps += [first, [x + y for x, y in zip(first, taps[2])]]
        for n, (top, mid, low) in enumerate(taps):
            half = 0.5 * (top + low)
            mid = 0.5 * mid
            bank[4 * n, r] = top.astype(BF16)
            bank[4 * n + 1, r] = (half + mid).astype(BF16)
            bank[4 * n + 2, r] = (half - mid).astype(BF16)
            bank[4 * n + 3, r] = low.astype(BF16)
        bank[4 * NONE, r] = jnp.zeros(taps[0][0].shape, BF16)
        return 0

    lax.fori_loop(0, w.shape[2] // 16, step, 0)


def weight_bank(weight, sides, page):
    return pl.pallas_call(
        bank_kernel,
        in_specs=[VM, ANY, HBM],
        out_specs=[VM, HBM],
        out_shape=[
            jax.ShapeDtypeStruct((4 * NONE + 1,) + weight.shape[2:], BF16),
            jax.ShapeDtypeStruct(page.shape, BF16),
        ],
        input_output_aliases={2: 1},
        compiler_params=pltpu.CompilerParams(vmem_limit_bytes=16 * MIB),
        cost_estimate=pl.CostEstimate(flops=LOW, bytes_accessed=LOW, transcendentals=0),
        name="weight_bank",
    )(weight, sides, page)


def lift_steps(row, pairs, hs, hb, top_on, bot_on, page, lifted):
    ring = page.shape[0]
    first, last = 2 * pairs[0], 2 * pairs[-1] + 3

    def normed(r):
        h = normed_rows(row(r - 1), hs, hb)
        if r == 0:
            return h * top_on
        return h * bot_on if r == 2 * PAIRS + 1 else h

    def step(rows):
        for r in rows:
            put_rows(page, r % ring, normed(r))
            if r % 2 == 0 or r == first + 1:
                continue
            p = (r - 3) // 2
            d0, d1, d2, d3 = (page[(2 * p + k) % ring] for k in range(4))
            lifted[0, p] = d0 - d2
            lifted[1, p] = d1 + d2
            lifted[2, p] = d2 - d1
            lifted[3, p] = d3 - d1

    cuts = [first + (last + 1 - first) * i // 4 for i in range(5)]
    return [functools.partial(step, range(cuts[i], cuts[i + 1])) for i in range(4)]


def rows_of(raw, top, bot):
    return lambda r: top[...] if r < 0 else bot[...] if r == 2 * PAIRS else raw(r)


def product(bank, taps, k, pairs, total=None):
    for lifted, pick in taps:
        lhs = lifted[k, pairs[0] : pairs[-1] + 1]
        lhs = lhs.reshape(len(pairs) * lhs.shape[1], lhs.shape[2])
        rhs = bank[jnp.where(pick == NONE, 4 * NONE, 4 * pick + k)]
        d = jnp.dot(lhs, rhs, preferred_element_type=F32)
        total = d if total is None else total + d
    return total


def conv_frame(bank, taps, out, base, beside, pairs=range(PAIRS)):
    r = pl.ds(pairs[0], len(pairs))
    shape = (len(pairs),) + out.shape[2:]
    steps = list(beside) + [lambda: None] * 4
    m1 = product(bank, taps, 1, pairs)
    steps[0]()
    m2 = product(bank, taps, 2, pairs)
    steps[1]()
    even, odd = m1 + m2, m1 - m2
    if base is not None:
        even = even + base[0, r].reshape(even.shape)
        odd = odd + base[1, r].reshape(odd.shape)
    out[0, r] = product(bank, taps, 0, pairs, even).reshape(shape)
    steps[2]()
    out[1, r] = product(bank, taps, 3, pairs, odd).reshape(shape)
    steps[3]()


def pick_taps(start, t):
    return [
        jnp.where(start == t, TAP012, TAP2),
        jnp.where(start <= t - 2, TAP1, jnp.where(start == t - 1, TAP01, NONE)),
        jnp.where(start <= t - 2, TAP0, NONE),
    ]


def finish_steps(conv, feat, cbias_ref, obuf, pairs=range(PAIRS)):
    def step(some):
        for p in some:
            for q in range(2):
                r = 2 * p + q
                total = conv[q, p] + feat[r].astype(F32) + cbias_ref[...]
                obuf[r] = total.astype(BF16)

    n = len(pairs) // 4
    return [functools.partial(step, pairs[n * i : n * i + n]) for i in range(4)]


def spread_latent(proj_ref, pbias_ref, projt, pbias):
    latent_ch, wide = proj_ref.shape[0], projt.shape[1]
    z = lax.broadcasted_iota(jnp.int32, (latent_ch, wide), 0)
    lane = lax.broadcasted_iota(jnp.int32, (latent_ch, wide), 1)
    spread = (lane % latent_ch == z).astype(F32)
    projt[...] = lax.dot_general(
        proj_ref[...], spread.astype(BF16), (((0,), (0,)), ((), ())), preferred_element_type=F32
    ).astype(BF16)
    pbias[...] = jnp.dot(
        pbias_ref[...], spread, precision=lax.Precision.HIGHEST, preferred_element_type=F32
    )


def latent_frame(block, projt, pbias, lscr, lat_ref, f):
    rows, width, chans = block.shape
    wide = projt.shape[1]
    per = wide // 16
    both = jnp.dot(
        block.reshape(rows * width, chans), projt[...], preferred_element_type=F32
    ).reshape(rows, width, wide)
    col = lax.broadcasted_iota(jnp.int32, both.shape, 1)
    lane = lax.broadcasted_iota(jnp.int32, both.shape, 2)
    lscr[...] = jnp.where(col % per == lane // 16, both, 0.0)
    for j in range(width // per):
        part = jnp.sum(lscr[:, per * j : per * (j + 1), :], axis=1) + pbias[...]
        lat_ref[j, f] = part.astype(BF16)


def local_kernel(
    table, feat, top, bot, bank, near, gamma_ref, beta_ref, cbias_ref, proj_ref, pbias_ref,
    block_hbm, part, lat_ref, affine_ref,
    page, lift0, lift1, lift2, lift3, conv2, conv3, obuf, lscr, projt, pbias, osems,
):
    tot = jnp.sum(near[...], axis=0)
    chans = tot.shape[1]
    per = chans // GROUPS
    group = (
        lax.broadcasted_iota(jnp.int32, (chans, chans), 0) // per
        == lax.broadcasted_iota(jnp.int32, (chans, chans), 1) // per
    ).astype(F32)
    tot = jnp.dot(tot, group, precision=lax.Precision.HIGHEST, preferred_element_type=F32)
    for f in range(4):
        count = ((table[ENDS + f] - table[STARTS + f]) * (NH * feat.shape[2] * per)).astype(F32)
        mean = tot[f : f + 1] / count
        var = tot[4 + f : 5 + f] / count - mean * mean
        scale = lax.rsqrt(var + 1e-06) * gamma_ref[...]
        affine_ref[f : f + 1] = 0.5 * scale
        affine_ref[4 + f : 5 + f] = 0.5 * (beta_ref[...] - mean * scale)
    spread_latent(proj_ref, pbias_ref, projt, pbias)

    starts = [table[STARTS + f] for f in range(4)]
    top_on = table[EDGES].astype(F32)
    bot_on = table[EDGES + 1].astype(F32)
    lifts = (lift0, lift1, lift2, lift3)
    picks = [pick_taps(starts[t], t) for t in range(4)]

    def lift(f):
        return lift_steps(
            rows_of(lambda r: feat[f, r], top.at[f], bot.at[f]), range(PAIRS),
            affine_ref[f : f + 1], affine_ref[4 + f : 5 + f], top_on, bot_on, page, lifts[f],
        )

    def taps(t):
        return [(lifts[t - k], picks[t][k]) for k in range(min(t, 2) + 1)]

    def finish(f, conv):
        return finish_steps(conv, feat.at[f], cbias_ref, obuf.at[f - 2])

    def send(f):
        return pltpu.make_async_copy(obuf.at[f - 2], block_hbm.at[f], osems.at[f - 2])

    for step in lift(0):
        step()
    conv_frame(bank, taps(0), part.at[0], None, lift(1))
    conv_frame(bank, taps(1), part.at[1], None, lift(2))
    conv_frame(bank, taps(2), conv2, None, lift(3))
    conv_frame(bank, taps(3), conv3, None, finish(2, conv2))
    send(2).start()
    for step in finish(3, conv3):
        step()
    send(3).start()
    latent_frame(obuf[0], projt, pbias, lscr, lat_ref, 0)
    latent_frame(obuf[1], projt, pbias, lscr, lat_ref, 1)
    send(2).wait()
    send(3).wait()


def local_part(table, feat, top, bot, bank, near, gamma, beta, cbias, proj, pbias):
    shape = feat.shape
    return pl.pallas_call(
        local_kernel,
        in_specs=[SM] + [VM] * 10,
        out_specs=[ANY, VM, VM, VM],
        out_shape=[
            jax.ShapeDtypeStruct(shape, BF16),
            jax.ShapeDtypeStruct((2, 2, PAIRS) + shape[2:], F32),
            jax.ShapeDtypeStruct((16, 2, 16, 128), BF16),
            jax.ShapeDtypeStruct((8, 256), F32),
        ],
        scratch_shapes=[
            pltpu.VMEM((8, 128, 768), BF16),
            pltpu.VMEM((4, PAIRS, 128, 768), BF16),
            pltpu.VMEM((4, PAIRS, 128, 768), BF16),
            pltpu.VMEM((4, PAIRS, 128, 768), BF16),
            pltpu.VMEM((4, PAIRS, 128, 768), BF16),
            pltpu.VMEM((2, PAIRS, 128, 256), F32),
            pltpu.VMEM((2, PAIRS, 128, 256), F32),
            pltpu.VMEM((2, 16, 128, 256), BF16),
            pltpu.VMEM((16, 128, 128), F32),
            pltpu.VMEM((256, 128), BF16),
            pltpu.VMEM((1, 128), F32),
            pltpu.SemaphoreType.DMA((2,)),
        ],
        compiler_params=pltpu.CompilerParams(vmem_limit_bytes=LOCAL_VMEM * MIB),
        cost_estimate=pl.CostEstimate(flops=LOW, bytes_accessed=LOW, transcendentals=0),
        name="local_conv",
    )(table, feat, top, bot, bank, near, gamma, beta, cbias, proj, pbias)


def past_affine(table, affine_ref, p):
    on = table[STARTS] < -p
    return jnp.where(on, affine_ref[0:1], 0.0), jnp.where(on, affine_ref[4:5], 0.0)


def one_kernel(
    table, past, sides, feat, bank, part, affine_ref, cbias_ref, proj_ref, pbias_ref, block_in,
    block_hbm, half0, lat_ref,
    page, lift1, lift2, conv1, obuf, lscr, projt, pbias, sem,
):
    del block_in
    spread_latent(proj_ref, pbias_ref, projt, pbias)
    pick0, pick1 = pick_taps(table[STARTS], 0), pick_taps(table[STARTS + 1], 1)
    on = (table[EDGES].astype(F32), table[EDGES + 1].astype(F32))
    hs, hb = past_affine(table, affine_ref, 0)
    one = rows_of(lambda r: past[AHEAD + r], sides.at[1], sides.at[3])
    for step in lift_steps(one, range(PAIRS), hs, hb, *on, page, lift1):
        step()
    hs, hb = past_affine(table, affine_ref, 1)
    low = rows_of(lambda r: two_row(r, None, sides, past), None, sides.at[2])
    steps = lift_steps(low, LOWER, hs, hb, *on, page, lift2)
    conv_frame(bank, [(lift1, pick1[2])], conv1, part.at[1], steps)
    conv_frame(
        bank, [(lift1, pick0[1])], half0, part.at[0],
        finish_steps(conv1, feat.at[0], cbias_ref, obuf),
    )
    out = pltpu.make_async_copy(obuf, block_hbm.at[1], sem)
    out.start()
    conv_frame(bank, [(lift2, pick0[2])], half0, half0, [], LOWER)
    latent_frame(obuf[...], projt, pbias, lscr, lat_ref, 0)
    out.wait()


def two_row(r, late, sides, past):
    if r < LATE:
        return late[r]
    return sides[4 + r - LATE] if r < 2 * PAIRS - AHEAD else past[r - 2 * PAIRS + AHEAD]


def two_kernel(
    table, late, past, sides, feat, bank, half0, affine_ref, cbias_ref, proj_ref, pbias_ref,
    early_ref, one_ref, block_in,
    block_hbm, lat_ref,
    page, lifted, conv0, obuf, lscr, projt, pbias, sem,
):
    del block_in
    spread_latent(proj_ref, pbias_ref, projt, pbias)
    pick0 = pick_taps(table[STARTS], 0)
    on = (table[EDGES].astype(F32), table[EDGES + 1].astype(F32))
    hs, hb = past_affine(table, affine_ref, 1)
    rows = rows_of(lambda r: two_row(r, late, sides, past), sides.at[0], None)
    for step in lift_steps(rows, UPPER, hs, hb, *on, page, lifted):
        step()
    conv_frame(
        bank, [(lifted, pick0[2])], conv0, half0,
        finish_steps(half0, feat.at[0], cbias_ref, obuf, LOWER), UPPER,
    )
    for step in finish_steps(conv0, feat.at[0], cbias_ref, obuf, UPPER):
        step()
    out = pltpu.make_async_copy(obuf, block_hbm.at[0], sem)
    out.start()
    latent_frame(obuf[...], projt, pbias, lscr, lat_ref, 0)
    lat_ref[:, 1:2] = one_ref[...]
    lat_ref[:, 2:4] = early_ref[...]
    out.wait()


def past_scratch(shape, lifts):
    return [pltpu.VMEM((8, 128, 768), BF16)] + lifts * [
        pltpu.VMEM((4, PAIRS, 128, 768), BF16)
    ] + [
        pltpu.VMEM((2, PAIRS) + shape[2:], F32),
        pltpu.VMEM(shape[1:], BF16),
        pltpu.VMEM((16, 128, 128), F32),
        pltpu.VMEM((256, 128), BF16),
        pltpu.VMEM((1, 128), F32),
        pltpu.SemaphoreType.DMA,
    ]


def one_part(table, past, sides, feat, bank, part, affine, cbias, proj, pbias, block):
    shape = feat.shape
    return pl.pallas_call(
        one_kernel,
        grid=(1,),
        in_specs=[SM, VM, VM, pl.BlockSpec((1,) + shape[1:], lambda i: (1, 0, 0, 0))]
        + [VM] * 6
        + [ANY],
        out_specs=[ANY, VM, VM],
        out_shape=[
            jax.ShapeDtypeStruct(shape, BF16),
            jax.ShapeDtypeStruct(part.shape[1:], F32),
            jax.ShapeDtypeStruct((16, 1, 16, 128), BF16),
        ],
        input_output_aliases={10: 0},
        scratch_shapes=past_scratch(shape, 2),
        compiler_params=pltpu.CompilerParams(vmem_limit_bytes=PAST_VMEM * MIB),
        cost_estimate=pl.CostEstimate(flops=LOW, bytes_accessed=LOW, transcendentals=0),
        name="past_one",
    )(table, past, sides, feat, bank, part, affine, cbias, proj, pbias, block)


def two_part(
    table, late, past, sides, feat, bank, half0, affine, cbias, proj, pbias, early, one, block
):
    shape = feat.shape
    return pl.pallas_call(
        two_kernel,
        grid=(1,),
        in_specs=[SM, VM, VM, VM, pl.BlockSpec((1,) + shape[1:], lambda i: (0, 0, 0, 0))]
        + [VM] * 8
        + [ANY],
        out_specs=[ANY, VM],
        out_shape=[
            jax.ShapeDtypeStruct(shape, BF16),
            jax.ShapeDtypeStruct((16, 4, 16, 128), BF16),
        ],
        input_output_aliases={13: 0},
        scratch_shapes=past_scratch(shape, 1),
        compiler_params=pltpu.CompilerParams(vmem_limit_bytes=PAST_VMEM * MIB),
        cost_estimate=pl.CostEstimate(flops=LOW, bytes_accessed=LOW, transcendentals=0),
        name="past_two",
    )(table, late, past, sides, feat, bank, half0, affine, cbias, proj, pbias, early, one, block)


def place_kernel(table, x_ref, o_ref):
    o_ref[...] = jnp.zeros_like(o_ref)

    def put(t, _):
        o_ref[table[CODES + t]] = x_ref[t]
        return 0

    lax.fori_loop(0, x_ref.shape[0], put, 0, unroll=8)


def place(table, shares):
    return pl.pallas_call(
        place_kernel,
        in_specs=[SM, VM],
        out_specs=VM,
        out_shape=jax.ShapeDtypeStruct((128, 16, 128), BF16),
        compiler_params=pltpu.CompilerParams(vmem_limit_bytes=4 * MIB),
        name="place_frames",
    )(table, shares)


def merge_kernel(x_ref, o_ref):
    for j in range(x_ref.shape[0]):
        o_ref[:, :, 128 * j : 128 * (j + 1)] = x_ref[j]


def merge(seq):
    return pl.pallas_call(
        merge_kernel,
        in_specs=[VM],
        out_specs=VM,
        out_shape=jax.ShapeDtypeStruct((8, 16, 2048), BF16),
        compiler_params=pltpu.CompilerParams(vmem_limit_bytes=4 * MIB),
        name="merge_columns",
    )(seq)


def shift(x, axis, by):
    n = lax.axis_size(axis)
    return lax.ppermute(x, axis, [(i, i + by) for i in range(n) if 0 <= i + by < n])


def on_device(feat, gamma, beta, conv_weight, conv_bias, proj, proj_bias, clip_len, owner):
    frames, band = feat.shape[:2]
    n_time = lax.axis_size("tm")

    place_of = jnp.stack([lax.axis_index("tm"), lax.axis_index("rows")]).astype(jnp.int32)
    ints = jnp.concatenate([place_of, clip_len, owner])
    sums, table, edge, one, mid, two = channel_stats(ints, feat, n_time)
    sums = lax.all_to_all(sums, "tm", split_axis=0, concat_axis=0, tiled=True)
    sums, one, edge = clip_sums(
        ints, table, sums.reshape(-1, sums.shape[-1]), one, edge, lax.axis_size("rows")
    )
    one = shift(one, "tm", 1)
    top, bot = shift(edge[0], "rows", 1), shift(edge[1], "rows", -1)
    near = lax.all_to_all(sums, "rows", split_axis=0, concat_axis=0, tiled=True)
    sides = pack_sides(near, top, bot, mid)
    bank, two = weight_bank(conv_weight, sides, two)
    sides = shift(sides, "tm", 1)
    two = shift(two, "tm", 1)

    cbias, pbias = conv_bias[None, :], proj_bias[None, :]
    block, part, early, affine = local_part(
        table, feat, top, bot, bank, near, gamma[None, :], beta[None, :], cbias, proj.T,
        pbias,
    )
    block, part, lat = one_part(
        table, one, sides, feat, bank, part, affine, cbias, proj.T, pbias, block
    )
    block, lat = two_part(
        table, two, one, sides, feat, bank, part, affine, cbias, proj.T, pbias, early, lat, block
    )
    shares = lax.all_to_all(lat, "tm", split_axis=0, concat_axis=0, tiled=True)
    placed = place(table, shares.reshape(n_time * frames, band, 128))
    seq = lax.all_to_all(
        placed.reshape(n_time, SEQ_CAP, band, 128), "tm", split_axis=0, concat_axis=0, tiled=True
    )
    return block, merge(seq)


def solution(mesh):
    in_specs = (P("tm", "rows", None, None), P(), P(), P(), P(), P(), P(), P(), P())
    out_specs = (P("tm", "rows", None, None), P("tm", "rows", None))
    return jax.shard_map(
        on_device, mesh=mesh, in_specs=in_specs, out_specs=out_specs, check_vma=False
    )
```

time: 118 us -> 108 us (0.915)
  Pallas kernels: 47.8 us -> 36.9 us
  starting transfers between devices: 9.64 us -> 13.2 us
  blocking collectives: 57.8 us -> 54.7 us
  waiting for transfers between devices: 0.01 us -> 1.61 us
    pallas_call x1, Pallas kernels: 36.9 us -> 18.1 us  [local_part(): pl.pallas_call(local_kernel, in_specs=[SM] + [VM] * 10, out_specs=[ANY, V...]
    pallas_call x3 -> x5, Pallas kernels: 4.53 us -> 12.5 us  [the longest x1 6.6 us: one_part(): pl.pallas_call(one_kernel, grid=(1,), in_specs=[SM, VM, VM, pl.BlockSpec(...]
    ppermute x4 -> x5, starting transfers between devices: 9.64 us -> 13.2 us  [shift(): lax.ppermute(x, axis, [(i, i + by) for i in range(n) if 0 <= i + by < n])]
    all_to_all x1, blocking collectives: 18.4 us -> 15.2 us  [on_device(): shares = lax.all_to_all(lat, 'tm', split_axis=0, concat_axis=0, tiled=True)]
    ppermute x4 -> x5, waiting for transfers between devices: 0.01 us -> 1.61 us  [shift(): lax.ppermute(x, axis, [(i, i + by) for i in range(n) if 0 <= i + by < n])]
  transfers between devices with their start and end apart: 4 -> 5, of which waited for: 0 -> 2; matrix products, arithmetic and copies ran while one was open for 0% -> 0% of each run, Pallas kernels for 32% -> 25%
where the time goes in v3:
time: 108 us
  blocking collectives  54.7 us (51%)
  Pallas kernels  36.9 us (34%)
  starting transfers between devices  13.2 us (12%)
  waiting for transfers between devices  1.61 us (1%)
    pallas_call x1, Pallas kernels, local_part(): pl.pallas_call(local_kernel, in_specs=[SM] + [VM] * 10, out_specs=[ANY, V...  18.1 us
    all_to_all x1, blocking collectives, on_device(): sums = lax.all_to_all(sums, 'tm', split_axis=0, concat_axis=0, tiled=True)  15.8 us
    all_to_all x1, blocking collectives, on_device(): shares = lax.all_to_all(lat, 'tm', split_axis=0, concat_axis=0, tiled=True)  15.2 us
    all_to_all x1, blocking collectives, on_device(): lax.all_to_all(placed.reshape(n_time, SEQ_CAP, band, 128), 'tm', split_ax...  13.6 us
    ppermute x5, starting transfers between devices, shift(): lax.ppermute(x, axis, [(i, i + by) for i in range(n) if 0 <= i + by < n])  13.2 us
    all_to_all x1, blocking collectives, on_device(): near = lax.all_to_all(sums, 'rows', split_axis=0, concat_axis=0, tiled=True)  10.1 us
    pallas_call x1, Pallas kernels, one_part(): pl.pallas_call(one_kernel, grid=(1,), in_specs=[SM, VM, VM, pl.BlockSpec(...  6.6 us
    pallas_call x1, Pallas kernels, channel_stats(): pl.pallas_call(stats_kernel, in_specs=[SM, ANY], out_specs=[VM, SM, ANY,...  4.56 us
  transfers between devices with their start and end apart: 5, of which 2 were waited for; matrix products, arithmetic and copies ran while one was open for 0% of the time, Pallas kernels for 25%

profile of v3, /device:TPU:0, one launch (start us, length us, event | category | flops | bytes accessed | tf_op | source)
XLA Modules:
  0.0 108.0 jit_solution(3517471638786491481)
XLA Ops:
  0.6 0.8 pad_add_fusion.ints
  1.4 0.0 copy-start.1
  1.4 4.6 %channel_stats.1 = (f32[16,8,256]{2,1,0:T(8,128)S(1)}, s32[88]{0:T(128)S(1)}, bf16[2,4,128,256]{3,2,1,0:T(8,128)(2,1)S(1)}, bf16[19,128,256]{2,1,0:T(8,128)(2,1)...) custom-call(s32[34]{0:T(128)S(1)} %pad_add_fusion.ints, bf16[4,16,128,256]{3,2,1,0:T(8,128)(2,1)} %feat.7), custom_call_target="tpu_custom_call" | custom-call | flops 1000 | bytes 1000 | tf_op jit(solution)/shard_map/channel_stats/pallas_call | solution.py:98
  6.0 15.8 %all_to_all.20 = f32[16,8,256]{2,1,0:T(8,128)S(1)} all-to-all(f32[16,8,256]{2,1,0:T(8,128)S(1)} %get-tuple-element.23), channel_id=1, replica_groups=mesh['tm'=16,'rows'=8] {'tm'}, dimensions={0} | all-to-all | bytes 262144 | tf_op jit(solution)/shard_map/all_to_all | solution.py:612
  21.7 0.7 clip_sums.1
  22.4 0.0 copy-start
  22.5 0.0 copy-start.2
  22.5 0.0 copy-start.3
  22.5 0.0 copy-start.4
  22.5 0.0 copy-start.5
  22.5 0.0 copy-start.6
  22.5 2.7 %collective-permute-start.3 = (bf16[19,128,256]{2,1,0:T(8,128)(2,1)S(1)}, bf16[19,128,256]{2,1,0:T(8,128)(2,1)S(1)}, u32[]{:S(2)}, u32[]{:S(2)}) collective-permute-start(bf16[19,128,256]{2,1,0:T(8,128)(2,1)S(1)} %get-tuple-element.31), channel_id=1, source_target_pairs={{0,8},{8,16},{16,24},{24,32},{32,40},{40,48},{48,56},{56,64},{64,7... | collective-permute-start | bytes 3735560 | tf_op jit(solution)/shard_map/ppermute | solution.py:602
  25.3 1.3 %collective-permute-start.1 = (bf16[4,128,256]{2,1,0:T(8,128)(2,1)S(1)}, bf16[4,128,256]{2,1,0:T(8,128)(2,1)S(1)}, u32[]{:S(2)}, u32[]{:S(2)}) collective-permute-start(bf16[4,128,256]{2,1,0:T(8,128)(2,1)S(1)} %get-tuple-element.42), channel_id=1, source_target_pairs={{1,0},{2,1},{3,2},{4,3},{5,4},{6,5},{7,6},{9,8},{10,9},{11,10},{12... | collective-permute-start | bytes 786440 | tf_op jit(solution)/shard_map/ppermute | solution.py:602
  26.6 3.0 %collective-permute-start = (bf16[4,128,256]{2,1,0:T(8,128)(2,1)S(1)}, bf16[4,128,256]{2,1,0:T(8,128)(2,1)S(1)}, u32[]{:S(2)}, u32[]{:S(2)}) collective-permute-start(bf16[4,128,256]{2,1,0:T(8,128)(2,1)S(1)} %get-tuple-element.43), channel_id=1, source_target_pairs={{0,1},{1,2},{2,3},{3,4},{4,5},{5,6},{6,7},{8,9},{9,10},{10,11},{11... | collective-permute-start | bytes 786440 | tf_op jit(solution)/shard_map/ppermute | solution.py:602
  29.7 10.1 %all_to_all.21.near = f32[8,8,256]{2,1,0:T(8,128)S(1)} all-to-all(f32[8,8,256]{2,1,0:T(8,128)S(1)} %get-tuple-element.26), channel_id=1, replica_groups=mesh['tm'=16,'rows'=8] {'rows'}, dimensions={0} | all-to-all | bytes 131072 | tf_op jit(solution)/shard_map/all_to_all | solution.py:618
  39.8 0.0 collective-permute-done.1.bot
  39.8 0.0 collective-permute-done.top
  39.8 0.6 pack_sides.1.sides
  40.4 2.9 %collective-permute-start.4 = (bf16[10,128,256]{2,1,0:T(8,128)(2,1)S(1)}, bf16[10,128,256]{2,1,0:T(8,128)(2,1)S(1)}, u32[]{:S(2)}, u32[]{:S(2)}) collective-permute-start(bf16[10,128,256]{2,1,0:T(8,128)(2,1)S(1)} %pack_sides.1.sides), channel_id=1, source_target_pairs={{0,8},{8,16},{16,24},{24,32},{32,40},{40,48},{48,56},{56,64},{64,7... | collective-permute-start | bytes 1966088 | tf_op jit(solution)/shard_map/ppermute | solution.py:602
  43.2 0.0 copy-done.1
  43.3 1.4 %weight_bank.1 = (bf16[21,768,256]{2,1,0:T(8,128)(2,1)S(1)}, bf16[7,128,256]{2,1,0:T(8,128)(2,1)S(1)}) custom-call(bf16[3,3,768,256]{3,2,1,0:T(8,128)(2,1)S(1)} %copy-done.1, bf16[10,128,256]{2,1,0:T(8,128)(2,1)S(1)} %pack_sides.1.sides, bf16[7,128,256]{2,1,0:T(8,128)(2,1)S(1)} %get-tuple-element.29.page_in), custom_call_target="tpu_custom_call", output_to_operand_aliasing={{1}: (2, {})} | custom-call | flops 1000 | bytes 1000 | tf_op jit(solution)/shard_map/weight_bank/pallas_call | solution.py:226
  44.6 3.3 %collective-permute-start.2 = (bf16[7,128,256]{2,1,0:T(8,128)(2,1)S(1)}, bf16[7,128,256]{2,1,0:T(8,128)(2,1)S(1)}, u32[]{:S(2)}, u32[]{:S(2)}) collective-permute-start(bf16[7,128,256]{2,1,0:T(8,128)(2,1)S(1)} %get-tuple-element.30), channel_id=1, source_target_pairs={{0,8},{8,16},{16,24},{24,32},{32,40},{40,48},{48,56},{56,64},{64,7... | collective-permute-start | bytes 1376264 | tf_op jit(solution)/shard_map/ppermute | solution.py:602
  47.9 0.0 copy-done
  47.9 0.0 copy-done.2
  47.9 0.0 copy-done.3
  47.9 0.0 copy-done.4
  48.0 0.0 copy-done.5
  48.0 0.0 copy-done.6
  48.0 18.1 %local_conv.1 = (bf16[4,16,128,256]{3,2,1,0:T(8,128)(2,1)}, f32[2,2,8,128,256]{4,3,2,1,0:T(8,128)S(1)}, bf16[16,2,16,128]{3,2,1,0:T(8,128)(2,1)S(1)}, f32[8,256]{1,0:T(8,128)S(1)}) custom-call(s32[88]{0:T(128)S(1)} %get-tuple-element.22.table, bf16[4,16,128,256]{3,2,1,0:T(8,128)(2,1)S(1)} %copy-done, bf16[4,128,256]{2,1,0:T(8,128)(2,1)S(1)} %collective-permute-done.top, ...), custom_call_target="tpu_custom_call" | custom-call | flops 1000 | bytes 1000 | tf_op jit(solution)/shard_map/local_conv/pallas_call | solution.py:408
  66.1 0.9 collective-permute-done.4.sides
  67.0 0.0 collective-permute-done.3.past
  67.0 6.6 %past_one.1 = (bf16[4,16,128,256]{3,2,1,0:T(8,128)(2,1)}, f32[2,8,128,256]{3,2,1,0:T(8,128)S(1)}, bf16[16,1,16,128]{3,2,1,0:T(8,128)(2,1)S(1)}) custom-call(s32[88]{0:T(128)S(1)} %get-tuple-element.22.table, bf16[19,128,256]{2,1,0:T(8,128)(2,1)S(1)} %collective-permute-done.3.past, ...), custom_call_target="tpu_custom_call", output_to_operand_aliasing={{0}: (10, {})} | custom-call | flops 1000 | bytes 1000 | tf_op jit(solution)/shard_map/past_one/pallas_call | solution.py:520
  73.6 0.7 collective-permute-done.2.late
  74.3 3.3 %past_two.1 = (bf16[4,16,128,256]{3,2,1,0:T(8,128)(2,1)}, bf16[16,4,16,128]{3,2,1,0:T(8,128)(2,1)S(1)}) custom-call(s32[88]{0:T(128)S(1)} %get-tuple-element.22.table, bf16[7,128,256]{2,1,0:T(8,128)(2,1)S(1)} %collective-permute-done.2.late, bf16[19,128,256]{2,1,0:T(8,128)(2,1)S(1)} %collective-permute-done.3.past, ...), custom_call_target="tpu_custom_call", output_to_operand_aliasing={{0}: (13, {})} | custom-call | flops 1000 | bytes 1000 | tf_op jit(solution)/shard_map/past_two/pallas_call | solution.py:544
  77.6 15.2 %all_to_all.22 = bf16[16,4,16,128]{3,2,1,0:T(8,128)(2,1)S(1)} all-to-all(bf16[16,4,16,128]{3,2,1,0:T(8,128)(2,1)S(1)} %get-tuple-element.41), channel_id=1, replica_groups=mesh['tm'=16,'rows'=8] {'tm'}, dimensions={0} | all-to-all | bytes 524288 | tf_op jit(solution)/shard_map/all_to_all | solution.py:635
  92.8 0.7 place_frames.1
  93.5 13.6 %all_to_all.23.x_ref = bf16[16,8,16,128]{3,2,1,0:T(8,128)(2,1)S(1)} all-to-all(bf16[16,8,16,128]{3,2,1,0:T(8,128)(2,1)S(1)} %bitcast.14), channel_id=1, replica_groups=mesh['tm'=16,'rows'=8] {'tm'}, dimensions={0} | all-to-all | bytes 1048576 | tf_op jit(solution)/shard_map/all_to_all | solution.py:637
  107.1 0.9 merge_columns.1
  (1 shorter events, 0.0 us)
Async XLA Ops:
  1.4 41.9 %copy-start.1 = (bf16[3,3,768,256]{3,2,1,0:T(8,128)(2,1)S(1)}, bf16[3,3,768,256]{3,2,1,0:T(8,128)(2,1)}, u32[]{:S(2)}) copy-start(bf16[3,3,768,256]{3,2,1,0:T(8,128)(2,1)} %w.1) | copy-start | bytes 10616836
  22.4 25.5 %copy-start = (bf16[4,16,128,256]{3,2,1,0:T(8,128)(2,1)S(1)}, bf16[4,16,128,256]{3,2,1,0:T(8,128)(2,1)}, u32[]{:S(2)}) copy-start(bf16[4,16,128,256]{3,2,1,0:T(8,128)(2,1)} %feat.7) | copy-start | bytes 12582916
  22.5 25.5 %copy-start.2 = (bf16[256,16]{0,1:T(8,128)(2,1)S(1)}, bf16[256,16]{0,1:T(8,128)(2,1)}, u32[]{:S(2)}) copy-start(bf16[256,16]{0,1:T(8,128)(2,1)} %param.14) | copy-start | bytes 24580
  22.5 25.5 %copy-start.3 = (f32[256]{0:T(256)S(1)}, f32[256]{0:T(256)}, u32[]{:S(2)}) copy-start(f32[256]{0:T(256)} %param.13) | copy-start | bytes 3076
  22.5 25.5 %copy-start.4 = (f32[16]{0:T(128)S(1)}, f32[16]{0:T(128)}, u32[]{:S(2)}) copy-start(f32[16]{0:T(128)} %param.15) | copy-start | bytes 196
  22.5 25.5 %copy-start.5 = (f32[256]{0:T(256)S(1)}, f32[256]{0:T(256)}, u32[]{:S(2)}) copy-start(f32[256]{0:T(256)} %param.10) | copy-start | bytes 3076
  22.5 25.5 %copy-start.6 = (f32[256]{0:T(256)S(1)}, f32[256]{0:T(256)}, u32[]{:S(2)}) copy-start(f32[256]{0:T(256)} %param.11) | copy-start | bytes 3076
  22.5 44.5 %collective-permute-start.3 = (bf16[19,128,256]{2,1,0:T(8,128)(2,1)S(1)}, bf16[19,128,256]{2,1,0:T(8,128)(2,1)S(1)}, u32[]{:S(2)}, u32[]{:S(2)}) collective-permute-start(bf16[19,128,256]{2,1,0:T(8,128)(2,1)S(1)} %get-tuple-element.31), channel_id=1, source_target_pairs={{0,8},{8,16},{16,24},{24,32},{32,40},{40,48},{48,56},{56,64},{64,7... | collective-permute-start | bytes 3735560 | tf_op jit(solution)/shard_map/ppermute | solution.py:602
  25.3 14.5 %collective-permute-start.1 = (bf16[4,128,256]{2,1,0:T(8,128)(2,1)S(1)}, bf16[4,128,256]{2,1,0:T(8,128)(2,1)S(1)}, u32[]{:S(2)}, u32[]{:S(2)}) collective-permute-start(bf16[4,128,256]{2,1,0:T(8,128)(2,1)S(1)} %get-tuple-element.42), channel_id=1, source_target_pairs={{1,0},{2,1},{3,2},{4,3},{5,4},{6,5},{7,6},{9,8},{10,9},{11,10},{12... | collective-permute-start | bytes 786440 | tf_op jit(solution)/shard_map/ppermute | solution.py:602
  26.6 13.2 %collective-permute-start = (bf16[4,128,256]{2,1,0:T(8,128)(2,1)S(1)}, bf16[4,128,256]{2,1,0:T(8,128)(2,1)S(1)}, u32[]{:S(2)}, u32[]{:S(2)}) collective-permute-start(bf16[4,128,256]{2,1,0:T(8,128)(2,1)S(1)} %get-tuple-element.43), channel_id=1, source_target_pairs={{0,1},{1,2},{2,3},{3,4},{4,5},{5,6},{6,7},{8,9},{9,10},{10,11},{11... | collective-permute-start | bytes 786440 | tf_op jit(solution)/shard_map/ppermute | solution.py:602
  40.4 26.7 %collective-permute-start.4 = (bf16[10,128,256]{2,1,0:T(8,128)(2,1)S(1)}, bf16[10,128,256]{2,1,0:T(8,128)(2,1)S(1)}, u32[]{:S(2)}, u32[]{:S(2)}) collective-permute-start(bf16[10,128,256]{2,1,0:T(8,128)(2,1)S(1)} %pack_sides.1.sides), channel_id=1, source_target_pairs={{0,8},{8,16},{16,24},{24,32},{32,40},{40,48},{48,56},{56,64},{64,7... | collective-permute-start | bytes 1966088 | tf_op jit(solution)/shard_map/ppermute | solution.py:602
  44.6 29.7 %collective-permute-start.2 = (bf16[7,128,256]{2,1,0:T(8,128)(2,1)S(1)}, bf16[7,128,256]{2,1,0:T(8,128)(2,1)S(1)}, u32[]{:S(2)}, u32[]{:S(2)}) collective-permute-start(bf16[7,128,256]{2,1,0:T(8,128)(2,1)S(1)} %get-tuple-element.30), channel_id=1, source_target_pairs={{0,8},{8,16},{16,24},{24,32},{32,40},{40,48},{48,56},{56,64},{64,7... | collective-permute-start | bytes 1376264 | tf_op jit(solution)/shard_map/ppermute | solution.py:602

commit v4 on v3

--- a/solution.py
+++ b/solution.py
@@ -19,51 +19,67 @@
 F32 = jnp.float32
 BF16 = jnp.bfloat16
 MIB = 2**20
-STARTS, ENDS, EDGES, CODES = 0, 4, 8, 16
+STARTS, ENDS, EDGES, FIRST, CODES = 0, 4, 8, 10, 16
 ANY = pl.BlockSpec(memory_space=pl.ANY)
 VM = pl.BlockSpec(memory_space=pltpu.VMEM)
 SM = pl.BlockSpec(memory_space=pltpu.SMEM)
 HBM = pl.BlockSpec(memory_space=pltpu.HBM)
 
 
-def stats_kernel(ints, feat, o_ref, table, edge_ref, one_ref, mid_ref, two_ref, x_ref, sums, sems, osems):
+def stats_kernel(
+    clip_len_hbm, owner_hbm, feat, o_ref, table, down_ref, up_ref, one_ref, mid_ref, two_ref, x_ref, sums,
+    clip_len, owner, sems, osems, isems,
+):
     frames, band = x_ref.shape[:2]
     quarter = band // 4
+    split = band - AHEAD
+    ints = [
+        pltpu.make_async_copy(clip_len_hbm, clip_len, isems.at[0]),
+        pltpu.make_async_copy(owner_hbm, owner, isems.at[1]),
+    ]
+    for c in ints:
+        c.start()
+    order = [(f, q) for f in (2, 3, 0, 1) for q in range(4)]
     loads = [
         pltpu.make_async_copy(
-            feat.at[i // 4, pl.ds((i % 4) * quarter, quarter)],
-            x_ref.at[i // 4, pl.ds((i % 4) * quarter, quarter)],
+            feat.at[f, pl.ds(q * quarter, quarter)],
+            x_ref.at[f, pl.ds(q * quarter, quarter)],
             sems.at[i],
         )
-        for i in range(CLIPS)
+        for i, (f, q) in enumerate(order)
     ]
     for c in loads:
         c.start()
-    passes = [
-        pltpu.make_async_copy(feat.at[f, row], edge_ref.at[side, f], osems.at[2 * f + side])
-        for f in range(frames)
-        for side, row in enumerate((band - 1, 0))
-    ]
-    split = band - AHEAD
-    for i, (src, dst) in enumerate((
-        (feat.at[3], one_ref.at[pl.ds(AHEAD, band)]),
-        (feat.at[2, pl.ds(split, AHEAD)], one_ref.at[pl.ds(0, AHEAD)]),
-        (feat.at[2, pl.ds(LATE, split - LATE)], mid_ref),
-        (feat.at[2, pl.ds(0, LATE)], two_ref),
-    )):
-        passes.append(pltpu.make_async_copy(src, dst, osems.at[2 * frames + i]))
-    for c in passes:
+    onward = {
+        2: (
+            (x_ref.at[2, pl.ds(split, AHEAD)], one_ref.at[pl.ds(0, AHEAD)]),
+            (x_ref.at[2, pl.ds(LATE, split - LATE)], mid_ref),
+            (x_ref.at[2, pl.ds(0, LATE)], two_ref),
+        ),
+        3: ((x_ref.at[3], one_ref.at[pl.ds(AHEAD, band)]),),
+        0: (),
+        1: (),
+    }
+    passes = []
+
+    def send_on(src, dst):
+        c = pltpu.make_async_copy(src, dst, osems.at[len(passes)])
         c.start()
-
-    first = ints[0] * 4
-    table[EDGES] = (ints[1] > 0).astype(jnp.int32)
-    table[EDGES + 1] = (ints[1] < 7).astype(jnp.int32)
+        passes.append(c)
+
+    first = lax.axis_index("tm") * 4
+    row = lax.axis_index("rows")
+    table[EDGES] = (row > 0).astype(jnp.int32)
+    table[EDGES + 1] = (row < lax.axis_size("rows") - 1).astype(jnp.int32)
+    table[FIRST] = first
     starts = [jnp.int32(0)] * 4
     ends = [jnp.int32(0)] * 4
     start = jnp.int32(0)
-    for i in range(CLIPS):
-        end = start + ints[2 + i]
-        base = ints[2 + CLIPS + i] * SEQ_CAP
+    for c in ints:
+        c.wait()
+    for i, (f, q) in enumerate(order):
+        end = start + clip_len[i]
+        base = owner[i] * SEQ_CAP
         for own in range(4):
             inside = jnp.logical_and(first + own >= start, first + own < end)
             starts[own] = jnp.where(inside, start - first, starts[own])
@@ -72,12 +88,16 @@
             table[CODES + start + k] = base + k
         start = end
         loads[i].wait()
-        f = i // 4
-        x = x_ref[f, pl.ds((i % 4) * quarter, quarter)].astype(F32)
+        if q == 3:
+            down_ref[f] = x_ref[f, band - 1]
+            up_ref[f] = x_ref[f, 0]
+            for src, dst in onward[f]:
+                send_on(src, dst)
+        x = x_ref[f, pl.ds(q * quarter, quarter)].astype(F32)
         x = x.reshape(-1, 8, x.shape[-1])
         one = jnp.sum(x, axis=0)
         two = jnp.sum(x * x, axis=0)
-        if i % 4 == 0:
+        if q == 0:
             sums[f] = one
             sums[4 + f] = two
         else:
@@ -93,16 +113,17 @@
         c.wait()
 
 
-def channel_stats(ints, feat, copies):
+def channel_stats(clip_len, owner, feat, copies):
     frames, band, width, chans = feat.shape
     return pl.pallas_call(
         stats_kernel,
-        in_specs=[SM, ANY],
-        out_specs=[VM, SM, ANY, HBM, HBM, HBM],
+        in_specs=[HBM, HBM, HBM],
+        out_specs=[VM, SM, VM, VM, HBM, HBM, HBM],
         out_shape=[
             jax.ShapeDtypeStruct((copies, 2 * frames, chans), F32),
             jax.ShapeDtypeStruct((CODES + 64 + SEQ_CAP,), jnp.int32),
-            jax.ShapeDtypeStruct((2, frames, width, chans), BF16),
+            jax.ShapeDtypeStruct((frames, width, chans), BF16),
+            jax.ShapeDtypeStruct((frames, width, chans), BF16),
             jax.ShapeDtypeStruct((band + AHEAD, width, chans), BF16),
             jax.ShapeDtypeStruct((band - AHEAD - LATE, width, chans), BF16),
             jax.ShapeDtypeStruct((LATE, width, chans), BF16),
@@ -110,21 +131,24 @@
         scratch_shapes=[
             pltpu.VMEM(feat.shape, BF16),
             pltpu.VMEM((2 * frames, 8, chans), F32),
+            pltpu.SMEM((CLIPS,), jnp.int32),
+            pltpu.SMEM((CLIPS,), jnp.int32),
             pltpu.SemaphoreType.DMA((CLIPS,)),
-            pltpu.SemaphoreType.DMA((2 * frames + 4,)),
+            pltpu.SemaphoreType.DMA((4,)),
+            pltpu.SemaphoreType.DMA((2,)),
         ],
         compiler_params=pltpu.CompilerParams(vmem_limit_bytes=16 * MIB),
         cost_estimate=pl.CostEstimate(flops=LOW, bytes_accessed=LOW, transcendentals=0),
         name="channel_stats",
-    )(ints, pltpu.with_memory_space_constraint(feat, pltpu.HBM))
-
-
-def clip_kernel(ints, table, sums, past_in, edge_in, o_ref, past, edge):
-    del past_in, edge_in, past, edge
+    )(*(pltpu.with_memory_space_constraint(x, pltpu.HBM) for x in (clip_len, owner, feat)))
+
+
+def clip_kernel(table, sums, past_in, down_in, up_in, o_ref, past, down, up):
+    del past_in, down_in, up_in, past, down, up
     shape = (8, sums.shape[0])
     row = lax.broadcasted_iota(jnp.int32, shape, 0)
     col = lax.broadcasted_iota(jnp.int32, shape, 1)
-    frame = (col // 8) * 4 + col % 4 - 4 * ints[0]
+    frame = (col // 8) * 4 + col % 4 - table[FIRST]
     start = jnp.zeros(shape, jnp.int32)
     end = jnp.zeros(shape, jnp.int32)
     for f in range(4):
@@ -137,21 +161,22 @@
         o_ref[d] = tot
 
 
-def clip_sums(ints, table, sums, past, edge, copies):
+def clip_sums(table, sums, past, down, up, copies):
     return pl.pallas_call(
         clip_kernel,
-        in_specs=[SM, SM, VM, HBM, ANY],
-        out_specs=[VM, HBM, ANY],
+        in_specs=[SM, VM, HBM, ANY, ANY],
+        out_specs=[VM, HBM, ANY, ANY],
         out_shape=[
             jax.ShapeDtypeStruct((copies, 8, sums.shape[1]), F32),
             jax.ShapeDtypeStruct(past.shape, BF16),
-            jax.ShapeDtypeStruct(edge.shape, BF16),
-        ],
-        input_output_aliases={3: 1, 4: 2},
+            jax.ShapeDtypeStruct(down.shape, BF16),
+            jax.ShapeDtypeStruct(up.shape, BF16),
+        ],
+        input_output_aliases={2: 1, 3: 2, 4: 3},
         compiler_params=pltpu.CompilerParams(vmem_limit_bytes=4 * MIB),
         cost_estimate=pl.CostEstimate(flops=LOW, bytes_accessed=LOW, transcendentals=0),
         name="clip_sums",
-    )(ints, table, sums, past, edge)
+    )(table, sums, past, down, up)
 
 
 def sides_kernel(near, top, bot, mid, sides, sem):
@@ -346,8 +371,8 @@
 
 def local_kernel(
     table, feat, top, bot, bank, near, gamma_ref, beta_ref, cbias_ref, proj_ref, pbias_ref,
-    block_hbm, part, lat_ref, affine_ref,
-    page, lift0, lift1, lift2, lift3, conv2, conv3, obuf, lscr, projt, pbias, osems,
+    block_hbm, part, lat_ref, affine_ref, projt, pbias,
+    page, lift0, lift1, lift2, lift3, conv2, conv3, obuf, lscr, osems,
 ):
     tot = jnp.sum(near[...], axis=0)
     chans = tot.shape[1]
@@ -372,9 +397,9 @@
     lifts = (lift0, lift1, lift2, lift3)
     picks = [pick_taps(starts[t], t) for t in range(4)]
 
-    def lift(f):
+    def lift(f, pairs=range(PAIRS)):
         return lift_steps(
-            rows_of(lambda r: feat[f, r], top.at[f], bot.at[f]), range(PAIRS),
+            rows_of(lambda r: feat[f, r], top.at[f], bot.at[f]), pairs,
             affine_ref[f : f + 1], affine_ref[4 + f : 5 + f], top_on, bot_on, page, lifts[f],
         )
 
@@ -387,9 +412,10 @@
     def send(f):
         return pltpu.make_async_copy(obuf.at[f - 2], block_hbm.at[f], osems.at[f - 2])
 
-    for step in lift(0):
+    for step in lift(0, UPPER):
         step()
-    conv_frame(bank, taps(0), part.at[0], None, lift(1))
+    conv_frame(bank, taps(0), part.at[0], None, lift(0, LOWER), UPPER)
+    conv_frame(bank, taps(0), part.at[0], None, lift(1), LOWER)
     conv_frame(bank, taps(1), part.at[1], None, lift(2))
     conv_frame(bank, taps(2), conv2, None, lift(3))
     conv_frame(bank, taps(3), conv3, None, finish(2, conv2))
@@ -408,12 +434,14 @@
     return pl.pallas_call(
         local_kernel,
         in_specs=[SM] + [VM] * 10,
-        out_specs=[ANY, VM, VM, VM],
+        out_specs=[ANY, VM, VM, VM, VM, VM],
         out_shape=[
             jax.ShapeDtypeStruct(shape, BF16),
             jax.ShapeDtypeStruct((2, 2, PAIRS) + shape[2:], F32),
             jax.ShapeDtypeStruct((16, 2, 16, 128), BF16),
             jax.ShapeDtypeStruct((8, 256), F32),
+            jax.ShapeDtypeStruct((256, 128), BF16),
+            jax.ShapeDtypeStruct((1, 128), F32),
         ],
         scratch_shapes=[
             pltpu.VMEM((8, 128, 768), BF16),
@@ -425,8 +453,6 @@
             pltpu.VMEM((2, PAIRS, 128, 256), F32),
             pltpu.VMEM((2, 16, 128, 256), BF16),
             pltpu.VMEM((16, 128, 128), F32),
-            pltpu.VMEM((256, 128), BF16),
-            pltpu.VMEM((1, 128), F32),
             pltpu.SemaphoreType.DMA((2,)),
         ],
         compiler_params=pltpu.CompilerParams(vmem_limit_bytes=LOCAL_VMEM * MIB),
@@ -441,25 +467,26 @@
 
 
 def one_kernel(
-    table, past, sides, feat, bank, part, affine_ref, cbias_ref, proj_ref, pbias_ref, block_in,
+    table, past, sides, feat, bank, part, affine_ref, cbias_ref, projt, pbias, block_in,
     block_hbm, half0, lat_ref,
-    page, lift1, lift2, conv1, obuf, lscr, projt, pbias, sem,
+    page, lift1, lift2, conv1, obuf, lscr, sem,
 ):
     del block_in
-    spread_latent(proj_ref, pbias_ref, projt, pbias)
     pick0, pick1 = pick_taps(table[STARTS], 0), pick_taps(table[STARTS + 1], 1)
     on = (table[EDGES].astype(F32), table[EDGES + 1].astype(F32))
     hs, hb = past_affine(table, affine_ref, 0)
     one = rows_of(lambda r: past[AHEAD + r], sides.at[1], sides.at[3])
-    for step in lift_steps(one, range(PAIRS), hs, hb, *on, page, lift1):
+    for step in lift_steps(one, UPPER, hs, hb, *on, page, lift1):
         step()
+    rest = lift_steps(one, LOWER, hs, hb, *on, page, lift1)
     hs, hb = past_affine(table, affine_ref, 1)
     low = rows_of(lambda r: two_row(r, None, sides, past), None, sides.at[2])
     steps = lift_steps(low, LOWER, hs, hb, *on, page, lift2)
-    conv_frame(bank, [(lift1, pick1[2])], conv1, part.at[1], steps)
+    conv_frame(bank, [(lift1, pick1[2])], conv1, part.at[1], rest, UPPER)
+    conv_frame(bank, [(lift1, pick1[2])], conv1, part.at[1], steps, LOWER)
     conv_frame(
         bank, [(lift1, pick0[1])], half0, part.at[0],
-        finish_steps(conv1, feat.at[0], cbias_ref, obuf),
+        finish_steps(conv1, feat.at[1], cbias_ref, obuf),
     )
     out = pltpu.make_async_copy(obuf, block_hbm.at[1], sem)
     out.start()
@@ -475,13 +502,12 @@
 
 
 def two_kernel(
-    table, late, past, sides, feat, bank, half0, affine_ref, cbias_ref, proj_ref, pbias_ref,
+    table, late, past, sides, feat, bank, half0, affine_ref, cbias_ref, projt, pbias,
     early_ref, one_ref, block_in,
     block_hbm, lat_ref,
-    page, lifted, conv0, obuf, lscr, projt, pbias, sem,
+    page, lifted, conv0, obuf, lscr, sem,
 ):
     del block_in
-    spread_latent(proj_ref, pbias_ref, projt, pbias)
     pick0 = pick_taps(table[STARTS], 0)
     on = (table[EDGES].astype(F32), table[EDGES + 1].astype(F32))
     hs, hb = past_affine(table, affine_ref, 1)
@@ -509,8 +535,6 @@
         pltpu.VMEM((2, PAIRS) + shape[2:], F32),
         pltpu.VMEM(shape[1:], BF16),
         pltpu.VMEM((16, 128, 128), F32),
-        pltpu.VMEM((256, 128), BF16),
-        pltpu.VMEM((1, 128), F32),
         pltpu.SemaphoreType.DMA,
     ]
 
@@ -519,10 +543,7 @@
     shape = feat.shape
     return pl.pallas_call(
         one_kernel,
-        grid=(1,),
-        in_specs=[SM, VM, VM, pl.BlockSpec((1,) + shape[1:], lambda i: (1, 0, 0, 0))]
-        + [VM] * 6
-        + [ANY],
+        in_specs=[SM] + [VM] * 9 + [ANY],
         out_specs=[ANY, VM, VM],
         out_shape=[
             jax.ShapeDtypeStruct(shape, BF16),
@@ -543,10 +564,7 @@
     shape = feat.shape
     return pl.pallas_call(
         two_kernel,
-        grid=(1,),
-        in_specs=[SM, VM, VM, VM, pl.BlockSpec((1,) + shape[1:], lambda i: (0, 0, 0, 0))]
-        + [VM] * 8
-        + [ANY],
+        in_specs=[SM] + [VM] * 12 + [ANY],
         out_specs=[ANY, VM],
         out_shape=[
             jax.ShapeDtypeStruct(shape, BF16),
@@ -606,15 +624,13 @@
     frames, band = feat.shape[:2]
     n_time = lax.axis_size("tm")
 
-    place_of = jnp.stack([lax.axis_index("tm"), lax.axis_index("rows")]).astype(jnp.int32)
-    ints = jnp.concatenate([place_of, clip_len, owner])
-    sums, table, edge, one, mid, two = channel_stats(ints, feat, n_time)
+    sums, table, down, up, one, mid, two = channel_stats(clip_len, owner, feat, n_time)
     sums = lax.all_to_all(sums, "tm", split_axis=0, concat_axis=0, tiled=True)
-    sums, one, edge = clip_sums(
-        ints, table, sums.reshape(-1, sums.shape[-1]), one, edge, lax.axis_size("rows")
+    sums, one, down, up = clip_sums(
+        table, sums.reshape(-1, sums.shape[-1]), one, down, up, lax.axis_size("rows")
     )
     one = shift(one, "tm", 1)
-    top, bot = shift(edge[0], "rows", 1), shift(edge[1], "rows", -1)
+    top, bot = shift(down, "rows", 1), shift(up, "rows", -1)
     near = lax.all_to_all(sums, "rows", split_axis=0, concat_axis=0, tiled=True)
     sides = pack_sides(near, top, bot, mid)
     bank, two = weight_bank(conv_weight, sides, two)
@@ -622,15 +638,15 @@
     two = shift(two, "tm", 1)
 
     cbias, pbias = conv_bias[None, :], proj_bias[None, :]
-    block, part, early, affine = local_part(
+    block, part, early, affine, projt, ptile = local_part(
         table, feat, top, bot, bank, near, gamma[None, :], beta[None, :], cbias, proj.T,
         pbias,
     )
     block, part, lat = one_part(
-        table, one, sides, feat, bank, part, affine, cbias, proj.T, pbias, block
+        table, one, sides, feat, bank, part, affine, cbias, projt, ptile, block
     )
     block, lat = two_part(
-        table, two, one, sides, feat, bank, part, affine, cbias, proj.T, pbias, early, lat, block
+        table, two, one, sides, feat, bank, part, affine, cbias, projt, ptile, early, lat, block
     )
     shares = lax.all_to_all(lat, "tm", split_axis=0, concat_axis=0, tiled=True)
     placed = place(table, shares.reshape(n_time * frames, band, 128))

time: 108 us -> 107 us (level)
  blocking collectives: 54.7 us -> 57.2 us
  starting transfers between devices: 13.2 us -> 11.3 us
    all_to_all x1, blocking collectives: 10.1 us -> 12.7 us  [on_device(): near = lax.all_to_all(sums, 'rows', split_axis=0, concat_axis=0, tiled=True)]
    ppermute x5, starting transfers between devices: 13.2 us -> 11.3 us  [shift(): lax.ppermute(x, axis, [(i, i + by) for i in range(n) if 0 <= i + by < n])]
  transfers between devices with their start and end apart: 5 -> 5, of which waited for: 2 -> 1; matrix products, arithmetic and copies ran while one was open for 0% -> 0% of each run, Pallas kernels for 25% -> 25%
where the time goes in v4:
time: 107 us
  blocking collectives  57.2 us (53%)
  Pallas kernels  36.5 us (34%)
  starting transfers between devices  11.3 us (11%)
    pallas_call x1, Pallas kernels, local_part(): pl.pallas_call(local_kernel, in_specs=[SM] + [VM] * 10, out_specs=[ANY, V...  18.3 us
    all_to_all x1, blocking collectives, on_device(): sums = lax.all_to_all(sums, 'tm', split_axis=0, concat_axis=0, tiled=True)  15.8 us
    all_to_all x1, blocking collectives, on_device(): shares = lax.all_to_all(lat, 'tm', split_axis=0, concat_axis=0, tiled=True)  15.2 us
    all_to_all x1, blocking collectives, on_device(): lax.all_to_all(placed.reshape(n_time, SEQ_CAP, band, 128), 'tm', split_ax...  13.6 us
    all_to_all x1, blocking collectives, on_device(): near = lax.all_to_all(sums, 'rows', split_axis=0, concat_axis=0, tiled=True)  12.7 us
    ppermute x5, starting transfers between devices, shift(): lax.ppermute(x, axis, [(i, i + by) for i in range(n) if 0 <= i + by < n])  11.3 us
    pallas_call x1, Pallas kernels, one_part(): pl.pallas_call(one_kernel, in_specs=[SM] + [VM] * 9 + [ANY], out_specs=[A...  6.67 us
    pallas_call x1, Pallas kernels, channel_stats(): pl.pallas_call(stats_kernel, in_specs=[HBM, HBM, HBM], out_specs=[VM, SM,...  4.01 us
  transfers between devices with their start and end apart: 5, of which 1 were waited for; matrix products, arithmetic and copies ran while one was open for 0% of the time, Pallas kernels for 25%

profile of v4, /device:TPU:0, one launch (start us, length us, event | category | flops | bytes accessed | tf_op | source)
XLA Modules:
  0.0 106.5 jit_solution(11217875448377127110)
XLA Ops:
  0.6 0.0 copy-start.1
  0.6 4.0 %channel_stats.1 = (f32[16,8,256]{2,1,0:T(8,128)S(1)}, s32[88]{0:T(128)S(1)}, bf16[4,128,256]{2,1,0:T(8,128)(2,1)S(1)}, bf16[4,128,256]{2,1,0:T(8,128)(2,1)S(1)}...) custom-call(s32[16]{0:T(128)} %clip_len_hbm.1, ...), custom_call_target="tpu_custom_call" | custom-call | flops 1000 | bytes 1000 | tf_op jit(solution)/shard_map/channel_stats/pallas_call | solution.py:118
  4.7 15.8 %all_to_all.20 = f32[16,8,256]{2,1,0:T(8,128)S(1)} all-to-all(f32[16,8,256]{2,1,0:T(8,128)S(1)} %get-tuple-element.27), channel_id=1, replica_groups=mesh['tm'=16,'rows'=8] {'tm'}, dimensions={0} | all-to-all | bytes 262144 | tf_op jit(solution)/shard_map/all_to_all | solution.py:628
  20.4 0.0 copy-start
  20.4 0.0 copy-start.2
  20.4 0.0 copy-start.3
  20.4 0.0 copy-start.4
  20.4 0.0 copy-start.5
  20.5 0.0 copy-start.6
  20.5 0.7 clip_sums.1
  21.2 2.6 %collective-permute-start.3 = (bf16[19,128,256]{2,1,0:T(8,128)(2,1)S(1)}, bf16[19,128,256]{2,1,0:T(8,128)(2,1)S(1)}, u32[]{:S(2)}, u32[]{:S(2)}) collective-permute-start(bf16[19,128,256]{2,1,0:T(8,128)(2,1)S(1)} %get-tuple-element.37), channel_id=1, source_target_pairs={{0,8},{8,16},{16,24},{24,32},{32,40},{40,48},{48,56},{56,64},{64,7... | collective-permute-start | bytes 3735560 | tf_op jit(solution)/shard_map/ppermute | solution.py:620
  23.8 1.3 %collective-permute-start = (bf16[4,128,256]{2,1,0:T(8,128)(2,1)S(1)}, bf16[4,128,256]{2,1,0:T(8,128)(2,1)S(1)}, u32[]{:S(2)}, u32[]{:S(2)}) collective-permute-start(bf16[4,128,256]{2,1,0:T(8,128)(2,1)S(1)} %get-tuple-element.32), channel_id=1, source_target_pairs={{0,1},{1,2},{2,3},{3,4},{4,5},{5,6},{6,7},{8,9},{9,10},{10,11},{11... | collective-permute-start | bytes 786440 | tf_op jit(solution)/shard_map/ppermute | solution.py:620
  25.1 1.3 %collective-permute-start.1 = (bf16[4,128,256]{2,1,0:T(8,128)(2,1)S(1)}, bf16[4,128,256]{2,1,0:T(8,128)(2,1)S(1)}, u32[]{:S(2)}, u32[]{:S(2)}) collective-permute-start(bf16[4,128,256]{2,1,0:T(8,128)(2,1)S(1)} %get-tuple-element.33), channel_id=1, source_target_pairs={{1,0},{2,1},{3,2},{4,3},{5,4},{6,5},{7,6},{9,8},{10,9},{11,10},{12... | collective-permute-start | bytes 786440 | tf_op jit(solution)/shard_map/ppermute | solution.py:620
  26.4 12.7 %all_to_all.21.near = f32[8,8,256]{2,1,0:T(8,128)S(1)} all-to-all(f32[8,8,256]{2,1,0:T(8,128)S(1)} %get-tuple-element.31), channel_id=1, replica_groups=mesh['tm'=16,'rows'=8] {'rows'}, dimensions={0} | all-to-all | bytes 131072 | tf_op jit(solution)/shard_map/all_to_all | solution.py:634
  39.1 0.0 collective-permute-done.top
  39.1 0.0 collective-permute-done.1.bot
  39.1 0.6 pack_sides.1.sides
  39.7 2.9 %collective-permute-start.4 = (bf16[10,128,256]{2,1,0:T(8,128)(2,1)S(1)}, bf16[10,128,256]{2,1,0:T(8,128)(2,1)S(1)}, u32[]{:S(2)}, u32[]{:S(2)}) collective-permute-start(bf16[10,128,256]{2,1,0:T(8,128)(2,1)S(1)} %pack_sides.1.sides), channel_id=1, source_target_pairs={{0,8},{8,16},{16,24},{24,32},{32,40},{40,48},{48,56},{56,64},{64,7... | collective-permute-start | bytes 1966088 | tf_op jit(solution)/shard_map/ppermute | solution.py:620
  42.6 0.0 copy-done.1
  42.6 1.4 %weight_bank.1 = (bf16[21,768,256]{2,1,0:T(8,128)(2,1)S(1)}, bf16[7,128,256]{2,1,0:T(8,128)(2,1)S(1)}) custom-call(bf16[3,3,768,256]{3,2,1,0:T(8,128)(2,1)S(1)} %copy-done.1, bf16[10,128,256]{2,1,0:T(8,128)(2,1)S(1)} %pack_sides.1.sides, bf16[7,128,256]{2,1,0:T(8,128)(2,1)S(1)} %get-tuple-element.35.page_in), custom_call_target="tpu_custom_call", output_to_operand_aliasing={{1}: (2, {})} | custom-call | flops 1000 | bytes 1000 | tf_op jit(solution)/shard_map/weight_bank/pallas_call | solution.py:251
  43.9 3.3 %collective-permute-start.2 = (bf16[7,128,256]{2,1,0:T(8,128)(2,1)S(1)}, bf16[7,128,256]{2,1,0:T(8,128)(2,1)S(1)}, u32[]{:S(2)}, u32[]{:S(2)}) collective-permute-start(bf16[7,128,256]{2,1,0:T(8,128)(2,1)S(1)} %get-tuple-element.36), channel_id=1, source_target_pairs={{0,8},{8,16},{16,24},{24,32},{32,40},{40,48},{48,56},{56,64},{64,7... | collective-permute-start | bytes 1376264 | tf_op jit(solution)/shard_map/ppermute | solution.py:620
  47.2 0.0 copy-done
  47.2 0.0 copy-done.2
  47.2 0.0 copy-done.3
  47.2 0.0 copy-done.4
  47.3 0.0 copy-done.5
  47.3 0.0 copy-done.6
  47.3 18.3 %local_conv.1 = (bf16[4,16,128,256]{3,2,1,0:T(8,128)(2,1)}, f32[2,2,8,128,256]{4,3,2,1,0:T(8,128)S(1)}, bf16[16,2,16,128]{3,2,1,0:T(8,128)(2,1)S(1)}, f32[8,256]...) custom-call(s32[88]{0:T(128)S(1)} %get-tuple-element.26.table, ...), custom_call_target="tpu_custom_call" | custom-call | flops 1000 | bytes 1000 | tf_op jit(solution)/shard_map/local_conv/pallas_call | solution.py:434
  65.6 0.0 collective-permute-done.4.sides
  65.6 0.0 collective-permute-done.3.past
  65.6 6.7 %past_one.1 = (bf16[4,16,128,256]{3,2,1,0:T(8,128)(2,1)}, f32[2,8,128,256]{3,2,1,0:T(8,128)S(1)}, bf16[16,1,16,128]{3,2,1,0:T(8,128)(2,1)S(1)}) custom-call(s32[88]{0:T(128)S(1)} %get-tuple-element.26.table, bf16[19,128,256]{2,1,0:T(8,128)(2,1)S(1)} %collective-permute-done.3.past, ...), custom_call_target="tpu_custom_call", output_to_operand_aliasing={{0}: (10, {})} | custom-call | flops 1000 | bytes 1000 | tf_op jit(solution)/shard_map/past_one/pallas_call | solution.py:544
  72.3 0.6 collective-permute-done.2.late
  72.9 3.2 %past_two.1 = (bf16[4,16,128,256]{3,2,1,0:T(8,128)(2,1)}, bf16[16,4,16,128]{3,2,1,0:T(8,128)(2,1)S(1)}) custom-call(s32[88]{0:T(128)S(1)} %get-tuple-element.26.table, bf16[7,128,256]{2,1,0:T(8,128)(2,1)S(1)} %collective-permute-done.2.late, bf16[19,128,256]{2,1,0:T(8,128)(2,1)S(1)} %collective-permute-done.3.past, ...), custom_call_target="tpu_custom_call", output_to_operand_aliasing={{0}: (13, {})} | custom-call | flops 1000 | bytes 1000 | tf_op jit(solution)/shard_map/past_two/pallas_call | solution.py:565
  76.1 15.2 %all_to_all.22 = bf16[16,4,16,128]{3,2,1,0:T(8,128)(2,1)S(1)} all-to-all(bf16[16,4,16,128]{3,2,1,0:T(8,128)(2,1)S(1)} %get-tuple-element.49), channel_id=1, replica_groups=mesh['tm'=16,'rows'=8] {'tm'}, dimensions={0} | all-to-all | bytes 524288 | tf_op jit(solution)/shard_map/all_to_all | solution.py:651
  91.3 0.7 place_frames.1
  92.0 13.6 %all_to_all.23.x_ref = bf16[16,8,16,128]{3,2,1,0:T(8,128)(2,1)S(1)} all-to-all(bf16[16,8,16,128]{3,2,1,0:T(8,128)(2,1)S(1)} %bitcast.8), channel_id=1, replica_groups=mesh['tm'=16,'rows'=8] {'tm'}, dimensions={0} | all-to-all | bytes 1048576 | tf_op jit(solution)/shard_map/all_to_all | solution.py:653
  105.6 0.9 merge_columns.1
Async XLA Ops:
  0.6 41.9 %copy-start.1 = (bf16[3,3,768,256]{3,2,1,0:T(8,128)(2,1)S(1)}, bf16[3,3,768,256]{3,2,1,0:T(8,128)(2,1)}, u32[]{:S(2)}) copy-start(bf16[3,3,768,256]{3,2,1,0:T(8,128)(2,1)} %w.1) | copy-start | bytes 10616836
  20.4 26.8 %copy-start = (bf16[4,16,128,256]{3,2,1,0:T(8,128)(2,1)S(1)}, bf16[4,16,128,256]{3,2,1,0:T(8,128)(2,1)}, u32[]{:S(2)}) copy-start(bf16[4,16,128,256]{3,2,1,0:T(8,128)(2,1)} %feat.7) | copy-start | bytes 12582916
  20.4 26.8 %copy-start.2 = (f32[256]{0:T(256)S(1)}, f32[256]{0:T(256)}, u32[]{:S(2)}) copy-start(f32[256]{0:T(256)} %param.13) | copy-start | bytes 3076
  20.4 26.8 %copy-start.3 = (bf16[256,16]{0,1:T(8,128)(2,1)S(1)}, bf16[256,16]{0,1:T(8,128)(2,1)}, u32[]{:S(2)}) copy-start(bf16[256,16]{0,1:T(8,128)(2,1)} %param.14) | copy-start | bytes 24580
  20.4 26.8 %copy-start.4 = (f32[256]{0:T(256)S(1)}, f32[256]{0:T(256)}, u32[]{:S(2)}) copy-start(f32[256]{0:T(256)} %param.10) | copy-start | bytes 3076
  20.4 26.8 %copy-start.5 = (f32[256]{0:T(256)S(1)}, f32[256]{0:T(256)}, u32[]{:S(2)}) copy-start(f32[256]{0:T(256)} %param.11) | copy-start | bytes 3076
  20.5 26.8 %copy-start.6 = (f32[16]{0:T(128)S(1)}, f32[16]{0:T(128)}, u32[]{:S(2)}) copy-start(f32[16]{0:T(128)} %param.15) | copy-start | bytes 196
  21.2 44.4 %collective-permute-start.3 = (bf16[19,128,256]{2,1,0:T(8,128)(2,1)S(1)}, bf16[19,128,256]{2,1,0:T(8,128)(2,1)S(1)}, u32[]{:S(2)}, u32[]{:S(2)}) collective-permute-start(bf16[19,128,256]{2,1,0:T(8,128)(2,1)S(1)} %get-tuple-element.37), channel_id=1, source_target_pairs={{0,8},{8,16},{16,24},{24,32},{32,40},{40,48},{48,56},{56,64},{64,7... | collective-permute-start | bytes 3735560 | tf_op jit(solution)/shard_map/ppermute | solution.py:620
  23.8 15.3 %collective-permute-start = (bf16[4,128,256]{2,1,0:T(8,128)(2,1)S(1)}, bf16[4,128,256]{2,1,0:T(8,128)(2,1)S(1)}, u32[]{:S(2)}, u32[]{:S(2)}) collective-permute-start(bf16[4,128,256]{2,1,0:T(8,128)(2,1)S(1)} %get-tuple-element.32), channel_id=1, source_target_pairs={{0,1},{1,2},{2,3},{3,4},{4,5},{5,6},{6,7},{8,9},{9,10},{10,11},{11... | collective-permute-start | bytes 786440 | tf_op jit(solution)/shard_map/ppermute | solution.py:620
  25.1 14.0 %collective-permute-start.1 = (bf16[4,128,256]{2,1,0:T(8,128)(2,1)S(1)}, bf16[4,128,256]{2,1,0:T(8,128)(2,1)S(1)}, u32[]{:S(2)}, u32[]{:S(2)}) collective-permute-start(bf16[4,128,256]{2,1,0:T(8,128)(2,1)S(1)} %get-tuple-element.33), channel_id=1, source_target_pairs={{1,0},{2,1},{3,2},{4,3},{5,4},{6,5},{7,6},{9,8},{10,9},{11,10},{12... | collective-permute-start | bytes 786440 | tf_op jit(solution)/shard_map/ppermute | solution.py:620
  39.7 25.9 %collective-permute-start.4 = (bf16[10,128,256]{2,1,0:T(8,128)(2,1)S(1)}, bf16[10,128,256]{2,1,0:T(8,128)(2,1)S(1)}, u32[]{:S(2)}, u32[]{:S(2)}) collective-permute-start(bf16[10,128,256]{2,1,0:T(8,128)(2,1)S(1)} %pack_sides.1.sides), channel_id=1, source_target_pairs={{0,8},{8,16},{16,24},{24,32},{32,40},{40,48},{48,56},{56,64},{64,7... | collective-permute-start | bytes 1966088 | tf_op jit(solution)/shard_map/ppermute | solution.py:620
  43.9 28.9 %collective-permute-start.2 = (bf16[7,128,256]{2,1,0:T(8,128)(2,1)S(1)}, bf16[7,128,256]{2,1,0:T(8,128)(2,1)S(1)}, u32[]{:S(2)}, u32[]{:S(2)}) collective-permute-start(bf16[7,128,256]{2,1,0:T(8,128)(2,1)S(1)} %get-tuple-element.36), channel_id=1, source_target_pairs={{0,8},{8,16},{16,24},{24,32},{32,40},{40,48},{48,56},{56,64},{64,7... | collective-permute-start | bytes 1376264 | tf_op jit(solution)/shard_map/ppermute | solution.py:620

commit v5 on v4

--- a/solution.py
+++ b/solution.py
@@ -19,7 +19,7 @@
 F32 = jnp.float32
 BF16 = jnp.bfloat16
 MIB = 2**20
-STARTS, ENDS, EDGES, FIRST, CODES = 0, 4, 8, 10, 16
+STARTS, ENDS, EDGES, FIRST, TABLE = 0, 4, 8, 10, 16
 ANY = pl.BlockSpec(memory_space=pl.ANY)
 VM = pl.BlockSpec(memory_space=pltpu.VMEM)
 SM = pl.BlockSpec(memory_space=pltpu.SMEM)
@@ -27,18 +27,14 @@
 
 
 def stats_kernel(
-    clip_len_hbm, owner_hbm, feat, o_ref, table, down_ref, up_ref, one_ref, mid_ref, two_ref, x_ref, sums,
-    clip_len, owner, sems, osems, isems,
+    clip_len_hbm, feat, o_ref, table, down_ref, up_ref, one_ref, mid_ref, two_ref, x_ref, sums,
+    clip_len, sems, osems, isem,
 ):
     frames, band = x_ref.shape[:2]
     quarter = band // 4
     split = band - AHEAD
-    ints = [
-        pltpu.make_async_copy(clip_len_hbm, clip_len, isems.at[0]),
-        pltpu.make_async_copy(owner_hbm, owner, isems.at[1]),
-    ]
-    for c in ints:
-        c.start()
+    ints = pltpu.make_async_copy(clip_len_hbm, clip_len, isem)
+    ints.start()
     order = [(f, q) for f in (2, 3, 0, 1) for q in range(4)]
     loads = [
         pltpu.make_async_copy(
@@ -75,17 +71,13 @@
     starts = [jnp.int32(0)] * 4
     ends = [jnp.int32(0)] * 4
     start = jnp.int32(0)
-    for c in ints:
-        c.wait()
+    ints.wait()
     for i, (f, q) in enumerate(order):
         end = start + clip_len[i]
-        base = owner[i] * SEQ_CAP
         for own in range(4):
             inside = jnp.logical_and(first + own >= start, first + own < end)
             starts[own] = jnp.where(inside, start - first, starts[own])
             ends[own] = jnp.where(inside, end - first, ends[own])
-        for k in range(SEQ_CAP):
-            table[CODES + start + k] = base + k
         start = end
         loads[i].wait()
         if q == 3:
@@ -113,15 +105,15 @@
         c.wait()
 
 
-def channel_stats(clip_len, owner, feat, copies):
+def channel_stats(clip_len, feat, copies):
     frames, band, width, chans = feat.shape
     return pl.pallas_call(
         stats_kernel,
-        in_specs=[HBM, HBM, HBM],
+        in_specs=[HBM, HBM],
         out_specs=[VM, SM, VM, VM, HBM, HBM, HBM],
         out_shape=[
             jax.ShapeDtypeStruct((copies, 2 * frames, chans), F32),
-            jax.ShapeDtypeStruct((CODES + 64 + SEQ_CAP,), jnp.int32),
+            jax.ShapeDtypeStruct((TABLE,), jnp.int32),
             jax.ShapeDtypeStruct((frames, width, chans), BF16),
             jax.ShapeDtypeStruct((frames, width, chans), BF16),
             jax.ShapeDtypeStruct((band + AHEAD, width, chans), BF16),
@@ -132,19 +124,35 @@
             pltpu.VMEM(feat.shape, BF16),
             pltpu.VMEM((2 * frames, 8, chans), F32),
             pltpu.SMEM((CLIPS,), jnp.int32),
-            pltpu.SMEM((CLIPS,), jnp.int32),
             pltpu.SemaphoreType.DMA((CLIPS,)),
             pltpu.SemaphoreType.DMA((4,)),
-            pltpu.SemaphoreType.DMA((2,)),
+            pltpu.SemaphoreType.DMA,
         ],
         compiler_params=pltpu.CompilerParams(vmem_limit_bytes=16 * MIB),
         cost_estimate=pl.CostEstimate(flops=LOW, bytes_accessed=LOW, transcendentals=0),
         name="channel_stats",
-    )(*(pltpu.with_memory_space_constraint(x, pltpu.HBM) for x in (clip_len, owner, feat)))
-
-
-def clip_kernel(table, sums, past_in, down_in, up_in, o_ref, past, down, up):
-    del past_in, down_in, up_in, past, down, up
+    )(*(pltpu.with_memory_space_constraint(x, pltpu.HBM) for x in (clip_len, feat)))
+
+
+def after_kernel(sums, page_in, page):
+    del sums, page_in, page
+
+
+def after(sums, page):
+    return pl.pallas_call(
+        after_kernel,
+        in_specs=[ANY, HBM],
+        out_specs=HBM,
+        out_shape=jax.ShapeDtypeStruct(page.shape, BF16),
+        input_output_aliases={1: 0},
+        compiler_params=pltpu.CompilerParams(vmem_limit_bytes=4 * MIB),
+        cost_estimate=pl.CostEstimate(flops=LOW, bytes_accessed=LOW, transcendentals=0),
+        name="after_sums",
+    )(sums, page)
+
+
+def clip_kernel(table, sums, down_in, up_in, o_ref, down, up):
+    del down_in, up_in, down, up
     shape = (8, sums.shape[0])
     row = lax.broadcasted_iota(jnp.int32, shape, 0)
     col = lax.broadcasted_iota(jnp.int32, shape, 1)
@@ -161,22 +169,21 @@
         o_ref[d] = tot
 
 
-def clip_sums(table, sums, past, down, up, copies):
+def clip_sums(table, sums, down, up, copies):
     return pl.pallas_call(
         clip_kernel,
-        in_specs=[SM, VM, HBM, ANY, ANY],
-        out_specs=[VM, HBM, ANY, ANY],
+        in_specs=[SM, VM, ANY, ANY],
+        out_specs=[VM, ANY, ANY],
         out_shape=[
             jax.ShapeDtypeStruct((copies, 8, sums.shape[1]), F32),
-            jax.ShapeDtypeStruct(past.shape, BF16),
             jax.ShapeDtypeStruct(down.shape, BF16),
             jax.ShapeDtypeStruct(up.shape, BF16),
         ],
-        input_output_aliases={2: 1, 3: 2, 4: 3},
+        input_output_aliases={2: 1, 3: 2},
         compiler_params=pltpu.CompilerParams(vmem_limit_bytes=4 * MIB),
         cost_estimate=pl.CostEstimate(flops=LOW, bytes_accessed=LOW, transcendentals=0),
         name="clip_sums",
-    )(table, sums, past, down, up)
+    )(table, sums, down, up)
 
 
 def sides_kernel(near, top, bot, mid, sides, sem):
@@ -226,8 +233,16 @@
 TAP0, TAP1, TAP2, TAP01, TAP012, NONE = 0, 1, 2, 3, 4, 5
 
 
-def bank_kernel(w, sides, page_in, bank, page):
+def bank_kernel(
+    clip_len_hbm, owner_hbm, w, sides, page_in, bank, codes, page, clip_len, owner, sems
+):
     del sides, page_in, page
+    ints = [
+        pltpu.make_async_copy(clip_len_hbm, clip_len, sems.at[0]),
+        pltpu.make_async_copy(owner_hbm, owner, sems.at[1]),
+    ]
+    for c in ints:
+        c.start()
 
     def step(i, _):
         r = pl.ds(pl.multiple_of(i * 16, 16), 16)
@@ -245,22 +260,39 @@
         return 0
 
     lax.fori_loop(0, w.shape[2] // 16, step, 0)
-
-
-def weight_bank(weight, sides, page):
+    for c in ints:
+        c.wait()
+    start = jnp.int32(0)
+    for i in range(CLIPS):
+        for k in range(SEQ_CAP):
+            codes[start + k] = owner[i] * SEQ_CAP + k
+        start = start + clip_len[i]
+
+
+def weight_bank(clip_len, owner, weight, sides, page):
     return pl.pallas_call(
         bank_kernel,
-        in_specs=[VM, ANY, HBM],
-        out_specs=[VM, HBM],
+        in_specs=[HBM, HBM, VM, ANY, HBM],
+        out_specs=[VM, SM, HBM],
         out_shape=[
             jax.ShapeDtypeStruct((4 * NONE + 1,) + weight.shape[2:], BF16),
+            jax.ShapeDtypeStruct((64 + SEQ_CAP,), jnp.int32),
             jax.ShapeDtypeStruct(page.shape, BF16),
         ],
-        input_output_aliases={2: 1},
+        input_output_aliases={4: 2},
+        scratch_shapes=[
+            pltpu.SMEM((CLIPS,), jnp.int32),
+            pltpu.SMEM((CLIPS,), jnp.int32),
+            pltpu.SemaphoreType.DMA((2,)),
+        ],
         compiler_params=pltpu.CompilerParams(vmem_limit_bytes=16 * MIB),
         cost_estimate=pl.CostEstimate(flops=LOW, bytes_accessed=LOW, transcendentals=0),
         name="weight_bank",
-    )(weight, sides, page)
+    )(
+        pltpu.with_memory_space_constraint(clip_len, pltpu.HBM),
+        pltpu.with_memory_space_constraint(owner, pltpu.HBM),
+        weight, sides, page,
+    )
 
 
 def lift_steps(row, pairs, hs, hb, top_on, bot_on, page, lifted):
@@ -578,17 +610,17 @@
     )(table, late, past, sides, feat, bank, half0, affine, cbias, proj, pbias, early, one, block)
 
 
-def place_kernel(table, x_ref, o_ref):
+def place_kernel(codes, x_ref, o_ref):
     o_ref[...] = jnp.zeros_like(o_ref)
 
     def put(t, _):
-        o_ref[table[CODES + t]] = x_ref[t]
+        o_ref[codes[t]] = x_ref[t]
         return 0
 
     lax.fori_loop(0, x_ref.shape[0], put, 0, unroll=8)
 
 
-def place(table, shares):
+def place(codes, shares):
     return pl.pallas_call(
         place_kernel,
         in_specs=[SM, VM],
@@ -596,7 +628,7 @@
         out_shape=jax.ShapeDtypeStruct((128, 16, 128), BF16),
         compiler_params=pltpu.CompilerParams(vmem_limit_bytes=4 * MIB),
         name="place_frames",
-    )(table, shares)
+    )(codes, shares)
 
 
 def merge_kernel(x_ref, o_ref):
@@ -624,16 +656,16 @@
     frames, band = feat.shape[:2]
     n_time = lax.axis_size("tm")
 
-    sums, table, down, up, one, mid, two = channel_stats(clip_len, owner, feat, n_time)
+    sums, table, down, up, one, mid, two = channel_stats(clip_len, feat, n_time)
     sums = lax.all_to_all(sums, "tm", split_axis=0, concat_axis=0, tiled=True)
-    sums, one, down, up = clip_sums(
-        table, sums.reshape(-1, sums.shape[-1]), one, down, up, lax.axis_size("rows")
-    )
-    one = shift(one, "tm", 1)
+    one = shift(after(sums, one), "tm", 1)
+    sums, down, up = clip_sums(
+        table, sums.reshape(-1, sums.shape[-1]), down, up, lax.axis_size("rows")
+    )
     top, bot = shift(down, "rows", 1), shift(up, "rows", -1)
     near = lax.all_to_all(sums, "rows", split_axis=0, concat_axis=0, tiled=True)
     sides = pack_sides(near, top, bot, mid)
-    bank, two = weight_bank(conv_weight, sides, two)
+    bank, codes, two = weight_bank(clip_len, owner, conv_weight, sides, two)
     sides = shift(sides, "tm", 1)
     two = shift(two, "tm", 1)
 
@@ -649,7 +681,7 @@
         table, two, one, sides, feat, bank, part, affine, cbias, projt, ptile, early, lat, block
     )
     shares = lax.all_to_all(lat, "tm", split_axis=0, concat_axis=0, tiled=True)
-    placed = place(table, shares.reshape(n_time * frames, band, 128))
+    placed = place(codes, shares.reshape(n_time * frames, band, 128))
     seq = lax.all_to_all(
         placed.reshape(n_time, SEQ_CAP, band, 128), "tm", split_axis=0, concat_axis=0, tiled=True
     )

time: 107 us -> 106 us (level)
    pallas_call x3 -> x4, Pallas kernels: 6.1 us -> 6.7 us  [the longest x1 3.87 us: channel_stats(): pl.pallas_call(stats_kernel, in_specs=[HBM, HBM], out_specs=[VM, SM, VM,...]
  transfers between devices with their start and end apart: 5 -> 5, of which waited for: 1 -> 0; matrix products, arithmetic and copies ran while one was open for 0% -> 0% of each run, Pallas kernels for 25% -> 27%
where the time goes in v5:
time: 106 us
  blocking collectives  56.3 us (53%)
  Pallas kernels  37.1 us (35%)
  starting transfers between devices  11.5 us (11%)
    pallas_call x1, Pallas kernels, local_part(): pl.pallas_call(local_kernel, in_specs=[SM] + [VM] * 10, out_specs=[ANY, V...  18.3 us
    all_to_all x1, blocking collectives, on_device(): sums = lax.all_to_all(sums, 'tm', split_axis=0, concat_axis=0, tiled=True)  15.8 us
    all_to_all x1, blocking collectives, on_device(): shares = lax.all_to_all(lat, 'tm', split_axis=0, concat_axis=0, tiled=True)  14.3 us
    all_to_all x1, blocking collectives, on_device(): lax.all_to_all(placed.reshape(n_time, SEQ_CAP, band, 128), 'tm', split_ax...  13.6 us
    all_to_all x1, blocking collectives, on_device(): near = lax.all_to_all(sums, 'rows', split_axis=0, concat_axis=0, tiled=True)  12.7 us
    ppermute x5, starting transfers between devices, shift(): lax.ppermute(x, axis, [(i, i + by) for i in range(n) if 0 <= i + by < n])  11.5 us
    pallas_call x1, Pallas kernels, one_part(): pl.pallas_call(one_kernel, in_specs=[SM] + [VM] * 9 + [ANY], out_specs=[A...  6.68 us
    pallas_call x1, Pallas kernels, channel_stats(): pl.pallas_call(stats_kernel, in_specs=[HBM, HBM], out_specs=[VM, SM, VM,...  3.87 us
  transfers between devices with their start and end apart: 5, of which 0 were waited for; matrix products, arithmetic and copies ran while one was open for 0% of the time, Pallas kernels for 27%

profile of v5, /device:TPU:0, one launch (start us, length us, event | category | flops | bytes accessed | tf_op | source)
XLA Modules:
  0.0 105.8 jit_solution(15901076580240765046)
XLA Ops:
  0.6 0.0 copy-start.1
  0.6 3.9 %channel_stats.1 = (f32[16,8,256]{2,1,0:T(8,128)S(1)}, s32[16]{0:T(128)S(1)}, bf16[4,128,256]{2,1,0:T(8,128)(2,1)S(1)}, bf16[4,128,256]{2,1,0:T(8,128)(2,1)S(1)}...) custom-call(s32[16]{0:T(128)} %clip_len_hbm.3, ...), custom_call_target="tpu_custom_call" | custom-call | flops 1000 | bytes 1000 | tf_op jit(solution)/shard_map/channel_stats/pallas_call | solution.py:110
  4.5 15.8 %all_to_all.20.sums = f32[16,8,256]{2,1,0:T(8,128)S(1)} all-to-all(f32[16,8,256]{2,1,0:T(8,128)S(1)} %get-tuple-element.27), channel_id=1, replica_groups=mesh['tm'=16,'rows'=8] {'tm'}, dimensions={0} | all-to-all | bytes 262144 | tf_op jit(solution)/shard_map/all_to_all | solution.py:660
  20.3 0.0 copy-start
  20.3 0.0 copy-start.2
  20.3 0.0 copy-start.3
  20.3 0.0 copy-start.4
  20.3 0.0 copy-start.5
  20.3 0.0 copy-start.6
  20.3 2.7 %collective-permute-start.3 = (bf16[19,128,256]{2,1,0:T(8,128)(2,1)S(1)}, bf16[19,128,256]{2,1,0:T(8,128)(2,1)S(1)}, u32[]{:S(2)}, u32[]{:S(2)}) collective-permute-start(bf16[19,128,256]{2,1,0:T(8,128)(2,1)S(1)} %after_sums.1), channel_id=1, source_target_pairs={{0,8},{8,16},{16,24},{24,32},{32,40},{40,48},{48,56},{56,64},{64,7... | collective-permute-start | bytes 3735560 | tf_op jit(solution)/shard_map/ppermute | solution.py:652
  23.1 0.7 clip_sums.1
  23.8 1.3 %collective-permute-start = (bf16[4,128,256]{2,1,0:T(8,128)(2,1)S(1)}, bf16[4,128,256]{2,1,0:T(8,128)(2,1)S(1)}, u32[]{:S(2)}, u32[]{:S(2)}) collective-permute-start(bf16[4,128,256]{2,1,0:T(8,128)(2,1)S(1)} %get-tuple-element.31), channel_id=1, source_target_pairs={{0,1},{1,2},{2,3},{3,4},{4,5},{5,6},{6,7},{8,9},{9,10},{10,11},{11... | collective-permute-start | bytes 786440 | tf_op jit(solution)/shard_map/ppermute | solution.py:652
  25.1 1.3 %collective-permute-start.1 = (bf16[4,128,256]{2,1,0:T(8,128)(2,1)S(1)}, bf16[4,128,256]{2,1,0:T(8,128)(2,1)S(1)}, u32[]{:S(2)}, u32[]{:S(2)}) collective-permute-start(bf16[4,128,256]{2,1,0:T(8,128)(2,1)S(1)} %get-tuple-element.32), channel_id=1, source_target_pairs={{1,0},{2,1},{3,2},{4,3},{5,4},{6,5},{7,6},{9,8},{10,9},{11,10},{12... | collective-permute-start | bytes 786440 | tf_op jit(solution)/shard_map/ppermute | solution.py:652
  26.4 12.7 %all_to_all.21.near = f32[8,8,256]{2,1,0:T(8,128)S(1)} all-to-all(f32[8,8,256]{2,1,0:T(8,128)S(1)} %get-tuple-element.30), channel_id=1, replica_groups=mesh['tm'=16,'rows'=8] {'rows'}, dimensions={0} | all-to-all | bytes 131072 | tf_op jit(solution)/shard_map/all_to_all | solution.py:666
  39.1 0.0 collective-permute-done.top
  39.1 0.0 collective-permute-done.1.bot
  39.1 0.6 pack_sides.1.sides
  39.7 2.9 %collective-permute-start.4 = (bf16[10,128,256]{2,1,0:T(8,128)(2,1)S(1)}, bf16[10,128,256]{2,1,0:T(8,128)(2,1)S(1)}, u32[]{:S(2)}, u32[]{:S(2)}) collective-permute-start(bf16[10,128,256]{2,1,0:T(8,128)(2,1)S(1)} %pack_sides.1.sides), channel_id=1, source_target_pairs={{0,8},{8,16},{16,24},{24,32},{32,40},{40,48},{48,56},{56,64},{64,7... | collective-permute-start | bytes 1966088 | tf_op jit(solution)/shard_map/ppermute | solution.py:652
  42.5 0.0 copy-done.1
  42.6 2.1 %weight_bank.1 = (bf16[21,768,256]{2,1,0:T(8,128)(2,1)S(1)}, s32[72]{0:T(128)S(1)}, bf16[7,128,256]{2,1,0:T(8,128)(2,1)S(1)}) custom-call(s32[16]{0:T(128)} %clip_len_hbm.3, s32[16]{0:T(128)} %owner_hbm.1, bf16[3,3,768,256]{3,2,1,0:T(8,128)(2,1)S(1)} %copy-done.1, bf16[10,128,256]{2,1,0:T(8,128)(2,1)S(1)} %pack_sides.1.sides, ...), custom_call_target="tpu_custom_call", output_to_operand_aliasing={{2}: (4, {})} | custom-call | flops 1000 | bytes 1000 | tf_op jit(solution)/shard_map/weight_bank/pallas_call | solution.py:273
  44.7 3.3 %collective-permute-start.2 = (bf16[7,128,256]{2,1,0:T(8,128)(2,1)S(1)}, bf16[7,128,256]{2,1,0:T(8,128)(2,1)S(1)}, u32[]{:S(2)}, u32[]{:S(2)}) collective-permute-start(bf16[7,128,256]{2,1,0:T(8,128)(2,1)S(1)} %get-tuple-element.35), channel_id=1, source_target_pairs={{0,8},{8,16},{16,24},{24,32},{32,40},{40,48},{48,56},{56,64},{64,7... | collective-permute-start | bytes 1376264 | tf_op jit(solution)/shard_map/ppermute | solution.py:652
  48.0 0.0 copy-done
  48.0 0.0 copy-done.2
  48.0 0.0 copy-done.3
  48.0 0.0 copy-done.4
  48.0 0.0 copy-done.5
  48.0 0.0 copy-done.6
  48.0 18.3 %local_conv.1 = (bf16[4,16,128,256]{3,2,1,0:T(8,128)(2,1)}, f32[2,2,8,128,256]{4,3,2,1,0:T(8,128)S(1)}, bf16[16,2,16,128]{3,2,1,0:T(8,128)(2,1)S(1)}, f32[8,256]...) custom-call(s32[16]{0:T(128)S(1)} %get-tuple-element.26.table, ...), custom_call_target="tpu_custom_call" | custom-call | flops 1000 | bytes 1000 | tf_op jit(solution)/shard_map/local_conv/pallas_call | solution.py:466
  66.3 0.0 collective-permute-done.4.sides
  66.3 0.0 collective-permute-done.3.past
  66.3 6.7 %past_one.1 = (bf16[4,16,128,256]{3,2,1,0:T(8,128)(2,1)}, f32[2,8,128,256]{3,2,1,0:T(8,128)S(1)}, bf16[16,1,16,128]{3,2,1,0:T(8,128)(2,1)S(1)}) custom-call(s32[16]{0:T(128)S(1)} %get-tuple-element.26.table, bf16[19,128,256]{2,1,0:T(8,128)(2,1)S(1)} %collective-permute-done.3.past, ...), custom_call_target="tpu_custom_call", output_to_operand_aliasing={{0}: (10, {})} | custom-call | flops 1000 | bytes 1000 | tf_op jit(solution)/shard_map/past_one/pallas_call | solution.py:576
  73.0 0.0 collective-permute-done.2.late
  73.0 3.2 %past_two.1 = (bf16[4,16,128,256]{3,2,1,0:T(8,128)(2,1)}, bf16[16,4,16,128]{3,2,1,0:T(8,128)(2,1)S(1)}) custom-call(s32[16]{0:T(128)S(1)} %get-tuple-element.26.table, bf16[7,128,256]{2,1,0:T(8,128)(2,1)S(1)} %collective-permute-done.2.late, bf16[19,128,256]{2,1,0:T(8,128)(2,1)S(1)} %collective-permute-done.3.past, ...), custom_call_target="tpu_custom_call", output_to_operand_aliasing={{0}: (13, {})} | custom-call | flops 1000 | bytes 1000 | tf_op jit(solution)/shard_map/past_two/pallas_call | solution.py:597
  76.2 14.3 %all_to_all.22 = bf16[16,4,16,128]{3,2,1,0:T(8,128)(2,1)S(1)} all-to-all(bf16[16,4,16,128]{3,2,1,0:T(8,128)(2,1)S(1)} %get-tuple-element.49), channel_id=1, replica_groups=mesh['tm'=16,'rows'=8] {'tm'}, dimensions={0} | all-to-all | bytes 524288 | tf_op jit(solution)/shard_map/all_to_all | solution.py:683
  90.6 0.7 place_frames.1
  91.3 13.6 %all_to_all.23.x_ref = bf16[16,8,16,128]{3,2,1,0:T(8,128)(2,1)S(1)} all-to-all(bf16[16,8,16,128]{3,2,1,0:T(8,128)(2,1)S(1)} %bitcast.8), channel_id=1, replica_groups=mesh['tm'=16,'rows'=8] {'tm'}, dimensions={0} | all-to-all | bytes 1048576 | tf_op jit(solution)/shard_map/all_to_all | solution.py:685
  104.9 0.9 merge_columns.1
  (1 shorter events, 0.0 us)
Async XLA Ops:
  0.6 41.9 %copy-start.1 = (bf16[3,3,768,256]{3,2,1,0:T(8,128)(2,1)S(1)}, bf16[3,3,768,256]{3,2,1,0:T(8,128)(2,1)}, u32[]{:S(2)}) copy-start(bf16[3,3,768,256]{3,2,1,0:T(8,128)(2,1)} %w.1) | copy-start | bytes 10616836
  20.3 27.7 %copy-start = (bf16[4,16,128,256]{3,2,1,0:T(8,128)(2,1)S(1)}, bf16[4,16,128,256]{3,2,1,0:T(8,128)(2,1)}, u32[]{:S(2)}) copy-start(bf16[4,16,128,256]{3,2,1,0:T(8,128)(2,1)} %feat.7) | copy-start | bytes 12582916
  20.3 27.7 %copy-start.2 = (f32[256]{0:T(256)S(1)}, f32[256]{0:T(256)}, u32[]{:S(2)}) copy-start(f32[256]{0:T(256)} %param.13) | copy-start | bytes 3076
  20.3 27.7 %copy-start.3 = (bf16[256,16]{0,1:T(8,128)(2,1)S(1)}, bf16[256,16]{0,1:T(8,128)(2,1)}, u32[]{:S(2)}) copy-start(bf16[256,16]{0,1:T(8,128)(2,1)} %param.14) | copy-start | bytes 24580
  20.3 27.7 %copy-start.4 = (f32[256]{0:T(256)S(1)}, f32[256]{0:T(256)}, u32[]{:S(2)}) copy-start(f32[256]{0:T(256)} %param.10) | copy-start | bytes 3076
  20.3 27.7 %copy-start.5 = (f32[256]{0:T(256)S(1)}, f32[256]{0:T(256)}, u32[]{:S(2)}) copy-start(f32[256]{0:T(256)} %param.11) | copy-start | bytes 3076
  20.3 27.7 %copy-start.6 = (f32[16]{0:T(128)S(1)}, f32[16]{0:T(128)}, u32[]{:S(2)}) copy-start(f32[16]{0:T(128)} %param.15) | copy-start | bytes 196
  20.3 46.0 %collective-permute-start.3 = (bf16[19,128,256]{2,1,0:T(8,128)(2,1)S(1)}, bf16[19,128,256]{2,1,0:T(8,128)(2,1)S(1)}, u32[]{:S(2)}, u32[]{:S(2)}) collective-permute-start(bf16[19,128,256]{2,1,0:T(8,128)(2,1)S(1)} %after_sums.1), channel_id=1, source_target_pairs={{0,8},{8,16},{16,24},{24,32},{32,40},{40,48},{48,56},{56,64},{64,7... | collective-permute-start | bytes 3735560 | tf_op jit(solution)/shard_map/ppermute | solution.py:652
  23.8 15.3 %collective-permute-start = (bf16[4,128,256]{2,1,0:T(8,128)(2,1)S(1)}, bf16[4,128,256]{2,1,0:T(8,128)(2,1)S(1)}, u32[]{:S(2)}, u32[]{:S(2)}) collective-permute-start(bf16[4,128,256]{2,1,0:T(8,128)(2,1)S(1)} %get-tuple-element.31), channel_id=1, source_target_pairs={{0,1},{1,2},{2,3},{3,4},{4,5},{5,6},{6,7},{8,9},{9,10},{10,11},{11... | collective-permute-start | bytes 786440 | tf_op jit(solution)/shard_map/ppermute | solution.py:652
  25.1 14.0 %collective-permute-start.1 = (bf16[4,128,256]{2,1,0:T(8,128)(2,1)S(1)}, bf16[4,128,256]{2,1,0:T(8,128)(2,1)S(1)}, u32[]{:S(2)}, u32[]{:S(2)}) collective-permute-start(bf16[4,128,256]{2,1,0:T(8,128)(2,1)S(1)} %get-tuple-element.32), channel_id=1, source_target_pairs={{1,0},{2,1},{3,2},{4,3},{5,4},{6,5},{7,6},{9,8},{10,9},{11,10},{12... | collective-permute-start | bytes 786440 | tf_op jit(solution)/shard_map/ppermute | solution.py:652
  39.7 26.6 %collective-permute-start.4 = (bf16[10,128,256]{2,1,0:T(8,128)(2,1)S(1)}, bf16[10,128,256]{2,1,0:T(8,128)(2,1)S(1)}, u32[]{:S(2)}, u32[]{:S(2)}) collective-permute-start(bf16[10,128,256]{2,1,0:T(8,128)(2,1)S(1)} %pack_sides.1.sides), channel_id=1, source_target_pairs={{0,8},{8,16},{16,24},{24,32},{32,40},{40,48},{48,56},{56,64},{64,7... | collective-permute-start | bytes 1966088 | tf_op jit(solution)/shard_map/ppermute | solution.py:652
  44.7 28.3 %collective-permute-start.2 = (bf16[7,128,256]{2,1,0:T(8,128)(2,1)S(1)}, bf16[7,128,256]{2,1,0:T(8,128)(2,1)S(1)}, u32[]{:S(2)}, u32[]{:S(2)}) collective-permute-start(bf16[7,128,256]{2,1,0:T(8,128)(2,1)S(1)} %get-tuple-element.35), channel_id=1, source_target_pairs={{0,8},{8,16},{16,24},{24,32},{32,40},{40,48},{48,56},{56,64},{64,7... | collective-permute-start | bytes 1376264 | tf_op jit(solution)/shard_map/ppermute | solution.py:652

commit v6 on v5

--- a/solution.py
+++ b/solution.py
@@ -71,14 +71,16 @@
     starts = [jnp.int32(0)] * 4
     ends = [jnp.int32(0)] * 4
     start = jnp.int32(0)
-    ints.wait()
     for i, (f, q) in enumerate(order):
-        end = start + clip_len[i]
-        for own in range(4):
-            inside = jnp.logical_and(first + own >= start, first + own < end)
-            starts[own] = jnp.where(inside, start - first, starts[own])
-            ends[own] = jnp.where(inside, end - first, ends[own])
-        start = end
+        if i == CLIPS // 2:
+            ints.wait()
+        for c in range(max(2 * i - CLIPS, 0), max(2 * i - CLIPS + 2, 0)):
+            end = start + clip_len[c]
+            for own in range(4):
+                inside = jnp.logical_and(first + own >= start, first + own < end)
+                starts[own] = jnp.where(inside, start - first, starts[own])
+                ends[own] = jnp.where(inside, end - first, ends[own])
+            start = end
         loads[i].wait()
         if q == 3:
             down_ref[f] = x_ref[f, band - 1]
@@ -631,17 +633,24 @@
     )(codes, shares)
 
 
-def merge_kernel(x_ref, o_ref):
-    for j in range(x_ref.shape[0]):
-        o_ref[:, :, 128 * j : 128 * (j + 1)] = x_ref[j]
+def merge_kernel(x_ref, o_ref, sems):
+    copies = [
+        pltpu.make_async_copy(x_ref.at[j], o_ref.at[:, :, pl.ds(128 * j, 128)], sems.at[j])
+        for j in range(x_ref.shape[0])
+    ]
+    for c in copies:
+        c.start()
+    for c in copies:
+        c.wait()
 
 
 def merge(seq):
     return pl.pallas_call(
         merge_kernel,
-        in_specs=[VM],
-        out_specs=VM,
+        in_specs=[ANY],
+        out_specs=HBM,
         out_shape=jax.ShapeDtypeStruct((8, 16, 2048), BF16),
+        scratch_shapes=[pltpu.SemaphoreType.DMA((16,))],
         compiler_params=pltpu.CompilerParams(vmem_limit_bytes=4 * MIB),
         name="merge_columns",
     )(seq)

time: 106 us -> 106 us (level)
  no operation moved by 1% of the time
where the time goes in v6:
time: 106 us
  blocking collectives  56.4 us (53%)
  Pallas kernels  37.1 us (35%)
  starting transfers between devices  11.5 us (11%)
    pallas_call x1, Pallas kernels, local_part(): pl.pallas_call(local_kernel, in_specs=[SM] + [VM] * 10, out_specs=[ANY, V...  18.3 us
    all_to_all x1, blocking collectives, on_device(): sums = lax.all_to_all(sums, 'tm', split_axis=0, concat_axis=0, tiled=True)  15.8 us
    all_to_all x1, blocking collectives, on_device(): shares = lax.all_to_all(lat, 'tm', split_axis=0, concat_axis=0, tiled=True)  14.3 us
    all_to_all x1, blocking collectives, on_device(): lax.all_to_all(placed.reshape(n_time, SEQ_CAP, band, 128), 'tm', split_ax...  13.6 us
    all_to_all x1, blocking collectives, on_device(): near = lax.all_to_all(sums, 'rows', split_axis=0, concat_axis=0, tiled=True)  12.7 us
    ppermute x5, starting transfers between devices, shift(): lax.ppermute(x, axis, [(i, i + by) for i in range(n) if 0 <= i + by < n])  11.5 us
    pallas_call x1, Pallas kernels, one_part(): pl.pallas_call(one_kernel, in_specs=[SM] + [VM] * 9 + [ANY], out_specs=[A...  6.67 us
    pallas_call x1, Pallas kernels, channel_stats(): pl.pallas_call(stats_kernel, in_specs=[HBM, HBM], out_specs=[VM, SM, VM,...  3.89 us
  transfers between devices with their start and end apart: 5, of which 0 were waited for; matrix products, arithmetic and copies ran while one was open for 0% of the time, Pallas kernels for 27%

profile of v6, /device:TPU:0, one launch (start us, length us, event | category | flops | bytes accessed | tf_op | source)
XLA Modules:
  0.0 106.0 jit_solution(13737543042485928287)
XLA Ops:
  0.6 0.0 copy-start.1
  0.6 3.9 %channel_stats.1 = (f32[16,8,256]{2,1,0:T(8,128)S(1)}, s32[16]{0:T(128)S(1)}, bf16[4,128,256]{2,1,0:T(8,128)(2,1)S(1)}, bf16[4,128,256]{2,1,0:T(8,128)(2,1)S(1)}...) custom-call(s32[16]{0:T(128)} %clip_len_hbm.3, ...), custom_call_target="tpu_custom_call" | custom-call | flops 1000 | bytes 1000 | tf_op jit(solution)/shard_map/channel_stats/pallas_call | solution.py:112
  4.5 15.8 %all_to_all.20.sums = f32[16,8,256]{2,1,0:T(8,128)S(1)} all-to-all(f32[16,8,256]{2,1,0:T(8,128)S(1)} %get-tuple-element.27), channel_id=1, replica_groups=mesh['tm'=16,'rows'=8] {'tm'}, dimensions={0} | all-to-all | bytes 262144 | tf_op jit(solution)/shard_map/all_to_all | solution.py:669
  20.3 0.0 copy-start
  20.3 0.0 copy-start.2
  20.3 0.0 copy-start.3
  20.3 0.0 copy-start.4
  20.3 0.0 copy-start.5
  20.3 0.0 copy-start.6
  20.4 2.7 %collective-permute-start.3 = (bf16[19,128,256]{2,1,0:T(8,128)(2,1)S(1)}, bf16[19,128,256]{2,1,0:T(8,128)(2,1)S(1)}, u32[]{:S(2)}, u32[]{:S(2)}) collective-permute-start(bf16[19,128,256]{2,1,0:T(8,128)(2,1)S(1)} %after_sums.1), channel_id=1, source_target_pairs={{0,8},{8,16},{16,24},{24,32},{32,40},{40,48},{48,56},{56,64},{64,7... | collective-permute-start | bytes 3735560 | tf_op jit(solution)/shard_map/ppermute | solution.py:661
  23.1 0.7 clip_sums.1
  23.8 1.3 %collective-permute-start = (bf16[4,128,256]{2,1,0:T(8,128)(2,1)S(1)}, bf16[4,128,256]{2,1,0:T(8,128)(2,1)S(1)}, u32[]{:S(2)}, u32[]{:S(2)}) collective-permute-start(bf16[4,128,256]{2,1,0:T(8,128)(2,1)S(1)} %get-tuple-element.31), channel_id=1, source_target_pairs={{0,1},{1,2},{2,3},{3,4},{4,5},{5,6},{6,7},{8,9},{9,10},{10,11},{11... | collective-permute-start | bytes 786440 | tf_op jit(solution)/shard_map/ppermute | solution.py:661
  25.1 1.3 %collective-permute-start.1 = (bf16[4,128,256]{2,1,0:T(8,128)(2,1)S(1)}, bf16[4,128,256]{2,1,0:T(8,128)(2,1)S(1)}, u32[]{:S(2)}, u32[]{:S(2)}) collective-permute-start(bf16[4,128,256]{2,1,0:T(8,128)(2,1)S(1)} %get-tuple-element.32), channel_id=1, source_target_pairs={{1,0},{2,1},{3,2},{4,3},{5,4},{6,5},{7,6},{9,8},{10,9},{11,10},{12... | collective-permute-start | bytes 786440 | tf_op jit(solution)/shard_map/ppermute | solution.py:661
  26.4 12.7 %all_to_all.21.near = f32[8,8,256]{2,1,0:T(8,128)S(1)} all-to-all(f32[8,8,256]{2,1,0:T(8,128)S(1)} %get-tuple-element.30), channel_id=1, replica_groups=mesh['tm'=16,'rows'=8] {'rows'}, dimensions={0} | all-to-all | bytes 131072 | tf_op jit(solution)/shard_map/all_to_all | solution.py:675
  39.1 0.0 collective-permute-done.top
  39.1 0.0 collective-permute-done.1.bot
  39.1 0.6 pack_sides.1.sides
  39.7 2.9 %collective-permute-start.4 = (bf16[10,128,256]{2,1,0:T(8,128)(2,1)S(1)}, bf16[10,128,256]{2,1,0:T(8,128)(2,1)S(1)}, u32[]{:S(2)}, u32[]{:S(2)}) collective-permute-start(bf16[10,128,256]{2,1,0:T(8,128)(2,1)S(1)} %pack_sides.1.sides), channel_id=1, source_target_pairs={{0,8},{8,16},{16,24},{24,32},{32,40},{40,48},{48,56},{56,64},{64,7... | collective-permute-start | bytes 1966088 | tf_op jit(solution)/shard_map/ppermute | solution.py:661
  42.6 0.0 copy-done.1
  42.6 2.1 %weight_bank.1 = (bf16[21,768,256]{2,1,0:T(8,128)(2,1)S(1)}, s32[72]{0:T(128)S(1)}, bf16[7,128,256]{2,1,0:T(8,128)(2,1)S(1)}) custom-call(s32[16]{0:T(128)} %clip_len_hbm.3, s32[16]{0:T(128)} %owner_hbm.1, bf16[3,3,768,256]{3,2,1,0:T(8,128)(2,1)S(1)} %copy-done.1, bf16[10,128,256]{2,1,0:T(8,128)(2,1)S(1)} %pack_sides.1.sides, ...), custom_call_target="tpu_custom_call", output_to_operand_aliasing={{2}: (4, {})} | custom-call | flops 1000 | bytes 1000 | tf_op jit(solution)/shard_map/weight_bank/pallas_call | solution.py:275
  44.7 3.3 %collective-permute-start.2 = (bf16[7,128,256]{2,1,0:T(8,128)(2,1)S(1)}, bf16[7,128,256]{2,1,0:T(8,128)(2,1)S(1)}, u32[]{:S(2)}, u32[]{:S(2)}) collective-permute-start(bf16[7,128,256]{2,1,0:T(8,128)(2,1)S(1)} %get-tuple-element.35), channel_id=1, source_target_pairs={{0,8},{8,16},{16,24},{24,32},{32,40},{40,48},{48,56},{56,64},{64,7... | collective-permute-start | bytes 1376264 | tf_op jit(solution)/shard_map/ppermute | solution.py:661
  48.0 0.0 copy-done
  48.0 0.0 copy-done.2
  48.0 0.0 copy-done.3
  48.0 0.0 copy-done.4
  48.0 0.0 copy-done.5
  48.0 0.0 copy-done.6
  48.0 18.3 %local_conv.1 = (bf16[4,16,128,256]{3,2,1,0:T(8,128)(2,1)}, f32[2,2,8,128,256]{4,3,2,1,0:T(8,128)S(1)}, bf16[16,2,16,128]{3,2,1,0:T(8,128)(2,1)S(1)}, f32[8,256]...) custom-call(s32[16]{0:T(128)S(1)} %get-tuple-element.26.table, ...), custom_call_target="tpu_custom_call" | custom-call | flops 1000 | bytes 1000 | tf_op jit(solution)/shard_map/local_conv/pallas_call | solution.py:468
  66.3 0.0 collective-permute-done.4.sides
  66.3 0.0 collective-permute-done.3.past
  66.3 6.7 %past_one.1 = (bf16[4,16,128,256]{3,2,1,0:T(8,128)(2,1)}, f32[2,8,128,256]{3,2,1,0:T(8,128)S(1)}, bf16[16,1,16,128]{3,2,1,0:T(8,128)(2,1)S(1)}) custom-call(s32[16]{0:T(128)S(1)} %get-tuple-element.26.table, bf16[19,128,256]{2,1,0:T(8,128)(2,1)S(1)} %collective-permute-done.3.past, ...), custom_call_target="tpu_custom_call", output_to_operand_aliasing={{0}: (10, {})} | custom-call | flops 1000 | bytes 1000 | tf_op jit(solution)/shard_map/past_one/pallas_call | solution.py:578
  73.0 0.0 collective-permute-done.2.late
  73.0 3.2 %past_two.1 = (bf16[4,16,128,256]{3,2,1,0:T(8,128)(2,1)}, bf16[16,4,16,128]{3,2,1,0:T(8,128)(2,1)S(1)}) custom-call(s32[16]{0:T(128)S(1)} %get-tuple-element.26.table, bf16[7,128,256]{2,1,0:T(8,128)(2,1)S(1)} %collective-permute-done.2.late, bf16[19,128,256]{2,1,0:T(8,128)(2,1)S(1)} %collective-permute-done.3.past, ...), custom_call_target="tpu_custom_call", output_to_operand_aliasing={{0}: (13, {})} | custom-call | flops 1000 | bytes 1000 | tf_op jit(solution)/shard_map/past_two/pallas_call | solution.py:599
  76.3 14.3 %all_to_all.22 = bf16[16,4,16,128]{3,2,1,0:T(8,128)(2,1)S(1)} all-to-all(bf16[16,4,16,128]{3,2,1,0:T(8,128)(2,1)S(1)} %get-tuple-element.49), channel_id=1, replica_groups=mesh['tm'=16,'rows'=8] {'tm'}, dimensions={0} | all-to-all | bytes 524288 | tf_op jit(solution)/shard_map/all_to_all | solution.py:692
  90.6 0.7 place_frames.1
  91.3 13.6 %all_to_all.23.x_ref = bf16[16,8,16,128]{3,2,1,0:T(8,128)(2,1)S(1)} all-to-all(bf16[16,8,16,128]{3,2,1,0:T(8,128)(2,1)S(1)} %bitcast.8), channel_id=1, replica_groups=mesh['tm'=16,'rows'=8] {'tm'}, dimensions={0} | all-to-all | bytes 1048576 | tf_op jit(solution)/shard_map/all_to_all | solution.py:694
  104.9 0.9 merge_columns.1
  (1 shorter events, 0.0 us)
Async XLA Ops:
  0.6 41.9 %copy-start.1 = (bf16[3,3,768,256]{3,2,1,0:T(8,128)(2,1)S(1)}, bf16[3,3,768,256]{3,2,1,0:T(8,128)(2,1)}, u32[]{:S(2)}) copy-start(bf16[3,3,768,256]{3,2,1,0:T(8,128)(2,1)} %w.1) | copy-start | bytes 10616836
  20.3 27.7 %copy-start = (bf16[4,16,128,256]{3,2,1,0:T(8,128)(2,1)S(1)}, bf16[4,16,128,256]{3,2,1,0:T(8,128)(2,1)}, u32[]{:S(2)}) copy-start(bf16[4,16,128,256]{3,2,1,0:T(8,128)(2,1)} %feat.7) | copy-start | bytes 12582916
  20.3 27.7 %copy-start.2 = (f32[256]{0:T(256)S(1)}, f32[256]{0:T(256)}, u32[]{:S(2)}) copy-start(f32[256]{0:T(256)} %param.13) | copy-start | bytes 3076
  20.3 27.7 %copy-start.3 = (bf16[256,16]{0,1:T(8,128)(2,1)S(1)}, bf16[256,16]{0,1:T(8,128)(2,1)}, u32[]{:S(2)}) copy-start(bf16[256,16]{0,1:T(8,128)(2,1)} %param.14) | copy-start | bytes 24580
  20.3 27.7 %copy-start.4 = (f32[256]{0:T(256)S(1)}, f32[256]{0:T(256)}, u32[]{:S(2)}) copy-start(f32[256]{0:T(256)} %param.10) | copy-start | bytes 3076
  20.3 27.7 %copy-start.5 = (f32[256]{0:T(256)S(1)}, f32[256]{0:T(256)}, u32[]{:S(2)}) copy-start(f32[256]{0:T(256)} %param.11) | copy-start | bytes 3076
  20.3 27.7 %copy-start.6 = (f32[16]{0:T(128)S(1)}, f32[16]{0:T(128)}, u32[]{:S(2)}) copy-start(f32[16]{0:T(128)} %param.15) | copy-start | bytes 196
  20.4 46.0 %collective-permute-start.3 = (bf16[19,128,256]{2,1,0:T(8,128)(2,1)S(1)}, bf16[19,128,256]{2,1,0:T(8,128)(2,1)S(1)}, u32[]{:S(2)}, u32[]{:S(2)}) collective-permute-start(bf16[19,128,256]{2,1,0:T(8,128)(2,1)S(1)} %after_sums.1), channel_id=1, source_target_pairs={{0,8},{8,16},{16,24},{24,32},{32,40},{40,48},{48,56},{56,64},{64,7... | collective-permute-start | bytes 3735560 | tf_op jit(solution)/shard_map/ppermute | solution.py:661
  23.8 15.3 %collective-permute-start = (bf16[4,128,256]{2,1,0:T(8,128)(2,1)S(1)}, bf16[4,128,256]{2,1,0:T(8,128)(2,1)S(1)}, u32[]{:S(2)}, u32[]{:S(2)}) collective-permute-start(bf16[4,128,256]{2,1,0:T(8,128)(2,1)S(1)} %get-tuple-element.31), channel_id=1, source_target_pairs={{0,1},{1,2},{2,3},{3,4},{4,5},{5,6},{6,7},{8,9},{9,10},{10,11},{11... | collective-permute-start | bytes 786440 | tf_op jit(solution)/shard_map/ppermute | solution.py:661
  25.1 14.0 %collective-permute-start.1 = (bf16[4,128,256]{2,1,0:T(8,128)(2,1)S(1)}, bf16[4,128,256]{2,1,0:T(8,128)(2,1)S(1)}, u32[]{:S(2)}, u32[]{:S(2)}) collective-permute-start(bf16[4,128,256]{2,1,0:T(8,128)(2,1)S(1)} %get-tuple-element.32), channel_id=1, source_target_pairs={{1,0},{2,1},{3,2},{4,3},{5,4},{6,5},{7,6},{9,8},{10,9},{11,10},{12... | collective-permute-start | bytes 786440 | tf_op jit(solution)/shard_map/ppermute | solution.py:661
  39.7 26.6 %collective-permute-start.4 = (bf16[10,128,256]{2,1,0:T(8,128)(2,1)S(1)}, bf16[10,128,256]{2,1,0:T(8,128)(2,1)S(1)}, u32[]{:S(2)}, u32[]{:S(2)}) collective-permute-start(bf16[10,128,256]{2,1,0:T(8,128)(2,1)S(1)} %pack_sides.1.sides), channel_id=1, source_target_pairs={{0,8},{8,16},{16,24},{24,32},{32,40},{40,48},{48,56},{56,64},{64,7... | collective-permute-start | bytes 1966088 | tf_op jit(solution)/shard_map/ppermute | solution.py:661
  44.7 28.3 %collective-permute-start.2 = (bf16[7,128,256]{2,1,0:T(8,128)(2,1)S(1)}, bf16[7,128,256]{2,1,0:T(8,128)(2,1)S(1)}, u32[]{:S(2)}, u32[]{:S(2)}) collective-permute-start(bf16[7,128,256]{2,1,0:T(8,128)(2,1)S(1)} %get-tuple-element.35), channel_id=1, source_target_pairs={{0,8},{8,16},{16,24},{24,32},{32,40},{40,48},{48,56},{56,64},{64,7... | collective-permute-start | bytes 1376264 | tf_op jit(solution)/shard_map/ppermute | solution.py:661
